TPU v7x, 32 devices: a whole 2x2x4 slice. The times are simulated.
32 devices in a mesh: ctx: 8 (over z, y), head: 4 (over x, core).
Axes of the slice: x: 2, y: 2, z: 4, core: 2. Of those that a mesh axis runs over, the one named last changes fastest.
Arguments:
- enc_rows: bfloat16 [2048, 1024], P(('ctx', 'head')), may hold values from -6 to 6
- row_counts: int32 [8, 4], P('ctx'), may hold values from 0 to 64, as said below
- row_places: int32 [8, 256], P('ctx'), may hold values from 0 to 4095, as said below
- stream: bfloat16 [4096, 3072], P('ctx'), may hold values from -134 to 134
- norm_gain: float32 [3072], replicated, may hold values from 0.25 to 1.75
- proj_in: bfloat16 [1024, 6144], P('ctx', 'head'), may hold values from -0.1875 to 0.1875
- proj_out: bfloat16 [6144, 3072], P('head', 'ctx'), may hold values from -0.078125 to 0.078125
- qkv_weight: bfloat16 [3072, 3, 2048], P(None, None, 'head'), may hold values from -0.109375 to 0.109375
- head_gain: float32 [2048], P('head'), may hold values from 0.25 to 1.75
- mix_weight: bfloat16 [2048, 3072], P('head', 'ctx'), may hold values from -0.125 to 0.125
Outputs:
- layer_out: bfloat16 [4096, 3072], P('ctx', 'head')
Inputs may be any that keep to these rules, and one draw needn't show every extreme that they name: `row_counts`: the 4 devices of one ctx index hold 64 live rows together, and some device holds 64. `row_places`: the place of a live slot of a device with ctx index c lies from c * 512 to c * 512 + 511, and live places are distinct; a slot that is not live holds a place in the same range, which is ignored.
All inputs are finite; a program needn't handle non-finite values.
Results may differ from a plain program's by a relative error of at most 0.015.
Values may be sent and summed in bfloat16 or wider, within the bound.
No kernel may reach another device: no remote copies, remote signals or barrier semaphores. Data moves between devices by JAX's collectives and lax.ppermute only.
A program may use at most 128 MiB of HBM per device.

v0:
```python
import jax
import jax.numpy as jnp
from jax import lax
from jax.sharding import PartitionSpec as P

HEAD_DIM = 128


def prefix_2(x, axis, combine, identity):
    devices, position = (lax.axis_size(axis), lax.axis_index(axis))
    everything = lax.all_gather(x.astype(jnp.bfloat16), axis)
    start = jnp.broadcast_to(jnp.asarray(identity, x.dtype), x.shape)

    def lap(k, before):
        reached = k < position
        new = combine(before, everything[k].astype(x.dtype))
        return jnp.where(reached, new, before)

    return lax.fori_loop(0, devices, lap, start)


def on_device(
    enc_rows,
    row_counts,
    row_places,
    stream,
    norm_gain,
    proj_in,
    proj_out,
    qkv_weight,
    head_gain,
    mix_weight,
):
    capacity = enc_rows.shape[0]
    shard_rows = stream.shape[0]
    head_count = lax.axis_size("head")
    ctx_index = lax.axis_index("ctx")
    counts_each = jnp.broadcast_to(row_counts[0][:, None], (head_count, capacity)).reshape(-1)
    within = jnp.broadcast_to(
        jnp.arange(capacity, dtype=jnp.int32)[None, :], (head_count, capacity)
    ).reshape(-1)
    is_live = within < counts_each
    places = jnp.where(is_live, row_places[0] - ctx_index * shard_rows, shard_rows)
    group_rows = lax.all_gather(enc_rows, "head", axis=0, tiled=True)
    live_total = head_count * (capacity // 4)
    ordering = jnp.argsort(jnp.where(is_live, 0, 1).astype(jnp.int32), stable=True)[:live_total]
    picked_rows = jnp.take(group_rows, ordering, axis=0)
    picked_places = jnp.take(places, ordering)
    first_full, second_full, mix_full = (
        lax.all_gather(proj_in, "ctx", axis=0, tiled=True),
        lax.all_gather(proj_out, "ctx", axis=1, tiled=True),
        lax.all_gather(mix_weight, "ctx", axis=1, tiled=True),
    )
    hidden = jax.nn.gelu(
        jnp.dot(picked_rows, first_full, preferred_element_type=jnp.float32), approximate=False
    ).astype(jnp.bfloat16)
    partial_value = jnp.dot(hidden, second_full, preferred_element_type=jnp.float32)
    image_rows = lax.psum(partial_value.astype(jnp.bfloat16), "head")
    packed = stream.at[picked_places].set(image_rows, mode="drop")
    widened = packed.astype(jnp.float32)
    normed = (
        widened * lax.rsqrt(jnp.mean(widened * widened, axis=-1, keepdims=True) + 1e-05) * norm_gain
    ).astype(jnp.bfloat16)
    flat_qkv = qkv_weight.reshape(qkv_weight.shape[0], -1)
    projected = jax.nn.silu(jnp.dot(normed, flat_qkv, preferred_element_type=jnp.float32)).astype(
        jnp.bfloat16
    )
    heads_dev = qkv_weight.shape[2] // HEAD_DIM
    block_len = min(shard_rows, 512)
    block_count = shard_rows // block_len
    projected = projected.reshape(block_count, block_len, 3, heads_dev, HEAD_DIM)
    queries = projected[:, :, 0]
    key_rows = projected[:, :, 1]
    values = projected[:, :, 2]
    block_states = jnp.einsum(
        "bkhd,bkhe->bhde", key_rows, values, preferred_element_type=jnp.float32
    )
    shard_state = jnp.sum(block_states, axis=0)
    prefix = prefix_2(
        shard_state, "ctx", lambda earlier, latter: earlier + latter, jnp.zeros_like(shard_state)
    )
    running_states = jnp.cumsum(block_states, axis=0)
    earlier_states = jnp.concatenate([jnp.zeros_like(block_states), running_states[:-1]], axis=0)
    starting = prefix[None] + earlier_states
    causal = jnp.tril(jnp.ones((block_len, block_len), dtype=bool))
    scores = jnp.einsum("bqhd,bkhd->bhqk", queries, key_rows, preferred_element_type=jnp.float32)
    scores = jnp.where(causal, scores, 0.0).astype(jnp.bfloat16)
    attended = jnp.einsum("bhqk,bkhd->bqhd", scores, values, preferred_element_type=jnp.float32)
    attended = attended + jnp.einsum(
        "bqhd,bhde->bqhe", queries.astype(jnp.float32), starting, precision=lax.Precision.HIGHEST
    )
    inverse_rms = lax.rsqrt(jnp.mean(attended * attended, axis=-1, keepdims=True) + 1e-06)
    heads_out = (attended * inverse_rms * head_gain.reshape(heads_dev, HEAD_DIM)).astype(
        jnp.bfloat16
    )
    heads_out = heads_out.reshape(shard_rows, heads_dev * HEAD_DIM)
    group_part = jnp.dot(heads_out, mix_full, preferred_element_type=jnp.float32)
    summed = lax.psum_scatter(
        group_part.astype(jnp.bfloat16), "head", scatter_dimension=1, tiled=True
    )
    return summed


def solution(mesh):
    in_specs = (
        P(("ctx", "head"), None),
        P("ctx", None),
        P("ctx", None),
        P("ctx", None),
        P(),
        P("ctx", "head"),
        P("head", "ctx"),
        P(None, None, "head"),
        P("head"),
        P("head", "ctx"),
    )
    out_specs = P("ctx", "head")
    return jax.shard_map(
        on_device, mesh=mesh, in_specs=in_specs, out_specs=out_specs, check_vma=False
    )
```

profile of v0, /device:TPU:1, one launch (start us, length us, event | category | flops | bytes accessed | tf_op | source)
XLA Modules:
  0.0 422.7 jit_solution(11060082751884176605)
XLA Ops:
  8.2 3.2 sort.17
  12.2 8.5 %all_gather.16 = bf16[256,1024]{1,0:T(8,128)(2,1)S(1)} all-gather(bf16[64,1024]{1,0:T(8,128)(2,1)S(1)} %copy-done.1), channel_id=1, replica_groups=mesh['ctx'=8,'head'=4] {'head'}, dimensions={0}, use_global_device_ids=true | all-gather | bytes 655360 | tf_op jit(solution)/shard_map/all_gather | solution.py:44
  21.4 12.7 %copy.22 = bf16[3072,3,512]{0,2,1:T(8,128)(2,1)} copy(bf16[3072,3,512]{2,0,1:T(8,128)(2,1)} %param.19) | data formatting | bytes 18874368 | tf_op args[7]
  34.2 37.1 %all-gather.6.cloned.1.call-done = bf16[1024,1536]{1,0:T(8,128)(2,1)} async-done(((bf16[128,1536]{1,0:T(8,128)(2,1)}), bf16[1024,1536]{1,0:T(8,128)(2,1)}) %all-gather.6.cloned.1.call-update) | async-done | bytes 3145744 | tf_op jit(solution)/shard_map/all_gather | solution.py:50
  71.3 139.3 %all-gather.8.cloned.1.call-done = bf16[1536,3072]{1,0:T(8,128)(2,1)} async-done(((bf16[1536,384]{1,0:T(8,128)(2,1)}), bf16[1536,3072]{1,0:T(8,128)(2,1)}) %all-gather.8.cloned.1.call-update) | async-done | bytes 9437200 | tf_op jit(solution)/shard_map/all_gather | solution.py:51
  210.6 8.6 %convolution_convert_fusion.1 = bf16[64,3072]{1,0:T(8,128)(2,1)} fusion(bf16[1536,3072]{1,0:T(8,128)(2,1)} %all-gather.8.cloned.1.call-done, bf16[1024,1536]{1,0:T(8,128)(2,1)} %all-gather.6.cloned.1.call-done, bf16[64,1024]{1,0:T(8,128)(2,1)S(1)} %gather_fusion.1, pred[64]{0:T(512)(128)(4,1)S(1)} %get-tuple-element.110), kind=kOutput, calls=%fused_computation.11 | convolution fusion | flops 811958272 | bytes 13107264 | tf_op jit(solution)/shard_map/dot_general | solution.py:57
  219.2 29.7 %all-reduce.2.cloned.1.call-done = bf16[64,3072]{1,0:T(8,128)(2,1)} async-done(((bf16[64,3072]{1,0:T(8,128)(2,1)}), bf16[64,3072]{1,0:T(8,128)(2,1)}) %all-reduce.2.cloned.1.call-update) | async-done | bytes 393232 | tf_op jit(solution)/shard_map/psum | solution.py:58
  249.0 3.4 scatter_fusion
  253.1 10.3 %multiply_convert_fusion = bf16[512,1536]{1,0:T(8,128)(2,1)} fusion(bf16[3072,1536]{0,1:T(8,128)(2,1)} %bitcast.42, bf16[512,3072]{1,0:T(8,128)(2,1)S(1)} %scatter_fusion, f32[3072]{0:T(1024)S(1)} %copy-done.4, f32[512]{0:T(512)S(1)} %add_rsqrt_fusion.1), kind=kOutput, calls=%fused_computation.13 | convolution fusion | flops 4842061824 | bytes 14170112 | tf_op jit(solution)/shard_map/dot_general | solution.py:65
  263.4 3.0 reshape.84
  269.2 40.0 %all-gather.12.cloned.1.call-done = bf16[32,128,128]{2,1,0:T(8,128)(2,1)} async-done(((bf16[4,128,128]{2,1,0:T(8,128)(2,1)}), bf16[32,128,128]{2,1,0:T(8,128)(2,1)}) %all-gather.12.cloned.1.call-update) | async-done | bytes 1048592 | tf_op jit(solution)/shard_map/all_gather | solution.py:11
  309.2 8.5 %while.14 = (s32[]{:T(128)}, f32[4,128,128]{2,1,0:T(8,128)S(1)}, s32[]{:T(128)}, bf16[8,4,128,128]{3,2,1,0:T(8,128)(2,1)}, s32[]{:T(128)}, /*index=5*/s32[]{:T(128)}) while((s32[]{:T(128)}, f32[4,128,128]{2,1,0:T(8,128)S(1)}, s32[]{:T(128)}, bf16[8,4,128,128]{3,2,1,0:T(8,128)(2,1)}, s32[]{:T(128)}, /*index=5*/s32[]{:T(128)}) %tuple.52), condition=%wide.region_5.6_spmd.clone, body=%wide.region_4.5_spmd.clone.sunk | while | flops 262148 | bytes 655453 | solution.py:19
  310.3 1.0 add_select_fusion.2
  311.3 1.0 add_select_fusion.2
  312.4 1.0 add_select_fusion.2
  313.4 1.0 add_select_fusion.2
  314.5 1.0 add_select_fusion.2
  315.6 1.0 add_select_fusion.2
  317.7 1.6 fusion.14
  319.3 3.6 multiply_reduce_fusion
  322.9 1.4 multiply_convert_fusion.1
  324.3 49.5 %all-gather.10.cloned.1.call-done = bf16[512,3072]{1,0:T(8,128)(2,1)} async-done(((bf16[512,384]{1,0:T(8,128)(2,1)}), bf16[512,3072]{1,0:T(8,128)(2,1)}) %all-gather.10.cloned.1.call-update) | async-done | bytes 3145744 | tf_op jit(solution)/shard_map/all_gather | solution.py:52
  373.8 5.4 %convolution_convert_fusion = bf16[512,3072]{1,0:T(8,128)(2,1)} fusion(bf16[512,512]{0,1:T(8,128)(2,1)S(1)} %bitcast.43, bf16[512,3072]{1,0:T(8,128)(2,1)} %all-gather.10.cloned.1.call-done), kind=kOutput, calls=%fused_computation.9 | convolution fusion | flops 1612185600 | bytes 6815744 | tf_op jit(solution)/shard_map/dot_general | solution.py:97
  379.2 36.7 %reduce-scatter.2.cloned.1.call-done = bf16[512,768]{1,0:T(8,128)(2,1)} async-done(((bf16[512,3072]{1,0:T(8,128)(2,1)}), bf16[512,768]{1,0:T(8,128)(2,1)}) %reduce-scatter.2.cloned.1.call-update) | async-done | bytes 786448 | tf_op jit(solution)/shard_map/reduce_scatter | solution.py:98
  (44 shorter events, 8.8 us)
Async XLA Ops:
  6.5 64.7 %all-gather.6.cloned.1.call-start = ((), (), s32[]{:S(2)}) async-start(), calls=%async_computation.1 | async-start | bytes 3538944 | tf_op jit(solution)/shard_map/all_gather | solution.py:50
  6.5 1.5 copy-start.5
  6.5 1.7 copy-start.3
  6.5 5.7 %copy-start.1 = (bf16[64,1024]{1,0:T(8,128)(2,1)S(1)}, bf16[64,1024]{1,0:T(8,128)(2,1)}, u32[]{:S(2)}) copy-start(bf16[64,1024]{1,0:T(8,128)(2,1)} %param.12) | copy-start | bytes 393220
  7.3 203.3 %all-gather.8.cloned.1.call-start = ((), (), s32[]{:S(2)}) async-start(), calls=%async_computation.2 | async-start | bytes 10616832 | tf_op jit(solution)/shard_map/all_gather | solution.py:51
  8.0 241.0 %all-reduce.2.cloned.1.call-start = ((), (), s32[]{:S(2)}) async-start(), calls=%async_computation.3 | async-start | bytes 786432 | tf_op jit(solution)/shard_map/psum | solution.py:58
  210.6 38.4 %copy-start = (bf16[512,3072]{1,0:T(8,128)(2,1)S(1)}, bf16[512,3072]{1,0:T(8,128)(2,1)}, u32[]{:S(2)}) copy-start(bf16[512,3072]{1,0:T(8,128)(2,1)} %param.15) | copy-start | bytes 9437188
  219.2 90.1 %all-gather.12.cloned.1.call-start = ((), (), s32[]{:S(2)}) async-start(), calls=%async_computation.6 | async-start | bytes 1179648 | tf_op jit(solution)/shard_map/all_gather | solution.py:11
  252.4 0.7 copy-start.4
  268.3 105.5 %all-gather.10.cloned.1.call-start = ((), (), s32[]{:S(2)}) async-start(), calls=%async_computation.4 | async-start | bytes 3538944 | tf_op jit(solution)/shard_map/all_gather | solution.py:52
  268.9 147.0 %reduce-scatter.2.cloned.1.call-start = ((), (), s32[]{:S(2)}) async-start(), calls=%async_computation.5 | async-start | bytes 3932160 | tf_op jit(solution)/shard_map/reduce_scatter | solution.py:98
  319.3 3.6 copy-start.2
Sparse Core Ops, SparseCore 0:
  9.5 61.6 all-gather.5
  73.3 137.1 all-gather.7
  219.3 29.6 all-reduce.1
  268.4 40.7 all-gather.11
  311.3 62.4 all-gather.9
  379.3 36.5 reduce-scatter.1
where the time goes:
time: 424 us; the launch traced here: 423 us
  waiting for transfers between devices  334 us (79%)
  matrix products  30.5 us (7%)
  local copies, waits for them, and re-layouts  21.6 us (5%)
  other arithmetic  13.7 us (3%)
  between operations  13.6 us (3%)
  blocking collectives  8.51 us (2%)
    all_gather x1, waiting for transfers between devices, on_device(): lax.all_gather(proj_out, 'ctx', axis=1, tiled=True)  139 us
    all_gather x1, waiting for transfers between devices, on_device(): lax.all_gather(mix_weight, 'ctx', axis=1, tiled=True)  49.5 us
    all_gather x1, waiting for transfers between devices, prefix_2(): everything = lax.all_gather(x.astype(jnp.bfloat16), axis)  40 us
    all_gather x1, waiting for transfers between devices, on_device(): lax.all_gather(proj_in, 'ctx', axis=0, tiled=True)  37.1 us
    reduce_scatter x1, waiting for transfers between devices, on_device(): lax.psum_scatter(group_part.astype(jnp.bfloat16), 'head', scatter_dimensi...  36.7 us
    psum x1, waiting for transfers between devices, on_device(): image_rows = lax.psum(partial_value.astype(jnp.bfloat16), 'head')  29.7 us
    unnamed x14, local copies, waits for them, and re-layouts  13.1 us
    dot_general x1, matrix products, on_device(): jnp.dot(normed, flat_qkv, preferred_element_type=jnp.float32)  10.3 us
  transfers between devices with their start and end apart: 6, of which 6 were waited for; matrix products, arithmetic and copies ran while one was open for 8% of the time, Pallas kernels for 0%

commit v1 on v0

v1 whole, which is shorter than its diff:
```python
import jax
import jax.numpy as jnp
from jax import lax
from jax.sharding import PartitionSpec as P

HEAD_DIM = 128
F32 = jnp.float32
BF16 = jnp.bfloat16


def gather_head(x, bits, head_index, head_count):
    for bit in bits:
        other = lax.ppermute(x, "head", [(i, i ^ bit) for i in range(head_count)])
        upper = (head_index & bit) != 0
        x = jnp.stack([jnp.where(upper, other, x), jnp.where(upper, x, other)])
    return x


def on_device(
    enc_rows,
    row_counts,
    row_places,
    stream,
    norm_gain,
    proj_in,
    proj_out,
    qkv_weight,
    head_gain,
    mix_weight,
):
    both = ("ctx", "head")
    capacity, enc_width = enc_rows.shape
    shard_rows, width = stream.shape
    n_ctx, n_head = lax.axis_size("ctx"), lax.axis_size("head")
    ctx, head = lax.axis_index("ctx"), lax.axis_index("head")
    live_total = n_head * (capacity // 4)
    part_rows = live_total // n_head
    bits = []
    bit = n_head // 2
    while bit:
        bits.append(bit)
        bit //= 2
    flat = [(c, h) for c in range(n_ctx) for h in range(n_head)]

    def index(c, h):
        return c * n_head + h

    half = proj_in.shape[1] // 2
    in_halves = jnp.stack([proj_in[:, :half], proj_in[:, half:]])
    in_sends = jnp.broadcast_to(in_halves[None], (n_ctx // 2,) + in_halves.shape).reshape(
        (n_ctx,) + in_halves.shape[1:]
    )
    in_full = lax.all_to_all(in_sends, "ctx", 0, 0).reshape(enc_width, half)

    out_cols = proj_out.shape[1]
    out_parts = []
    for k in range(2):
        chosen = (head & 1) ^ k
        block = lax.dynamic_slice(proj_out, (chosen * half, 0), (half, out_cols))
        perm = [
            (index(c, h), index((c & ~1) | ((h & 1) ^ k), (h & ~1) | (c & 1))) for c, h in flat
        ]
        out_parts.append(lax.ppermute(block, both, perm))

    ratio = n_ctx // n_head
    perm = [(index(c, h), index((c % ratio) * n_head + h, c // ratio)) for c, h in flat]
    mix_own = lax.ppermute(mix_weight, both, perm)

    group_rows = lax.all_gather(enc_rows, "head", axis=0, tiled=True)
    counts = row_counts[0]
    starts = jnp.cumsum(counts) - counts
    within = jnp.arange(capacity, dtype=jnp.int32)[None, :]
    spot = jnp.where(within < counts[:, None], starts[:, None] + within, -1).reshape(-1)
    picks = spot[None, :] == jnp.arange(live_total, dtype=jnp.int32)[:, None]
    local_places = row_places[0] - ctx * shard_rows
    places = jnp.sum(jnp.where(picks, local_places[None, :], 0), axis=1)
    own_picks = (
        spot[None, :] == (head * part_rows + jnp.arange(part_rows, dtype=jnp.int32))[:, None]
    )
    own_rows = jnp.dot(own_picks.astype(BF16), group_rows, preferred_element_type=F32).astype(BF16)
    part = lax.all_to_all(
        jnp.broadcast_to(own_rows[None], (n_ctx,) + own_rows.shape), "ctx", 0, 0
    )
    all_rows = gather_head(part, bits, head, n_head)
    hidden = jax.nn.gelu(
        jnp.dot(all_rows.reshape(-1, enc_width), in_full, preferred_element_type=F32),
        approximate=False,
    ).astype(BF16)
    hidden_other = lax.ppermute(hidden, "head", [(i, i ^ 1) for i in range(n_head)])
    aligned = (head & 1) == (ctx & 1)
    hid_a = jnp.where(aligned, hidden, hidden_other)
    hid_b = jnp.where(aligned, hidden_other, hidden)
    partial_rows = jnp.dot(hid_a, out_parts[0], preferred_element_type=F32) + jnp.dot(
        hid_b, out_parts[1], preferred_element_type=F32
    )
    n_bits = len(bits)
    partial_rows = partial_rows.astype(BF16).reshape((2,) * n_bits + (n_ctx, part_rows, out_cols))
    order = (n_bits,) + tuple(reversed(range(n_bits))) + (n_bits + 1, n_bits + 2)
    sends = partial_rows.transpose(order).reshape(n_ctx * n_head, part_rows, out_cols)
    received = lax.all_to_all(sends, both, 0, 0)
    received = received.reshape(n_ctx // 2, 2, n_head // 2, 2, part_rows, out_cols)
    summed = jnp.sum(received.astype(F32), axis=(1, 2)).astype(BF16)
    img_part = summed.transpose(2, 0, 1, 3).reshape(part_rows, width)
    image_rows = lax.all_gather(img_part, "head", axis=0, tiled=True)

    flat_qkv = qkv_weight.reshape(width, -1)

    def project(rows):
        widened = rows.astype(F32)
        normed = (
            widened
            * lax.rsqrt(jnp.mean(widened * widened, axis=-1, keepdims=True) + 1e-05)
            * norm_gain
        ).astype(BF16)
        return jax.nn.silu(jnp.dot(normed, flat_qkv, preferred_element_type=F32)).astype(BF16)

    text_qkv = project(stream)
    image_qkv = project(image_rows)
    put = jnp.arange(shard_rows, dtype=jnp.int32)[:, None] == places[None, :]
    placed = jnp.dot(put.astype(BF16), image_qkv, preferred_element_type=F32).astype(BF16)
    projected = jnp.where(jnp.any(put, axis=1)[:, None], placed, text_qkv)

    heads_dev = qkv_weight.shape[2] // HEAD_DIM
    block_len = min(shard_rows, 512)
    block_count = shard_rows // block_len
    projected = projected.reshape(block_count, block_len, 3, heads_dev, HEAD_DIM)
    queries = projected[:, :, 0]
    key_rows = projected[:, :, 1]
    values = projected[:, :, 2]
    block_states = jnp.einsum("bkhd,bkhe->bhde", key_rows, values, preferred_element_type=F32)
    shard_state = jnp.sum(block_states, axis=0)
    pieces = shard_state.astype(BF16).reshape(n_ctx, -1, HEAD_DIM)
    pieces = lax.all_to_all(pieces, "ctx", 0, 0).astype(F32)
    before = jnp.cumsum(pieces, axis=0) - pieces
    prefix = lax.all_to_all(before.astype(BF16), "ctx", 0, 0).astype(F32).reshape(shard_state.shape)
    running_states = jnp.cumsum(block_states, axis=0)
    earlier_states = jnp.concatenate([jnp.zeros_like(block_states), running_states[:-1]], axis=0)
    starting = prefix[None] + earlier_states
    causal = jnp.tril(jnp.ones((block_len, block_len), dtype=bool))
    scores = jnp.einsum("bqhd,bkhd->bhqk", queries, key_rows, preferred_element_type=F32)
    scores = jnp.where(causal, scores, 0.0).astype(BF16)
    attended = jnp.einsum("bhqk,bkhd->bqhd", scores, values, preferred_element_type=F32)
    attended = attended + jnp.einsum(
        "bqhd,bhde->bqhe", queries, starting.astype(BF16), preferred_element_type=F32
    )
    inverse_rms = lax.rsqrt(jnp.mean(attended * attended, axis=-1, keepdims=True) + 1e-06)
    heads_out = (attended * inverse_rms * head_gain.reshape(heads_dev, HEAD_DIM)).astype(BF16)
    heads_out = heads_out.reshape(shard_rows, heads_dev * HEAD_DIM)

    all_heads = gather_head(heads_out, bits, head, n_head)
    mix_full = lax.all_gather(mix_own, "ctx", axis=0)
    group_width, mix_cols = mix_weight.shape
    mix_full = mix_full.reshape(ratio, n_head, group_width, mix_cols)
    total = 0.0
    for g in range(n_head):
        at = tuple((g >> b) & 1 for b in range(n_bits))
        group = jnp.concatenate([mix_full[r, g] for r in range(ratio)], axis=1)
        one = jnp.dot(all_heads[at], group, preferred_element_type=F32).astype(BF16)
        total = total + one.astype(F32)
    return total.astype(BF16)


def solution(mesh):
    in_specs = (
        P(("ctx", "head"), None),
        P("ctx", None),
        P("ctx", None),
        P("ctx", None),
        P(),
        P("ctx", "head"),
        P("head", "ctx"),
        P(None, None, "head"),
        P("head"),
        P("head", "ctx"),
    )
    out_specs = P("ctx", "head")
    return jax.shard_map(
        on_device, mesh=mesh, in_specs=in_specs, out_specs=out_specs, check_vma=False
    )
```

time: 424 us -> 206 us (0.49)
  waiting for transfers between devices: 334 us -> 59.7 us
  starting transfers between devices: 0.38 us -> 38.3 us
  blocking collectives: 8.51 us -> 26.1 us
  other arithmetic: 13.7 us -> 7.26 us
  matrix products: 30.5 us -> 36.5 us
    all_gather x4 -> x1, waiting for transfers between devices: 266 us -> 0.75 us  [on_device(): mix_full = lax.all_gather(mix_own, 'ctx', axis=0)]
    all_to_all x0 -> x4, waiting for transfers between devices: none -> 42.5 us  [the longest x1 24.1 us: on_device(): in_full = lax.all_to_all(in_sends, 'ctx', 0, 0).reshape(enc_width, half)]
    reduce_scatter x1 -> x0, waiting for transfers between devices: 36.7 us -> none  [on_device(): lax.psum_scatter(group_part.astype(jnp.bfloat16), 'head', scatter_dimensi...]
    psum x1 -> x0, waiting for transfers between devices: 29.7 us -> none  [on_device(): image_rows = lax.psum(partial_value.astype(jnp.bfloat16), 'head')]
    all_to_all x0 -> x4, starting transfers between devices: none -> 22 us  [the longest x1 8.44 us: on_device(): received = lax.all_to_all(sends, both, 0, 0)]
    ppermute x0 -> x8, waiting for transfers between devices: none -> 16.5 us  [the longest x4 16.4 us: gather_head(): other = lax.ppermute(x, 'head', [(i, i ^ bit) for i in range(head_count)])]
    ppermute x0 -> x8, starting transfers between devices: none -> 16.3 us  [the longest x4 8.35 us: gather_head(): other = lax.ppermute(x, 'head', [(i, i ^ bit) for i in range(head_count)])]
    all_to_all x0 -> x1, blocking collectives: none -> 10.2 us  [on_device(): pieces = lax.all_to_all(pieces, 'ctx', 0, 0).astype(F32)]
  transfers between devices with their start and end apart: 6 -> 13, of which waited for: 6 -> 8; matrix products, arithmetic and copies ran while one was open for 8% -> 25% of each run, Pallas kernels for 0% -> 0%
where the time goes in v1:
time: 206 us; the launch traced here: 203 us
  waiting for transfers between devices  59.7 us (29%)
  starting transfers between devices  38.3 us (19%)
  matrix products  36.5 us (18%)
  blocking collectives  26.1 us (13%)
  local copies, waits for them, and re-layouts  21.6 us (10%)
  between operations  13.7 us (7%)
  other arithmetic  7.26 us (4%)
    all_to_all x1, waiting for transfers between devices, on_device(): in_full = lax.all_to_all(in_sends, 'ctx', 0, 0).reshape(enc_width, half)  24.1 us
    ppermute x4, waiting for transfers between devices, gather_head(): other = lax.ppermute(x, 'head', [(i, i ^ bit) for i in range(head_count)])  16.4 us
    unnamed x10, local copies, waits for them, and re-layouts  13.1 us
    dot_general x1, matrix products, project(): jnp.dot(normed, flat_qkv, preferred_element_type=F32)  10.3 us
    all_to_all x1, blocking collectives, on_device(): pieces = lax.all_to_all(pieces, 'ctx', 0, 0).astype(F32)  10.2 us
    all_to_all x1, waiting for transfers between devices, on_device(): lax.all_to_all(before.astype(BF16), 'ctx', 0, 0).astype(F32)  9.19 us
    all_gather x1, blocking collectives, on_device(): group_rows = lax.all_gather(enc_rows, 'head', axis=0, tiled=True)  8.71 us
    all_to_all x1, starting transfers between devices, on_device(): received = lax.all_to_all(sends, both, 0, 0)  8.44 us
  transfers between devices with their start and end apart: 13, of which 8 were waited for; matrix products, arithmetic and copies ran while one was open for 25% of the time, Pallas kernels for 0%

profile of v1, /device:TPU:1, one launch (start us, length us, event | category | flops | bytes accessed | tf_op | source)
XLA Modules:
  0.0 203.1 jit_solution(16356056837876097518)
XLA Ops:
  8.9 8.7 %all_gather.12 = bf16[256,1024]{1,0:T(8,128)(2,1)S(1)} all-gather(bf16[64,1024]{1,0:T(8,128)(2,1)} %param.10), channel_id=1, replica_groups=mesh['ctx'=8,'head'=4] {'head'}, dimensions={0}, use_global_device_ids=true | all-gather | bytes 655360 | tf_op jit(solution)/shard_map/all_gather | solution.py:69
  18.6 5.6 %all-to-all-start = ((bf16[8,16,1024]{2,1,0:T(8,128)(2,1)}), bf16[8,16,1024]{2,1,0:T(8,128)(2,1)S(1)}, u32[]{:S(2)}, u32[]{:S(2)}) async-start(bf16[8,16,1024]{2,1,0:T(8,128)(2,1)} %broadcast_in_dim.67), calls=%async_computation | async-start | bytes 524288 | tf_op jit(solution)/shard_map/all_to_all | solution.py:81
  24.2 7.9 %all-to-all-done = bf16[8,16,1024]{2,1,0:T(8,128)(2,1)S(1)} async-done(((bf16[8,16,1024]{2,1,0:T(8,128)(2,1)}), bf16[8,16,1024]{2,1,0:T(8,128)(2,1)S(1)}, u32[]{:S(2)}, u32[]{:S(2)}) %all-to-all-start) | async-done | bytes 262176 | tf_op jit(solution)/shard_map/all_to_all | solution.py:81
  33.3 4.6 %all-to-all-start.1 = ((bf16[8,128,768]{2,1,0:T(8,128)(2,1)}), bf16[8,128,768]{2,1,0:T(8,128)(2,1)}, u32[]{:S(2)}, u32[]{:S(2)}) async-start(bf16[8,128,768]{2,1,0:T(8,128)(2,1)} %bitcast.11), calls=%async_computation.1 | async-start | bytes 3145728 | tf_op jit(solution)/shard_map/all_to_all | solution.py:53
  38.8 5.4 %collective-permute-done = bf16[8,16,1024]{2,1,0:T(8,128)(2,1)S(1)} collective-permute-done((bf16[8,16,1024]{2,1,0:T(8,128)(2,1)S(1)}, bf16[8,16,1024]{2,1,0:T(8,128)(2,1)S(1)}, u32[]{:S(2)}, u32[]{:S(2)}) %collective-permute-start) | collective-permute-done | bytes 262176 | tf_op jit(solution)/shard_map/ppermute | solution.py:13
  44.3 2.5 %collective-permute-start.1 = (bf16[2,8,16,1024]{3,2,1,0:T(8,128)(2,1)S(1)}, bf16[2,8,16,1024]{3,2,1,0:T(8,128)(2,1)S(1)}, u32[]{:S(2)}, u32[]{:S(2)}) collective-permute-start(bf16[2,8,16,1024]{3,2,1,0:T(8,128)(2,1)S(1)} %pad_maximum_fusion.2), channel_id=1, source_target_pairs={{0,1},{1,0},{2,3},{3,2},{4,5},{5,4},{6,7},{7,6},{8,9},{9,8},{10,11... | collective-permute-start | bytes 1572872 | tf_op jit(solution)/shard_map/ppermute | solution.py:13
  49.5 24.1 %all-to-all-done.1 = bf16[8,128,768]{2,1,0:T(8,128)(2,1)} async-done(((bf16[8,128,768]{2,1,0:T(8,128)(2,1)}), bf16[8,128,768]{2,1,0:T(8,128)(2,1)}, u32[]{:S(2)}, u32[]{:S(2)}) %all-to-all-start.1) | async-done | bytes 1572896 | tf_op jit(solution)/shard_map/all_to_all | solution.py:53
  73.7 6.8 %fusion.13 = bf16[512,768]{1,0:T(8,128)(2,1)} fusion(bf16[512,1024]{1,0:T(8,128)(2,1)} %bitcast.111, bf16[1024,768]{1,0:T(8,128)(2,1)} %bitcast.12), kind=kOutput, calls=%fused_computation.16 | convolution fusion | flops 830865408 | bytes 3407872 | tf_op jit(solution)/shard_map/dot_general | solution.py:86
  80.5 2.3 %collective-permute-start.2 = (bf16[512,768]{1,0:T(8,128)(2,1)}, bf16[512,768]{1,0:T(8,128)(2,1)}, u32[]{:S(2)}, u32[]{:S(2)}) collective-permute-start(bf16[512,768]{1,0:T(8,128)(2,1)} %fusion.13), channel_id=1, source_target_pairs={{0,1},{1,0},{2,3},{3,2},{4,5},{5,4},{6,7},{7,6},{8,9},{9,8},{10,11... | collective-permute-start | bytes 2359304 | tf_op jit(solution)/shard_map/ppermute | solution.py:89
  82.9 2.4 %constant_dynamic-slice_fusion = (bf16[768,384]{1,0:T(8,128)(2,1)}, bf16[768,384]{1,0:T(8,128)(2,1)}) fusion(bf16[1536,384]{1,0:T(8,128)(2,1)} %param.16, s32[]{:T(128)S(6)} %select_n.105, s32[]{:T(128)S(6)} %select_n.107), kind=kLoop, calls=%fused_computation.123 | loop fusion | bytes 2359304 | tf_op jit(solution)/shard_map/dynamic_slice | solution.py:59
  85.2 3.4 %collective-permute-start.3 = (bf16[768,384]{1,0:T(8,128)(2,1)}, bf16[768,384]{1,0:T(8,128)(2,1)}, u32[]{:S(2)}, u32[]{:S(2)}) collective-permute-start(bf16[768,384]{1,0:T(8,128)(2,1)} %get-tuple-element.18), channel_id=1, source_target_pairs={{0,0},{1,4},{2,2},{3,6},{4,1},{5,5},{6,3},{7,7},{8,8},{9,12},{10,1... | collective-permute-start | bytes 1769480 | tf_op jit(solution)/shard_map/ppermute | solution.py:63
  88.7 2.1 %collective-permute-start.7 = (bf16[512,384]{1,0:T(8,128)(2,1)}, bf16[512,384]{1,0:T(8,128)(2,1)}, u32[]{:S(2)}, u32[]{:S(2)}) collective-permute-start(bf16[512,384]{1,0:T(8,128)(2,1)} %param.19), channel_id=1, source_target_pairs={{0,0},{1,4},{2,8},{3,12},{4,16},{5,20},{6,24},{7,28},{8,1},{9,5},{... | collective-permute-start | bytes 1179656 | tf_op jit(solution)/shard_map/ppermute | solution.py:67
  91.5 12.7 %copy.33 = bf16[3072,3,512]{0,2,1:T(8,128)(2,1)} copy(bf16[3072,3,512]{2,0,1:T(8,128)(2,1)} %param.17) | data formatting | bytes 18874368 | tf_op args[7]
  109.5 8.4 %all-to-all-start.2 = ((bf16[32,16,384]{2,1,0:T(8,128)(2,1)}), bf16[32,16,384]{2,1,0:T(8,128)(2,1)S(1)}, u32[]{:S(2)}, u32[]{:S(2)}) async-start(bf16[32,16,384]{2,1,0:T(8,128)(2,1)} %bitcast.109), calls=%async_computation.2 | async-start | bytes 786432 | tf_op jit(solution)/shard_map/all_to_all | solution.py:100
  118.0 10.3 %multiply_convert_fusion = bf16[512,1536]{1,0:T(8,128)(2,1)} fusion(bf16[3072,1536]{0,1:T(8,128)(2,1)} %bitcast.104, bf16[512,3072]{1,0:T(8,128)(2,1)S(1)} %copy-done, f32[3072]{0:T(1024)S(1)} %copy-done.2, f32[512]{0:T(512)} %add_rsqrt_fusion.1), kind=kOutput, calls=%fused_computation.7 | convolution fusion | flops 4842061824 | bytes 14170112 | tf_op jit(solution)/shard_map/dot_general | solution.py:115
  130.7 7.2 %all_gather.13 = bf16[64,3072]{1,0:T(8,128)(2,1)S(1)} all-gather(bf16[16,3072]{1,0:T(8,128)(2,1)S(1)} %reshape.181), channel_id=1, replica_groups=mesh['ctx'=8,'head'=4] {'head'}, dimensions={0}, use_global_device_ids=true | all-gather | bytes 491520 | tf_op jit(solution)/shard_map/all_gather | solution.py:104
  138.0 7.6 %fusion.9 = bf16[512,1536]{1,0:T(8,128)(2,1)S(1)} fusion(bf16[512,1536]{1,0:T(8,128)(2,1)} %multiply_convert_fusion, pred[512]{0:T(512)(128)(4,1)S(1)} %fusion.60, bf16[3072,1536]{0,1:T(8,128)(2,1)} %bitcast.105, bf16[64,3072]{1,0:T(8,128)(2,1)S(1)} %all_gather.13, f32[3072]{0:T(1024)S(1)} %copy-done.2, f32[64]{0:T(128)S(1)} %add_rsqrt_fusion.2, ...), kind=kOutput, calls=%fused_computation.11 | convolution fusion | flops 707526656 | bytes 12989440 | tf_op jit(solution)/shard_map/dot_general | solution.py:120
  147.3 10.2 %all_to_all.25 = bf16[8,64,128]{2,1,0:T(8,128)(2,1)S(1)} all-to-all(bf16[8,64,128]{2,1,0:T(8,128)(2,1)S(1)} %bitcast.112), channel_id=1, replica_groups=mesh['ctx'=8,'head'=4] {'ctx'}, dimensions={0} | all-to-all | bytes 262144 | tf_op jit(solution)/shard_map/all_to_all | solution.py:133
  158.2 3.4 %all-to-all-start.4 = ((bf16[8,64,128]{2,1,0:T(8,128)(2,1)}), bf16[8,64,128]{2,1,0:T(8,128)(2,1)S(1)}, u32[]{:S(2)}, u32[]{:S(2)}) async-start(bf16[8,64,128]{2,1,0:T(8,128)(2,1)} %fusion.24), calls=%async_computation.4 | async-start | bytes 262144 | tf_op jit(solution)/shard_map/all_to_all | solution.py:135
  161.7 9.2 %all-to-all-done.4 = bf16[8,64,128]{2,1,0:T(8,128)(2,1)S(1)} async-done(((bf16[8,64,128]{2,1,0:T(8,128)(2,1)}), bf16[8,64,128]{2,1,0:T(8,128)(2,1)S(1)}, u32[]{:S(2)}, u32[]{:S(2)}) %all-to-all-start.4) | async-done | bytes 131104 | tf_op jit(solution)/shard_map/all_to_all | solution.py:135
  172.2 2.6 %multiply_reduce_fusion = (f32[512,4]{0,1:T(4,128)S(1)}, f32[1,512,4,128]{1,3,2,0:T(8,128)S(1)}) fusion(f32[4,128,512]{2,1,0:T(8,128)} %fusion.47, pred[512,512]{1,0:T(8,128)(4,1)S(1)} %iota_compare_fusion, bf16[1,512,1,4,128]{4,3,2,1,0:T(4,128)(2,1)S(1)} %get-tuple-element.15, bf16[1,512,1,4,128]{4,3,2,1,0:T(4,128)(2,1)S(1)} %get-tuple-element.17, ...), kind=kOutput, calls=%fused_computation.50 | convolution fusion | flops 539752448 | bytes 3940352 | tf_op jit(solution)/shard_map/bhqk,bkhd->bqhd/dot_general | solution.py:142
  176.3 9.5 %collective-permute-done.5 = bf16[512,512]{0,1:T(8,128)(2,1)S(1)} collective-permute-done((bf16[512,512]{0,1:T(8,128)(2,1)S(1)}, bf16[512,512]{0,1:T(8,128)(2,1)S(1)}, u32[]{:S(2)}, u32[]{:S(2)}) %collective-permute-start.5) | collective-permute-done | bytes 524320 | tf_op jit(solution)/shard_map/ppermute | solution.py:13
  185.9 3.7 %collective-permute-start.6 = (bf16[2,512,512]{1,2,0:T(8,128)(2,1)S(1)}, bf16[2,512,512]{1,2,0:T(8,128)(2,1)S(1)}, u32[]{:S(2)}, u32[]{:S(2)}) collective-permute-start(bf16[2,512,512]{1,2,0:T(8,128)(2,1)S(1)} %pad_maximum_fusion.1), channel_id=1, source_target_pairs={{0,1},{1,0},{2,3},{3,2},{4,5},{5,4},{6,7},{7,6},{8,9},{9,8},{10,11... | collective-permute-start | bytes 3145736 | tf_op jit(solution)/shard_map/ppermute | solution.py:13
  190.4 2.1 %slice_bitcast_fusion.9 = (bf16[512,384]{1,0:T(8,128)(2,1)S(1)}, bf16[512,384]{1,0:T(8,128)(2,1)S(1)}, bf16[512,384]{1,0:T(8,128)(2,1)S(1)}, bf16[512,384]{1,0:T...) fusion(bf16[2,4,512,384]{3,2,1,0:T(8,128)(2,1)} %bitcast.106), kind=kLoop, calls=%fused_computation.90 | loop fusion | bytes 6291456 | tf_op jit(solution)/shard_map/squeeze | solution.py:157
  (64 shorter events, 26.3 us)
Async XLA Ops:
  6.5 17.6 %copy-start.1 = (bf16[128,1536]{1,0:T(8,128)(2,1)S(1)}, bf16[128,1536]{1,0:T(8,128)(2,1)}, u32[]{:S(2)}) copy-start(bf16[128,1536]{1,0:T(8,128)(2,1)} %param.15) | copy-start | bytes 1179652
  18.6 13.5 %all-to-all-start = ((bf16[8,16,1024]{2,1,0:T(8,128)(2,1)}), bf16[8,16,1024]{2,1,0:T(8,128)(2,1)S(1)}, u32[]{:S(2)}, u32[]{:S(2)}) async-start(bf16[8,16,1024]{2,1,0:T(8,128)(2,1)} %broadcast_in_dim.67), calls=%async_computation | async-start | bytes 524288 | tf_op jit(solution)/shard_map/all_to_all | solution.py:81
  33.3 40.3 %all-to-all-start.1 = ((bf16[8,128,768]{2,1,0:T(8,128)(2,1)}), bf16[8,128,768]{2,1,0:T(8,128)(2,1)}, u32[]{:S(2)}, u32[]{:S(2)}) async-start(bf16[8,128,768]{2,1,0:T(8,128)(2,1)} %bitcast.11), calls=%async_computation.1 | async-start | bytes 3145728 | tf_op jit(solution)/shard_map/all_to_all | solution.py:53
  37.9 6.3 %collective-permute-start = (bf16[8,16,1024]{2,1,0:T(8,128)(2,1)S(1)}, bf16[8,16,1024]{2,1,0:T(8,128)(2,1)S(1)}, u32[]{:S(2)}, u32[]{:S(2)}) collective-permute-start(bf16[8,16,1024]{2,1,0:T(8,128)(2,1)S(1)} %all-to-all-done), channel_id=1, source_target_pairs={{0,2},{1,3},{2,0},{3,1},{4,6},{5,7},{6,4},{7,5},{8,10},{9,11},{10,... | collective-permute-start | bytes 786440 | tf_op jit(solution)/shard_map/ppermute | solution.py:13
  44.3 4.1 %collective-permute-start.1 = (bf16[2,8,16,1024]{3,2,1,0:T(8,128)(2,1)S(1)}, bf16[2,8,16,1024]{3,2,1,0:T(8,128)(2,1)S(1)}, u32[]{:S(2)}, u32[]{:S(2)}) collective-permute-start(bf16[2,8,16,1024]{3,2,1,0:T(8,128)(2,1)S(1)} %pad_maximum_fusion.2), channel_id=1, source_target_pairs={{0,1},{1,0},{2,3},{3,2},{4,5},{5,4},{6,7},{7,6},{8,9},{9,8},{10,11... | collective-permute-start | bytes 1572872 | tf_op jit(solution)/shard_map/ppermute | solution.py:13
  73.7 17.1 %copy-start = (bf16[512,3072]{1,0:T(8,128)(2,1)S(1)}, bf16[512,3072]{1,0:T(8,128)(2,1)}, u32[]{:S(2)}) copy-start(bf16[512,3072]{1,0:T(8,128)(2,1)} %param.13) | copy-start | bytes 9437188
  80.5 24.4 %collective-permute-start.2 = (bf16[512,768]{1,0:T(8,128)(2,1)}, bf16[512,768]{1,0:T(8,128)(2,1)}, u32[]{:S(2)}, u32[]{:S(2)}) collective-permute-start(bf16[512,768]{1,0:T(8,128)(2,1)} %fusion.13), channel_id=1, source_target_pairs={{0,1},{1,0},{2,3},{3,2},{4,5},{5,4},{6,7},{7,6},{8,9},{9,8},{10,11... | collective-permute-start | bytes 2359304 | tf_op jit(solution)/shard_map/ppermute | solution.py:89
  85.2 19.6 %collective-permute-start.4 = (bf16[768,384]{1,0:T(8,128)(2,1)}, bf16[768,384]{1,0:T(8,128)(2,1)}, u32[]{:S(2)}, u32[]{:S(2)}) collective-permute-start(bf16[768,384]{1,0:T(8,128)(2,1)} %get-tuple-element.19), channel_id=1, source_target_pairs={{0,4},{1,0},{2,6},{3,2},{4,5},{5,1},{6,7},{7,3},{8,12},{9,8},{10,1... | collective-permute-start | bytes 1769480 | tf_op jit(solution)/shard_map/ppermute | solution.py:63
  85.2 21.5 %collective-permute-start.3 = (bf16[768,384]{1,0:T(8,128)(2,1)}, bf16[768,384]{1,0:T(8,128)(2,1)}, u32[]{:S(2)}, u32[]{:S(2)}) collective-permute-start(bf16[768,384]{1,0:T(8,128)(2,1)} %get-tuple-element.18), channel_id=1, source_target_pairs={{0,0},{1,4},{2,2},{3,6},{4,1},{5,5},{6,3},{7,7},{8,8},{9,12},{10,1... | collective-permute-start | bytes 1769480 | tf_op jit(solution)/shard_map/ppermute | solution.py:63
  88.7 39.6 %collective-permute-start.7 = (bf16[512,384]{1,0:T(8,128)(2,1)}, bf16[512,384]{1,0:T(8,128)(2,1)}, u32[]{:S(2)}, u32[]{:S(2)}) collective-permute-start(bf16[512,384]{1,0:T(8,128)(2,1)} %param.19), channel_id=1, source_target_pairs={{0,0},{1,4},{2,8},{3,12},{4,16},{5,20},{6,24},{7,28},{8,1},{9,5},{... | collective-permute-start | bytes 1179656 | tf_op jit(solution)/shard_map/ppermute | solution.py:67
  108.7 9.3 %copy-start.2 = (f32[3072]{0:T(1024)S(1)}, f32[3072]{0:T(1024)}, u32[]{:S(2)}) copy-start(f32[3072]{0:T(1024)} %param.14) | copy-start | bytes 36868
  109.5 21.0 %all-to-all-start.2 = ((bf16[32,16,384]{2,1,0:T(8,128)(2,1)}), bf16[32,16,384]{2,1,0:T(8,128)(2,1)S(1)}, u32[]{:S(2)}, u32[]{:S(2)}) async-start(bf16[32,16,384]{2,1,0:T(8,128)(2,1)} %bitcast.109), calls=%async_computation.2 | async-start | bytes 786432 | tf_op jit(solution)/shard_map/all_to_all | solution.py:100
  117.9 72.5 %all-gather.3.cloned.1.call-start = ((), (), s32[]{:S(2)}) async-start(), calls=%async_computation.5 | async-start | bytes 3538944 | tf_op jit(solution)/shard_map/all_gather | solution.py:151
  158.2 12.7 %all-to-all-start.4 = ((bf16[8,64,128]{2,1,0:T(8,128)(2,1)}), bf16[8,64,128]{2,1,0:T(8,128)(2,1)S(1)}, u32[]{:S(2)}, u32[]{:S(2)}) async-start(bf16[8,64,128]{2,1,0:T(8,128)(2,1)} %fusion.24), calls=%async_computation.4 | async-start | bytes 262144 | tf_op jit(solution)/shard_map/all_to_all | solution.py:135
  172.2 2.6 %copy-start.3 = (f32[512]{0:T(512)S(1)}, f32[512]{0:T(512)}, u32[]{:S(2)}) copy-start(f32[512]{0:T(512)} %param.18) | copy-start | bytes 6148
  175.0 10.7 %collective-permute-start.5 = (bf16[512,512]{0,1:T(8,128)(2,1)S(1)}, bf16[512,512]{0,1:T(8,128)(2,1)S(1)}, u32[]{:S(2)}, u32[]{:S(2)}) collective-permute-start(bf16[512,512]{0,1:T(8,128)(2,1)S(1)} %bitcast.107), channel_id=1, source_target_pairs={{0,2},{1,3},{2,0},{3,1},{4,6},{5,7},{6,4},{7,5},{8,10},{9,11},{10,... | collective-permute-start | bytes 1572872 | tf_op jit(solution)/shard_map/ppermute | solution.py:13
  185.9 6.7 %collective-permute-start.6 = (bf16[2,512,512]{1,2,0:T(8,128)(2,1)S(1)}, bf16[2,512,512]{1,2,0:T(8,128)(2,1)S(1)}, u32[]{:S(2)}, u32[]{:S(2)}) collective-permute-start(bf16[2,512,512]{1,2,0:T(8,128)(2,1)S(1)} %pad_maximum_fusion.1), channel_id=1, source_target_pairs={{0,1},{1,0},{2,3},{3,2},{4,5},{5,4},{6,7},{7,6},{8,9},{9,8},{10,11... | collective-permute-start | bytes 3145736 | tf_op jit(solution)/shard_map/ppermute | solution.py:13
Sparse Core Ops, SparseCore 0:
  128.4 61.9 all-gather.2

commit v2 on v1

v2 whole, which is shorter than its diff:
```python
import functools

import jax
import jax.numpy as jnp
from jax import lax
from jax.experimental import pallas as pl
from jax.experimental.pallas import tpu as pltpu
from jax.sharding import PartitionSpec as P

HEAD_DIM = 128
F32 = jnp.float32
BF16 = jnp.bfloat16
VMEM_LIMIT = 40 * 1024 * 1024
VMEM = pl.BlockSpec(memory_space=pltpu.VMEM)
SMEM = pl.BlockSpec(memory_space=pltpu.SMEM)
PARAMS = pltpu.CompilerParams(vmem_limit_bytes=VMEM_LIMIT)


def cost(flops, nbytes, transcendentals=0):
    return pl.CostEstimate(
        flops=int(flops), bytes_accessed=int(nbytes), transcendentals=int(transcendentals)
    )


def dot(a, b):
    return jnp.dot(a, b, preferred_element_type=F32)


def silu(x):
    return x * (1.0 / (1.0 + jnp.exp(-x)))


def projector_kernel(chunk, meta, own, other, first, second, second_next, keep, send, w_keep, w_send):
    same = meta[0] == meta[1]
    mine, near = second[...], second_next[...]
    w_keep[...] = jnp.where(same, mine, near)
    w_send[...] = jnp.where(same, near, mine)
    rows = own.shape[0]

    def run(source, base):
        @pl.loop(0, rows // chunk)
        def _(i):
            at = pl.ds(pl.multiple_of(i * chunk, chunk), chunk)
            to = pl.ds(pl.multiple_of(base + i * chunk, chunk), chunk)
            pre = dot(source[at, :], first[...])
            hid = (0.5 * pre * (1.0 + lax.erf(pre * 0.7071067811865476))).astype(BF16)
            keep[to, :] = dot(hid, w_keep[...]).astype(BF16)
            send[to, :] = dot(hid, w_send[...]).astype(BF16)

    run(own, 0)
    run(other, rows)


def projector(meta, own, other, first, second, second_next):
    rows, width = own.shape
    units, cols = second.shape
    out = jax.ShapeDtypeStruct((2 * rows, cols), BF16)
    return pl.pallas_call(
        functools.partial(projector_kernel, min(rows, 256)),
        out_shape=(out, out),
        in_specs=[SMEM] + [VMEM] * 5,
        out_specs=(VMEM, VMEM),
        scratch_shapes=[pltpu.VMEM((units, cols), BF16), pltpu.VMEM((units, cols), BF16)],
        compiler_params=PARAMS,
        cost_estimate=cost(4 * rows * units * (width + 2 * cols), 5e6, 2 * rows * units),
        name="projector",
    )(meta, own, other, first, second, second_next)


def order_kernel(pairs, meta, keep, got, out):
    parity, core, pair = meta[0], meta[1], meta[2]
    rows = out.shape[2]
    for i in range(2):
        for k in range(pairs):
            for j in range(2):
                at = pl.ds(((i * pairs + k) * 2 + j) * rows, rows)
                there = pl.ds((((1 - i) * pairs + k) * 2 + j) * rows, rows)
                total = keep[at, :].astype(F32) + got[there, :].astype(F32)
                out[(pair ^ k) * 2 + (parity ^ j), core ^ i] = total.astype(BF16)


def order_rows(meta, keep, got, n_ctx):
    rows, cols = keep.shape
    return pl.pallas_call(
        functools.partial(order_kernel, n_ctx // 2),
        out_shape=jax.ShapeDtypeStruct((n_ctx, 2, rows // n_ctx // 2, cols), BF16),
        in_specs=[SMEM, VMEM, VMEM],
        out_specs=VMEM,
        compiler_params=PARAMS,
        cost_estimate=cost(rows * cols, 6 * rows * cols),
        name="order_rows",
    )(meta, keep, got)


def image_kernel(x, wq, wk, wv, text_state, q, k, v, state):
    rows = x[...]
    q[...] = silu(dot(rows, wq[...])).astype(BF16)
    key = silu(dot(rows, wk[...])).astype(BF16)
    value = silu(dot(rows, wv[...])).astype(BF16)
    k[...] = key
    v[...] = value
    outer = lax.dot_general(key, value, (((0,), (0,)), ((), ())), preferred_element_type=F32)
    state[...] = (text_state[...] + outer[None]).astype(BF16)


def image_qkv(x, weights, text_state):
    rows, width = x.shape
    cols = weights[0].shape[1]
    heads = cols // HEAD_DIM
    w_spec = pl.BlockSpec((width, HEAD_DIM), lambda h: (0, h))
    o_spec = pl.BlockSpec((rows, HEAD_DIM), lambda h: (0, h))
    s_spec = pl.BlockSpec((1, HEAD_DIM, HEAD_DIM), lambda h: (h, 0, 0))
    out = jax.ShapeDtypeStruct((rows, cols), BF16)
    return pl.pallas_call(
        image_kernel,
        grid=(heads,),
        out_shape=(out, out, out, jax.ShapeDtypeStruct(text_state.shape, BF16)),
        in_specs=[pl.BlockSpec((rows, width), lambda h: (0, 0)), w_spec, w_spec, w_spec, s_spec],
        out_specs=(o_spec, o_spec, o_spec, s_spec),
        compiler_params=PARAMS,
        cost_estimate=cost(6 * rows * width * cols, 6 * width * cols, 3 * rows * cols),
        name="image_qkv",
    )(x, *weights, text_state)


def finish_kernel(intra, q, state, gain, out):
    total = intra[...] + dot(q[...], state[0])
    scale = lax.rsqrt(jnp.mean(total * total, axis=-1, keepdims=True) + 1e-06)
    out[...] = (total * scale * gain[...]).astype(BF16)


def finish(intra, q, state, gain):
    rows, cols = q.shape
    block = pl.BlockSpec((rows, HEAD_DIM), lambda h: (0, h))
    return pl.pallas_call(
        finish_kernel,
        grid=(cols // HEAD_DIM,),
        out_shape=jax.ShapeDtypeStruct((rows, cols), BF16),
        in_specs=[
            block,
            block,
            pl.BlockSpec((1, HEAD_DIM, HEAD_DIM), lambda h: (h, 0, 0)),
            pl.BlockSpec((1, HEAD_DIM), lambda h: (0, h)),
        ],
        out_specs=block,
        compiler_params=PARAMS,
        cost_estimate=cost(2 * rows * cols * HEAD_DIM, 8 * rows * cols),
        name="finish",
    )(intra, q, state, gain)


def mix_kernel(parts, has_before, meta, *refs):
    ins, (mix, *before, out) = refs[: len(parts)], refs[len(parts) :]
    head = meta[3]
    cols = mix.shape[3]
    for r in range(mix.shape[0]):
        total = before[0][:, r * cols : (r + 1) * cols] if has_before else 0.0
        for ref, offset in zip(ins, parts):
            total = total + dot(ref[...], mix[r, head ^ offset])
        out[:, r * cols : (r + 1) * cols] = total.astype(out.dtype)


def mix_part(meta, arrays, offsets, mix, before, dtype):
    rows, width = arrays[0].shape
    ratio, _, _, cols = mix.shape
    step = min(rows, 256)
    block = pl.BlockSpec((step, width), lambda i: (i, 0))
    out_block = pl.BlockSpec((step, ratio * cols), lambda i: (i, 0))
    whole = pl.BlockSpec(mix.shape, lambda i: (0, 0, 0, 0))
    extra = [] if before is None else [before]
    return pl.pallas_call(
        functools.partial(mix_kernel, tuple(offsets), before is not None),
        grid=(rows // step,),
        out_shape=jax.ShapeDtypeStruct((rows, ratio * cols), dtype),
        in_specs=[SMEM] + [block] * len(arrays) + [whole] + [out_block] * len(extra),
        out_specs=out_block,
        compiler_params=PARAMS,
        cost_estimate=cost(2 * rows * width * ratio * cols * len(arrays), 5e6),
        name="mix_part",
    )(meta, *arrays, mix, *extra)


def on_device(
    enc_rows,
    row_counts,
    row_places,
    stream,
    norm_gain,
    proj_in,
    proj_out,
    qkv_weight,
    head_gain,
    mix_weight,
):
    both = ("ctx", "head")
    capacity, enc_width = enc_rows.shape
    shard_rows, width = stream.shape
    n_ctx, n_head = lax.axis_size("ctx"), lax.axis_size("head")
    ctx, head = lax.axis_index("ctx"), lax.axis_index("head")
    live_total = n_head * (capacity // 4)
    core_rows = live_total // 2
    part_rows = live_total // n_head
    n_pairs = n_ctx // 2
    core, parity = head & 1, ctx & 1
    meta = jnp.stack([parity, core, ctx >> 1, head]).astype(jnp.int32)
    flat = [(c, h) for c in range(n_ctx) for h in range(n_head)]

    def along(axis, count, mask):
        return functools.partial(
            lax.ppermute, axis_name=axis, perm=[(i, i ^ mask) for i in range(count)]
        )

    def index(c, h):
        return c * n_head + h

    half = proj_in.shape[1] // 2
    in_halves = jnp.stack([proj_in[:, :half], proj_in[:, half:]])
    in_sends = jnp.broadcast_to(in_halves[None], (n_pairs,) + in_halves.shape).reshape(
        (n_ctx,) + in_halves.shape[1:]
    )
    in_full = lax.all_to_all(in_sends, "ctx", 0, 0).reshape(enc_width, half)

    out_cols = proj_out.shape[1]
    out_mine = lax.dynamic_slice(proj_out, (parity * half, 0), (half, out_cols))
    out_next = along("ctx", n_ctx, 1)(
        lax.dynamic_slice(proj_out, ((1 - parity) * half, 0), (half, out_cols))
    )

    ratio = n_ctx // n_head
    perm = [(index(c, h), index((c % ratio) * n_head + h, c // ratio)) for c, h in flat]
    mix_own = lax.ppermute(mix_weight, both, perm)

    group_rows = lax.all_gather(enc_rows, "head", axis=0, tiled=True)
    counts = row_counts[0]
    earlier = jnp.arange(n_head)[:, None] > jnp.arange(n_head)[None, :]
    starts = jnp.sum(jnp.where(earlier, counts[None, :], 0), axis=1)
    within = jnp.arange(capacity, dtype=jnp.int32)[None, :]
    spot = jnp.where(within < counts[:, None], starts[:, None] + within, -1).reshape(-1)
    wanted = core * core_rows + jnp.arange(core_rows, dtype=jnp.int32)
    own_picks = (spot[None, :] == wanted[:, None]).astype(BF16)
    own_rows = dot(own_picks, group_rows).astype(BF16)
    pair_rows = jnp.stack([own_rows, along("ctx", n_ctx, 1)(own_rows)])
    blocks = [pair_rows] + [along("ctx", n_ctx, 2 * k)(pair_rows) for k in range(1, n_pairs)]
    core_part = jnp.concatenate(blocks).reshape(-1, enc_width)
    other_part = along("head", n_head, 1)(core_part)

    keep, send = projector(meta, core_part, other_part, in_full, out_mine, out_next)
    ordered = order_rows(meta, keep, along("head", n_head, 1)(send), n_ctx)
    received = lax.all_to_all(ordered.reshape(n_ctx * n_head, part_rows, out_cols), both, 0, 0)
    received = received.reshape(n_pairs, 2, n_head // 2, 2, part_rows, out_cols)
    summed = jnp.sum(received.astype(F32), axis=(1, 2)).astype(BF16)
    img_part = summed.transpose(2, 0, 1, 3).reshape(part_rows, width)

    def norm(rows):
        widened = rows.astype(F32)
        return (
            widened
            * lax.rsqrt(jnp.mean(widened * widened, axis=-1, keepdims=True) + 1e-05)
            * norm_gain
        ).astype(BF16)

    image_rows = lax.all_gather(norm(img_part), "head", axis=0, tiled=True)

    local_places = row_places[0] - ctx * shard_rows
    picks = spot[None, :] == jnp.arange(live_total, dtype=jnp.int32)[:, None]
    places = jnp.sum(jnp.where(picks, local_places[None, :], 0), axis=1)
    put = jnp.arange(shard_rows, dtype=jnp.int32)[:, None] == places[None, :]
    is_text = jnp.logical_not(jnp.any(put, axis=1))[:, None]
    weights = [qkv_weight[:, i, :] for i in range(3)]
    text_rows = norm(stream)
    text_q, text_k, text_v = [
        jnp.where(is_text, jax.nn.silu(dot(text_rows, w)), 0.0).astype(BF16) for w in weights
    ]
    cols = text_q.shape[1]
    heads_dev = cols // HEAD_DIM

    def split(x):
        return x.reshape(x.shape[0], heads_dev, HEAD_DIM)

    text_state = jnp.einsum(
        "khd,khe->hde", split(text_k), split(text_v), preferred_element_type=F32
    )
    image_q, image_k, image_v, state = image_qkv(image_rows, weights, text_state)

    pieces = lax.all_to_all(state.reshape(n_ctx, -1, HEAD_DIM), "ctx", 0, 0).astype(F32)
    before = jnp.cumsum(pieces, axis=0) - pieces
    prefix = lax.all_to_all(before.astype(BF16), "ctx", 0, 0).reshape(state.shape)

    put = put.astype(BF16)

    def place(text, image):
        return (text.astype(F32) + dot(put, image)).astype(BF16)

    queries, key_rows, values = (
        place(text_q, image_q),
        place(text_k, image_k),
        place(text_v, image_v),
    )
    causal = jnp.tril(jnp.ones((shard_rows, shard_rows), dtype=bool))
    scores = jnp.einsum(
        "qhd,khd->hqk", split(queries), split(key_rows), preferred_element_type=F32
    )
    scores = jnp.where(causal, scores, 0.0).astype(BF16)
    intra = jnp.einsum("hqk,khd->qhd", scores, split(values), preferred_element_type=F32)
    intra = intra.reshape(shard_rows, cols)
    heads_out = finish(intra, queries, prefix, head_gain[None])

    mix_own, in_full = lax.optimization_barrier((mix_own, in_full))
    mix_full = lax.all_gather(mix_own, "ctx", axis=0)
    group_width, mix_cols = mix_weight.shape
    mix_full = mix_full.reshape(ratio, n_head, group_width, mix_cols)
    parts, offsets = [heads_out], [0]
    bit = n_head // 2
    while bit:
        parts = parts + [along("head", n_head, bit)(p) for p in parts]
        offsets = offsets + [o ^ bit for o in offsets]
        bit //= 2
    if mix_cols % 128 == 0:
        near = [i for i, o in enumerate(offsets) if o < 2]
        far = [i for i, o in enumerate(offsets) if o >= 2]
        first = mix_part(
            meta, [parts[i] for i in near], [offsets[i] for i in near], mix_full, None, F32
        )
        return mix_part(
            meta, [parts[i] for i in far], [offsets[i] for i in far], mix_full, first, BF16
        )
    total = 0.0
    for part, offset in zip(parts, offsets):
        group = lax.dynamic_index_in_dim(mix_full, head ^ offset, 1, keepdims=False)
        group = jnp.concatenate([group[r] for r in range(ratio)], axis=1)
        total = total + dot(part, group)
    return total.astype(BF16)


def solution(mesh):
    in_specs = (
        P(("ctx", "head"), None),
        P("ctx", None),
        P("ctx", None),
        P("ctx", None),
        P(),
        P("ctx", "head"),
        P("head", "ctx"),
        P(None, None, "head"),
        P("head"),
        P("head", "ctx"),
    )
    out_specs = P("ctx", "head")
    return jax.shard_map(
        on_device, mesh=mesh, in_specs=in_specs, out_specs=out_specs, check_vma=False
    )
```

time: 206 us -> 209 us (1.015); the launches traced: 203 us -> 208 us
  Pallas kernels: 0 us -> 16.5 us
  matrix products: 36.5 us -> 21.5 us
  waiting for transfers between devices: 59.7 us -> 72.4 us
  blocking collectives: 26.1 us -> 15.5 us
  local copies, waits for them, and re-layouts: 21.6 us -> 26 us
  starting transfers between devices: 38.3 us -> 35.5 us
    ppermute x7 -> x10, waiting for transfers between devices: 16.5 us -> 50.8 us  [the longest x3 42.6 us: on_device(): along('ctx', n_ctx, 2 * k)(pair_rows)]
    all_to_all x1, waiting for transfers between devices: 24.1 us -> 0.01 us  [on_device(): in_full = lax.all_to_all(in_sends, 'ctx', 0, 0).reshape(enc_width, half)]
    pallas_call x0 -> x6, Pallas kernels: none -> 16.5 us  [the longest x1 4.82 us: image_qkv(): pl.pallas_call(image_kernel, grid=(heads,), out_shape=(out, out, out, jax...]
    dot_general x13 -> x9, matrix products: 36.5 us -> 21.5 us  [the longest x7 18.6 us: dot(): return jnp.dot(a, b, preferred_element_type=F32)]
    all_to_all x1 -> x0, blocking collectives: 10.2 us -> none  [on_device(): pieces = lax.all_to_all(pieces, 'ctx', 0, 0).astype(F32)]
    all_to_all x3, starting transfers between devices: 17.4 us -> 10.1 us  [the longest x1 3.38 us: on_device(): lax.all_to_all(state.reshape(n_ctx, -1, HEAD_DIM), 'ctx', 0, 0).astype(F32)]
    squeeze x1, local copies, waits for them, and re-layouts: 2.15 us -> 6.09 us  [on_device(): weights = [qkv_weight[:, i, :] for i in range(3)]]
    all_to_all x3, waiting for transfers between devices: 18.3 us -> 21.6 us  [the longest x1 9.42 us: on_device(): lax.all_to_all(ordered.reshape(n_ctx * n_head, part_rows, out_cols), both...]
  transfers between devices with their start and end apart: 13 -> 16, of which waited for: 8 -> 6; matrix products, arithmetic and copies ran while one was open for 25% -> 21% of each run, Pallas kernels for 0% -> 7%
where the time goes in v2:
time: 209 us; the launch traced here: 208 us
  waiting for transfers between devices  72.4 us (35%)
  starting transfers between devices  35.5 us (17%)
  local copies, waits for them, and re-layouts  26 us (12%)
  matrix products  21.5 us (10%)
  Pallas kernels  16.5 us (8%)
  blocking collectives  15.5 us (7%)
  between operations  13.7 us (7%)
  other arithmetic  7.19 us (3%)
    ppermute x3, waiting for transfers between devices, on_device(): along('ctx', n_ctx, 2 * k)(pair_rows)  42.6 us
    dot_general x7, matrix products, dot(): return jnp.dot(a, b, preferred_element_type=F32)  18.6 us
    unnamed x47, local copies, waits for them, and re-layouts  10.3 us
    all_to_all x1, waiting for transfers between devices, on_device(): lax.all_to_all(ordered.reshape(n_ctx * n_head, part_rows, out_cols), both...  9.42 us
    all_gather x1, blocking collectives, on_device(): group_rows = lax.all_gather(enc_rows, 'head', axis=0, tiled=True)  8.71 us
    ppermute x3, waiting for transfers between devices, on_device(): parts = parts + [along('head', n_head, bit)(p) for p in parts]  8.18 us
    all_to_all x1, waiting for transfers between devices, on_device(): lax.all_to_all(state.reshape(n_ctx, -1, HEAD_DIM), 'ctx', 0, 0).astype(F32)  7.77 us
    all_gather x1, blocking collectives, on_device(): image_rows = lax.all_gather(norm(img_part), 'head', axis=0, tiled=True)  6.76 us
  transfers between devices with their start and end apart: 16, of which 6 were waited for; matrix products, arithmetic and copies ran while one was open for 21% of the time, Pallas kernels for 7%

profile of v2, /device:TPU:1, one launch (start us, length us, event | category | flops | bytes accessed | tf_op | source)
XLA Modules:
  0.0 208.3 jit_solution(17735227342234622687)
XLA Ops:
  8.2 8.7 %all_gather.12 = bf16[256,1024]{1,0:T(8,128)(2,1)S(1)} all-gather(bf16[64,1024]{1,0:T(8,128)(2,1)} %param.10), channel_id=1, replica_groups=mesh['ctx'=8,'head'=4] {'head'}, dimensions={0}, use_global_device_ids=true | all-gather | bytes 655360 | tf_op jit(solution)/shard_map/all_gather | solution.py:233
  19.0 2.4 %constant_dynamic-slice_fusion.1 = (bf16[768,384]{1,0:T(8,128)(2,1)}, bf16[768,384]{1,0:T(8,128)(2,1)}) fusion(bf16[1536,384]{1,0:T(8,128)(2,1)} %param.16, s32[]{:T(128)S(6)} %select_n.47, s32[]{:T(128)S(6)} %select_n.46), kind=kLoop, calls=%fused_computation.65 | loop fusion | bytes 2359304 | tf_op jit(solution)/shard_map/dynamic_slice | solution.py:226
  23.0 5.7 %all-to-all-start = ((bf16[8,128,768]{2,1,0:T(8,128)(2,1)}), bf16[8,128,768]{2,1,0:T(8,128)(2,1)}, u32[]{:S(2)}, u32[]{:S(2)}) async-start(bf16[8,128,768]{2,1,0:T(8,128)(2,1)} %bitcast.12), calls=%async_computation | async-start | bytes 3145728 | tf_op jit(solution)/shard_map/all_to_all | solution.py:221
  28.7 4.5 %collective-permute-start.9 = (bf16[512,384]{1,0:T(8,128)(2,1)}, bf16[512,384]{1,0:T(8,128)(2,1)S(1)}, u32[]{:S(2)}, u32[]{:S(2)}) collective-permute-start(bf16[512,384]{1,0:T(8,128)(2,1)} %param.19), channel_id=1, source_target_pairs={{0,0},{1,4},{2,8},{3,12},{4,16},{5,20},{6,24},{7,28},{8,1},{9,5},{... | collective-permute-start | bytes 1179656 | tf_op jit(solution)/shard_map/ppermute | solution.py:231
  34.1 6.1 %slice_bitcast_fusion.2 = (bf16[3072,512]{1,0:T(8,128)(2,1)S(1)}, bf16[3072,512]{1,0:T(8,128)(2,1)}, bf16[3072,512]{1,0:T(8,128)(2,1)}) fusion(bf16[3072,3,512]{2,0,1:T(8,128)(2,1)} %param.17), kind=kLoop, calls=%fused_computation.8 | loop fusion | bytes 18874368 | tf_op jit(solution)/shard_map/squeeze | solution.py:269
  41.3 2.6 %collective-permute-start.2 = (bf16[2,32,1024]{2,1,0:T(8,128)(2,1)S(1)}, bf16[2,32,1024]{2,1,0:T(8,128)(2,1)S(1)}, u32[]{:S(2)}, u32[]{:S(2)}) collective-permute-start(bf16[2,32,1024]{2,1,0:T(8,128)(2,1)S(1)} %pad_maximum_fusion.1), channel_id=1, source_target_pairs={{0,16},{4,20},{8,24},{12,28},{16,0},{20,4},{24,8},{28,12},{1,17},{... | collective-permute-start | bytes 393224 | tf_op jit(solution)/shard_map/ppermute | solution.py:243
  46.5 22.6 %collective-permute-done.1 = bf16[2,32,1024]{2,1,0:T(8,128)(2,1)S(1)} collective-permute-done((bf16[2,32,1024]{2,1,0:T(8,128)(2,1)S(1)}, bf16[2,32,1024]{2,1,0:T(8,128)(2,1)S(1)}, u32[]{:S(2)}, u32[]{:S(2)}) %collective-permute-start.1) | collective-permute-done | bytes 131104 | tf_op jit(solution)/shard_map/ppermute | solution.py:243
  69.7 20.0 %collective-permute-done.2 = bf16[2,32,1024]{2,1,0:T(8,128)(2,1)S(1)} collective-permute-done((bf16[2,32,1024]{2,1,0:T(8,128)(2,1)S(1)}, bf16[2,32,1024]{2,1,0:T(8,128)(2,1)S(1)}, u32[]{:S(2)}, u32[]{:S(2)}) %collective-permute-start.2) | collective-permute-done | bytes 131104 | tf_op jit(solution)/shard_map/ppermute | solution.py:243
  91.1 3.6 %collective-permute-start.4 = (bf16[256,1024]{1,0:T(8,128)(2,1)}, bf16[256,1024]{1,0:T(8,128)(2,1)}, u32[]{:S(2)}, u32[]{:S(2)}) collective-permute-start(bf16[256,1024]{1,0:T(8,128)(2,1)} %bitcast.9.own), channel_id=1, source_target_pairs={{0,1},{1,0},{2,3},{3,2},{4,5},{5,4},{6,7},{7,6},{8,9},{9,8},{10,11... | collective-permute-start | bytes 1572872 | tf_op jit(solution)/shard_map/ppermute | solution.py:245
  94.7 4.7 %select_convert_fusion.2 = bf16[512,512]{1,0:T(8,128)(2,1)} fusion(pred[512]{0:T(512)(128)(4,1)S(1)} %not.7, bf16[3072,3,512]{2,0,1:T(8,128)(2,1)} %param.17, bf16[512,3072]{1,0:T(8,128)(2,1)S(1)} %copy-done.7, f32[3072]{0:T(1024)S(1)} %copy-done.13, f32[512]{0:T(512)S(1)} %add_rsqrt_fusion), kind=kOutput, calls=%fused_computation.22 | convolution fusion | flops 1618477056 | bytes 6830592 | tf_op jit(solution)/shard_map/dot_general | solution.py:26
  103.4 4.0 %projector.1 = (bf16[512,384]{1,0:T(8,128)(2,1)S(1)}, bf16[512,384]{1,0:T(8,128)(2,1)S(1)}) custom-call(s32[4]{0:T(128)S(1)} %pad_add_fusion.meta, bf16[256,1024]{1,0:T(8,128)(2,1)} %bitcast.9.own, bf16[256,1024]{1,0:T(8,128)(2,1)} %collective-permute-done.4.other, bf16[1024,768]{1,0:T(8,128)(2,1)} %bitcast.13.first, bf16[768,384]{1,0:T(8,128)(2,1)S(1)} %copy-done.4, ...), custom_call_target="tpu_custom_call" | custom-call | flops 1409286144 | bytes 5000000 | tf_op jit(solution)/shard_map/projector/pallas_call | solution.py:58
  107.5 4.9 %select_convert_fusion.3 = bf16[512,512]{1,0:T(8,128)(2,1)} fusion(pred[512]{0:T(512)(128)(4,1)} %copy-done.19, bf16[3072,3,512]{2,0,1:T(8,128)(2,1)} %param.17, bf16[512,3072]{1,0:T(8,128)(2,1)S(1)} %copy-done.8, f32[3072]{0:T(1024)S(1)} %copy-done.13, f32[512]{0:T(512)} %copy-done.16), kind=kOutput, calls=%fused_computation.23 | convolution fusion | flops 1618477056 | bytes 6830592 | tf_op jit(solution)/shard_map/dot_general | solution.py:26
  113.7 3.3 %all-to-all-start.1 = ((bf16[32,16,384]{2,1,0:T(8,128)(2,1)}), bf16[32,16,384]{2,1,0:T(8,128)(2,1)}, u32[]{:S(2)}, u32[]{:S(2)}) async-start(bf16[32,16,384]{2,1,0:T(8,128)(2,1)} %bitcast.14), calls=%async_computation.1 | async-start | bytes 786432 | tf_op jit(solution)/shard_map/all_to_all | solution.py:249
  119.3 5.7 %fusion.31 = f32[512,512]{1,0:T(8,128)} fusion(bf16[3072,3,512]{2,0,1:T(8,128)(2,1)} %param.17, bf16[512,3072]{1,0:T(8,128)(2,1)} %param.13, f32[3072]{0:T(1024)S(1)} %copy-done.13, f32[512]{0:T(512)S(1)} %copy-done.17), kind=kOutput, calls=%fused_computation.68 | convolution fusion | flops 1616904192 | bytes 7354368 | tf_op jit(solution)/shard_map/dot_general | solution.py:26
  125.0 9.4 %all-to-all-done.1 = bf16[32,16,384]{2,1,0:T(8,128)(2,1)} async-done(((bf16[32,16,384]{2,1,0:T(8,128)(2,1)}), bf16[32,16,384]{2,1,0:T(8,128)(2,1)}, u32[]{:S(2)}, u32[]{:S(2)}) %all-to-all-start.1) | async-done | bytes 393248 | tf_op jit(solution)/shard_map/all_to_all | solution.py:249
  139.4 6.8 %all_gather.13.x = bf16[64,3072]{1,0:T(8,128)(2,1)S(1)} all-gather(bf16[16,3072]{1,0:T(8,128)(2,1)S(1)} %multiply_convert_fusion), channel_id=1, replica_groups=mesh['ctx'=8,'head'=4] {'head'}, dimensions={0}, use_global_device_ids=true | all-gather | bytes 491520 | tf_op jit(solution)/shard_map/all_gather | solution.py:262
  149.9 4.8 %image_qkv.1 = (bf16[64,512]{1,0:T(8,128)(2,1)S(1)}, bf16[64,512]{1,0:T(8,128)(2,1)S(1)}, bf16[64,512]{1,0:T(8,128)(2,1)S(1)}, bf16[4,128,128]{2,1,0:T(8,128)(2,1)}) custom-call(bf16[64,3072]{1,0:T(8,128)(2,1)S(1)} %all_gather.13.x, bf16[3072,512]{1,0:T(8,128)(2,1)S(1)} %copy-done.1, bf16[3072,512]{1,0:T(8,128)(2,1)S(1)} %copy-done, ...), custom_call_target="tpu_custom_call" | custom-call | flops 603979776 | bytes 9437184 | tf_op jit(solution)/shard_map/image_qkv/pallas_call | solution.py:114
  155.4 3.4 %all-to-all-start.2 = ((bf16[8,64,128]{2,1,0:T(8,128)(2,1)}), bf16[8,64,128]{2,1,0:T(8,128)(2,1)S(1)}, u32[]{:S(2)}, u32[]{:S(2)}) async-start(bf16[8,64,128]{2,1,0:T(8,128)(2,1)} %bitcast.23), calls=%async_computation.2 | async-start | bytes 262144 | tf_op jit(solution)/shard_map/all_to_all | solution.py:285
  160.8 7.8 %all-to-all-done.2 = bf16[8,64,128]{2,1,0:T(8,128)(2,1)S(1)} async-done(((bf16[8,64,128]{2,1,0:T(8,128)(2,1)}), bf16[8,64,128]{2,1,0:T(8,128)(2,1)S(1)}, u32[]{:S(2)}, u32[]{:S(2)}) %all-to-all-start.2) | async-done | bytes 131104 | tf_op jit(solution)/shard_map/all_to_all | solution.py:285
  169.2 3.4 %all-to-all-start.3 = ((bf16[8,64,128]{2,1,0:T(8,128)(2,1)}), bf16[8,64,128]{2,1,0:T(8,128)(2,1)S(1)}, u32[]{:S(2)}, u32[]{:S(2)}) async-start(bf16[8,64,128]{2,1,0:T(8,128)(2,1)} %fusion.8), calls=%async_computation.3 | async-start | bytes 262144 | tf_op jit(solution)/shard_map/all_to_all | solution.py:287
  174.4 4.5 %all-to-all-done.3 = bf16[8,64,128]{2,1,0:T(8,128)(2,1)S(1)} async-done(((bf16[8,64,128]{2,1,0:T(8,128)(2,1)}), bf16[8,64,128]{2,1,0:T(8,128)(2,1)S(1)}, u32[]{:S(2)}, u32[]{:S(2)}) %all-to-all-start.3) | async-done | bytes 131104 | tf_op jit(solution)/shard_map/all_to_all | solution.py:287
  183.6 8.2 %collective-permute-done.7.refs_0_ = bf16[512,512]{1,0:T(8,128)(2,1)S(1)} collective-permute-done((bf16[512,512]{1,0:T(8,128)(2,1)S(1)}, bf16[512,512]{1,0:T(8,128)(2,1)S(1)}, u32[]{:S(2)}, u32[]{:S(2)}) %collective-permute-start.7) | collective-permute-done | bytes 524320 | tf_op jit(solution)/shard_map/ppermute | solution.py:315
  191.8 3.0 %collective-permute-start.8 = (bf16[512,512]{1,0:T(8,128)(2,1)S(1)}, bf16[512,512]{1,0:T(8,128)(2,1)S(1)}, u32[]{:S(2)}, u32[]{:S(2)}) collective-permute-start(bf16[512,512]{1,0:T(8,128)(2,1)S(1)} %collective-permute-done.7.refs_0_), channel_id=1, source_target_pairs={{0,1},{1,0},{2,3},{3,2},{4,5},{5,4},{6,7},{7,6},{8,9},{9,8},{10,11... | collective-permute-start | bytes 1572872 | tf_op jit(solution)/shard_map/ppermute | solution.py:315
  198.7 2.8 %mix_part.3 = bf16[512,768]{1,0:T(8,128)(2,1)} custom-call(s32[4]{0:T(128)S(1)} %pad_add_fusion.meta, bf16[512,512]{1,0:T(8,128)(2,1)S(1)} %collective-permute-done.7.refs_0_, bf16[512,512]{1,0:T(8,128)(2,1)S(1)} %collective-permute-done.8.refs_1_, bf16[2,4,512,384]{3,2,1,0:T(8,128)(2,1)S(1)} %bitcast.72, f32[512,768]{1,0:T(8,128)S(1)} %mix_part.2.refs_3_), custom_call_target="tpu_custom_call" | custom-call | flops 805306368 | bytes 5000000 | tf_op jit(solution)/shard_map/mix_part/pallas_call | solution.py:171
  (103 shorter events, 41.9 us)
Async XLA Ops:
  6.5 15.1 %copy-start.10 = (bf16[128,1536]{1,0:T(8,128)(2,1)S(1)}, bf16[128,1536]{1,0:T(8,128)(2,1)}, u32[]{:S(2)}) copy-start(bf16[128,1536]{1,0:T(8,128)(2,1)} %param.15) | copy-start | bytes 1179652
  17.8 22.5 %collective-permute-start = (bf16[32,1024]{1,0:T(8,128)(2,1)}, bf16[32,1024]{1,0:T(8,128)(2,1)}, u32[]{:S(2)}, u32[]{:S(2)}) collective-permute-start(bf16[32,1024]{1,0:T(8,128)(2,1)} %get-tuple-element.27), channel_id=1, source_target_pairs={{0,4},{4,0},{8,12},{12,8},{16,20},{20,16},{24,28},{28,24},{1,5},{5... | collective-permute-start | bytes 196616 | tf_op jit(solution)/shard_map/ppermute | solution.py:242
  21.4 80.9 %collective-permute-start.5 = (bf16[768,384]{1,0:T(8,128)(2,1)}, bf16[768,384]{1,0:T(8,128)(2,1)}, u32[]{:S(2)}, u32[]{:S(2)}) collective-permute-start(bf16[768,384]{1,0:T(8,128)(2,1)} %get-tuple-element.22), channel_id=1, source_target_pairs={{0,4},{4,0},{8,12},{12,8},{16,20},{20,16},{24,28},{28,24},{1,5},{5... | collective-permute-start | bytes 1769480 | tf_op jit(solution)/shard_map/ppermute | solution.py:225
  21.6 11.5 %copy-start.6 = (bf16[512,3072]{1,0:T(8,128)(2,1)S(1)}, bf16[512,3072]{1,0:T(8,128)(2,1)}, u32[]{:S(2)}) copy-start(bf16[512,3072]{1,0:T(8,128)(2,1)} %param.13) | copy-start | bytes 9437188
  23.0 10.9 %copy-start.18 = (s32[1,256]{1,0:T(1,128)S(1)}, s32[1,256]{1,0:T(1,128)}, u32[]{:S(2)}) copy-start(s32[1,256]{1,0:T(1,128)} %param.12) | copy-start | bytes 3076
  23.0 78.6 %all-to-all-start = ((bf16[8,128,768]{2,1,0:T(8,128)(2,1)}), bf16[8,128,768]{2,1,0:T(8,128)(2,1)}, u32[]{:S(2)}, u32[]{:S(2)}) async-start(bf16[8,128,768]{2,1,0:T(8,128)(2,1)} %bitcast.12), calls=%async_computation | async-start | bytes 3145728 | tf_op jit(solution)/shard_map/all_to_all | solution.py:221
  28.6 166.1 %all-gather.3.cloned.1.call-start = ((), (), s32[]{:S(2)}) async-start(), calls=%async_computation.4 | async-start | bytes 3538944 | tf_op jit(solution)/shard_map/all_gather | solution.py:309
  28.7 72.8 %collective-permute-start.9 = (bf16[512,384]{1,0:T(8,128)(2,1)}, bf16[512,384]{1,0:T(8,128)(2,1)S(1)}, u32[]{:S(2)}, u32[]{:S(2)}) collective-permute-start(bf16[512,384]{1,0:T(8,128)(2,1)} %param.19), channel_id=1, source_target_pairs={{0,0},{1,4},{2,8},{3,12},{4,16},{5,20},{6,24},{7,28},{8,1},{9,5},{... | collective-permute-start | bytes 1179656 | tf_op jit(solution)/shard_map/ppermute | solution.py:231
  33.9 60.8 %copy-start.16 = (f32[512]{0:T(512)}, f32[512]{0:T(512)S(1)}, u32[]{:S(2)}) copy-start(f32[512]{0:T(512)S(1)} %add_rsqrt_fusion) | copy-start | bytes 6148
  34.0 60.6 %copy-start.7 = (bf16[512,3072]{1,0:T(8,128)(2,1)S(1)}, bf16[512,3072]{1,0:T(8,128)(2,1)}, u32[]{:S(2)}) copy-start(bf16[512,3072]{1,0:T(8,128)(2,1)} %param.13) | copy-start | bytes 9437188
  34.1 60.6 %copy-start.13 = (f32[3072]{0:T(1024)S(1)}, f32[3072]{0:T(1024)}, u32[]{:S(2)}) copy-start(f32[3072]{0:T(1024)} %param.14) | copy-start | bytes 36868
  40.3 54.4 %copy-start.19 = (pred[512]{0:T(512)(128)(4,1)}, pred[512]{0:T(512)(128)(4,1)S(1)}, u32[]{:S(2)}) copy-start(pred[512]{0:T(512)(128)(4,1)S(1)} %not.7) | copy-start | bytes 1540
  41.2 27.9 %collective-permute-start.1 = (bf16[2,32,1024]{2,1,0:T(8,128)(2,1)S(1)}, bf16[2,32,1024]{2,1,0:T(8,128)(2,1)S(1)}, u32[]{:S(2)}, u32[]{:S(2)}) collective-permute-start(bf16[2,32,1024]{2,1,0:T(8,128)(2,1)S(1)} %pad_maximum_fusion.1), channel_id=1, source_target_pairs={{0,8},{4,12},{8,0},{12,4},{16,24},{20,28},{24,16},{28,20},{1,9},{5... | collective-permute-start | bytes 393224 | tf_op jit(solution)/shard_map/ppermute | solution.py:243
  41.3 48.5 %collective-permute-start.2 = (bf16[2,32,1024]{2,1,0:T(8,128)(2,1)S(1)}, bf16[2,32,1024]{2,1,0:T(8,128)(2,1)S(1)}, u32[]{:S(2)}, u32[]{:S(2)}) collective-permute-start(bf16[2,32,1024]{2,1,0:T(8,128)(2,1)S(1)} %pad_maximum_fusion.1), channel_id=1, source_target_pairs={{0,16},{4,20},{8,24},{12,28},{16,0},{20,4},{24,8},{28,12},{1,17},{... | collective-permute-start | bytes 393224 | tf_op jit(solution)/shard_map/ppermute | solution.py:243
  43.9 46.5 %collective-permute-start.3 = (bf16[2,32,1024]{2,1,0:T(8,128)(2,1)S(1)}, bf16[2,32,1024]{2,1,0:T(8,128)(2,1)S(1)}, u32[]{:S(2)}, u32[]{:S(2)}) collective-permute-start(bf16[2,32,1024]{2,1,0:T(8,128)(2,1)S(1)} %pad_maximum_fusion.1), channel_id=1, source_target_pairs={{0,24},{4,28},{8,16},{12,20},{16,8},{20,12},{24,0},{28,4},{1,25},{... | collective-permute-start | bytes 393224 | tf_op jit(solution)/shard_map/ppermute | solution.py:243
  91.1 11.2 %collective-permute-start.4 = (bf16[256,1024]{1,0:T(8,128)(2,1)}, bf16[256,1024]{1,0:T(8,128)(2,1)}, u32[]{:S(2)}, u32[]{:S(2)}) collective-permute-start(bf16[256,1024]{1,0:T(8,128)(2,1)} %bitcast.9.own), channel_id=1, source_target_pairs={{0,1},{1,0},{2,3},{3,2},{4,5},{5,4},{6,7},{7,6},{8,9},{9,8},{10,11... | collective-permute-start | bytes 1572872 | tf_op jit(solution)/shard_map/ppermute | solution.py:245
  107.4 5.0 %collective-permute-start.6 = (bf16[512,384]{1,0:T(8,128)(2,1)S(1)}, bf16[512,384]{1,0:T(8,128)(2,1)S(1)}, u32[]{:S(2)}, u32[]{:S(2)}) collective-permute-start(bf16[512,384]{1,0:T(8,128)(2,1)S(1)} %get-tuple-element.13), channel_id=1, source_target_pairs={{0,1},{1,0},{2,3},{3,2},{4,5},{5,4},{6,7},{7,6},{8,9},{9,8},{10,11... | collective-permute-start | bytes 1179656 | tf_op jit(solution)/shard_map/ppermute | solution.py:248
  113.7 20.7 %all-to-all-start.1 = ((bf16[32,16,384]{2,1,0:T(8,128)(2,1)}), bf16[32,16,384]{2,1,0:T(8,128)(2,1)}, u32[]{:S(2)}, u32[]{:S(2)}) async-start(bf16[32,16,384]{2,1,0:T(8,128)(2,1)} %bitcast.14), calls=%async_computation.1 | async-start | bytes 786432 | tf_op jit(solution)/shard_map/all_to_all | solution.py:249
  155.4 13.2 %all-to-all-start.2 = ((bf16[8,64,128]{2,1,0:T(8,128)(2,1)}), bf16[8,64,128]{2,1,0:T(8,128)(2,1)S(1)}, u32[]{:S(2)}, u32[]{:S(2)}) async-start(bf16[8,64,128]{2,1,0:T(8,128)(2,1)} %bitcast.23), calls=%async_computation.2 | async-start | bytes 262144 | tf_op jit(solution)/shard_map/all_to_all | solution.py:285
  160.2 12.4 %copy-start.12 = (pred[512,512]{1,0:T(8,128)(4,1)S(1)}, pred[512,512]{1,0:T(8,128)(4,1)}, u32[]{:S(2)}) copy-start(pred[512,512]{1,0:T(8,128)(4,1)} %iota_compare_fusion) | copy-start | bytes 786436
  169.2 9.6 %all-to-all-start.3 = ((bf16[8,64,128]{2,1,0:T(8,128)(2,1)}), bf16[8,64,128]{2,1,0:T(8,128)(2,1)S(1)}, u32[]{:S(2)}, u32[]{:S(2)}) async-start(bf16[8,64,128]{2,1,0:T(8,128)(2,1)} %fusion.8), calls=%async_computation.3 | async-start | bytes 262144 | tf_op jit(solution)/shard_map/all_to_all | solution.py:287
  180.4 11.4 %collective-permute-start.7 = (bf16[512,512]{1,0:T(8,128)(2,1)S(1)}, bf16[512,512]{1,0:T(8,128)(2,1)S(1)}, u32[]{:S(2)}, u32[]{:S(2)}) collective-permute-start(bf16[512,512]{1,0:T(8,128)(2,1)S(1)} %finish.1.refs_0_), channel_id=1, source_target_pairs={{0,2},{1,3},{2,0},{3,1},{4,6},{5,7},{6,4},{7,5},{8,10},{9,11},{10,... | collective-permute-start | bytes 1572872 | tf_op jit(solution)/shard_map/ppermute | solution.py:315
  181.3 13.5 %collective-permute-start.10 = (bf16[512,512]{1,0:T(8,128)(2,1)S(1)}, bf16[512,512]{1,0:T(8,128)(2,1)S(1)}, u32[]{:S(2)}, u32[]{:S(2)}) collective-permute-start(bf16[512,512]{1,0:T(8,128)(2,1)S(1)} %finish.1.refs_0_), channel_id=1, source_target_pairs={{0,1},{1,0},{2,3},{3,2},{4,5},{5,4},{6,7},{7,6},{8,9},{9,8},{10,11... | collective-permute-start | bytes 1572872 | tf_op jit(solution)/shard_map/ppermute | solution.py:315
  191.8 6.9 %collective-permute-start.8 = (bf16[512,512]{1,0:T(8,128)(2,1)S(1)}, bf16[512,512]{1,0:T(8,128)(2,1)S(1)}, u32[]{:S(2)}, u32[]{:S(2)}) collective-permute-start(bf16[512,512]{1,0:T(8,128)(2,1)S(1)} %collective-permute-done.7.refs_0_), channel_id=1, source_target_pairs={{0,1},{1,0},{2,3},{3,2},{4,5},{5,4},{6,7},{7,6},{8,9},{9,8},{10,11... | collective-permute-start | bytes 1572872 | tf_op jit(solution)/shard_map/ppermute | solution.py:315
  (14 other events, 53.6 us)
Sparse Core Ops, SparseCore 0:
  102.4 67.4 all-gather.2

commit v3 on v2

--- a/solution.py
+++ b/solution.py
@@ -30,11 +30,31 @@
     return x * (1.0 / (1.0 + jnp.exp(-x)))
 
 
-def projector_kernel(chunk, meta, own, other, first, second, second_next, keep, send, w_keep, w_send):
+def nothing(source, out):
+    pass
+
+
+def weighty(x, flops, nbytes):
+    return pl.pallas_call(
+        nothing,
+        out_shape=jax.ShapeDtypeStruct(x.shape, x.dtype),
+        in_specs=[pl.BlockSpec(memory_space=pl.ANY)],
+        out_specs=pl.BlockSpec(memory_space=pl.ANY),
+        input_output_aliases={0: 0},
+        cost_estimate=cost(flops, nbytes),
+        name="weighty",
+    )(x)
+
+
+def projector_kernel(chunk, span, meta, own, other, first, *refs):
+    seconds, (keep, send, w_keep, w_send) = refs[:span], refs[span:]
+    cols = seconds[0].shape[1]
     same = meta[0] == meta[1]
-    mine, near = second[...], second_next[...]
-    w_keep[...] = jnp.where(same, mine, near)
-    w_send[...] = jnp.where(same, near, mine)
+    for m in range(0, span, 2):
+        mine, near = seconds[m][...], seconds[m + 1][...]
+        slot = (meta[4] ^ m) >> 1
+        w_keep[slot] = jnp.where(same, mine, near)
+        w_send[slot] = jnp.where(same, near, mine)
     rows = own.shape[0]
 
     def run(source, base):
@@ -44,52 +64,115 @@
             to = pl.ds(pl.multiple_of(base + i * chunk, chunk), chunk)
             pre = dot(source[at, :], first[...])
             hid = (0.5 * pre * (1.0 + lax.erf(pre * 0.7071067811865476))).astype(BF16)
-            keep[to, :] = dot(hid, w_keep[...]).astype(BF16)
-            send[to, :] = dot(hid, w_send[...]).astype(BF16)
+            for n in range(span // 2):
+                keep[to, n * cols : (n + 1) * cols] = dot(hid, w_keep[n]).astype(BF16)
+                send[to, n * cols : (n + 1) * cols] = dot(hid, w_send[n]).astype(BF16)
 
     run(own, 0)
     run(other, rows)
 
 
-def projector(meta, own, other, first, second, second_next):
+def projector(meta, own, other, first, seconds):
     rows, width = own.shape
-    units, cols = second.shape
-    out = jax.ShapeDtypeStruct((2 * rows, cols), BF16)
-    return pl.pallas_call(
-        functools.partial(projector_kernel, min(rows, 256)),
+    units, cols = seconds[0].shape
+    span = len(seconds)
+    out = jax.ShapeDtypeStruct((2 * rows, span // 2 * cols), BF16)
+    scratch = pltpu.VMEM((span // 2, units, cols), BF16)
+    return pl.pallas_call(
+        functools.partial(projector_kernel, min(rows, 256), span),
         out_shape=(out, out),
-        in_specs=[SMEM] + [VMEM] * 5,
+        in_specs=[SMEM] + [VMEM] * (3 + span),
         out_specs=(VMEM, VMEM),
-        scratch_shapes=[pltpu.VMEM((units, cols), BF16), pltpu.VMEM((units, cols), BF16)],
+        scratch_shapes=[scratch, scratch],
+        compiler_params=pltpu.CompilerParams(vmem_limit_bytes=60 * 1024 * 1024),
+        cost_estimate=cost(4 * rows * units * (width + span * cols), 5e6, 2 * rows * units),
+        name="projector",
+    )(meta, own, other, first, *seconds)
+
+
+def pick_kernel(spot, *refs):
+    sources, out = refs[:-1], refs[-1]
+    rows = out.shape[0]
+    wanted = lax.broadcasted_iota(jnp.int32, (rows, spot.shape[1]), 0)
+    at, total = 0, 0.0
+    for ref in sources:
+        count = ref.shape[0]
+        picks = (spot[:, at : at + count] == wanted[:, at : at + count]).astype(F32).astype(BF16)
+        total = total + dot(picks, ref[...])
+        at += count
+    out[...] = total.astype(BF16)
+
+
+def pick_rows(spot, sources, rows):
+    width = sources[0].shape[1]
+    return pl.pallas_call(
+        pick_kernel,
+        out_shape=jax.ShapeDtypeStruct((rows, width), BF16),
+        in_specs=[VMEM] * (1 + len(sources)),
+        out_specs=VMEM,
         compiler_params=PARAMS,
-        cost_estimate=cost(4 * rows * units * (width + 2 * cols), 5e6, 2 * rows * units),
-        name="projector",
-    )(meta, own, other, first, second, second_next)
-
-
-def order_kernel(pairs, meta, keep, got, out):
-    parity, core, pair = meta[0], meta[1], meta[2]
-    rows = out.shape[2]
+        cost_estimate=cost(2 * rows * width * spot.shape[1], 2 * width * spot.shape[1]),
+        name="pick_rows",
+    )(spot, *sources)
+
+
+def order_kernel(offsets, meta, keep, got, out):
+    core, ctx = meta[1], meta[2]
+    rows, count = out.shape[2], len(offsets)
     for i in range(2):
-        for k in range(pairs):
-            for j in range(2):
-                at = pl.ds(((i * pairs + k) * 2 + j) * rows, rows)
-                there = pl.ds((((1 - i) * pairs + k) * 2 + j) * rows, rows)
-                total = keep[at, :].astype(F32) + got[there, :].astype(F32)
-                out[(pair ^ k) * 2 + (parity ^ j), core ^ i] = total.astype(BF16)
-
-
-def order_rows(meta, keep, got, n_ctx):
+        for b, offset in enumerate(offsets):
+            at = pl.ds((i * count + b) * rows, rows)
+            there = pl.ds(((1 - i) * count + b) * rows, rows)
+            total = keep[at, :].astype(F32) + got[there, :].astype(F32)
+            out[ctx ^ offset, core ^ i] = total.astype(BF16)
+
+
+def order_rows(meta, keep, got, offsets):
     rows, cols = keep.shape
-    return pl.pallas_call(
-        functools.partial(order_kernel, n_ctx // 2),
-        out_shape=jax.ShapeDtypeStruct((n_ctx, 2, rows // n_ctx // 2, cols), BF16),
+    count = len(offsets)
+    return pl.pallas_call(
+        functools.partial(order_kernel, tuple(offsets)),
+        out_shape=jax.ShapeDtypeStruct((count, 2, rows // count // 2, cols), BF16),
         in_specs=[SMEM, VMEM, VMEM],
         out_specs=VMEM,
         compiler_params=PARAMS,
         cost_estimate=cost(rows * cols, 6 * rows * cols),
         name="order_rows",
     )(meta, keep, got)
+
+
+def image_norm_kernel(groups, span, heads, got, gain, out, total):
+    wide = span // 2
+    cols = got.shape[2] // wide
+    square = 0.0
+    for g in range(groups):
+        for core in range(2):
+            part = 0.0
+            for s in range(span):
+                for h in range(heads // 2):
+                    part = part + got[((g * span + s) * heads) + 2 * h + core].astype(F32)
+            part = part.astype(BF16).astype(F32)
+            square = square + jnp.sum(part * part, axis=-1, keepdims=True)
+            for n in range(wide):
+                c = g * span + 2 * n + core
+                total[:, c * cols : (c + 1) * cols] = part[:, n * cols : (n + 1) * cols]
+    scale = lax.rsqrt(square / total.shape[1] + 1e-05)
+    out[...] = (total[...] * scale * gain[...]).astype(BF16)
+
+
+def image_norm(got, gain, n_ctx, span):
+    devices, rows, _ = got.shape
+    width = gain.shape[1]
+    return pl.pallas_call(
+        functools.partial(image_norm_kernel, n_ctx // span, span, devices // n_ctx),
+        out_shape=jax.ShapeDtypeStruct((rows, width), BF16),
+        in_specs=[VMEM, VMEM],
+        out_specs=VMEM,
+        scratch_shapes=[pltpu.VMEM((rows, width), F32)],
+        compiler_params=PARAMS,
+        cost_estimate=cost(4 * got.size, 2 * got.size),
+        name="image_norm",
+    )(got, gain)
 
 
 def image_kernel(x, wq, wk, wv, text_state, q, k, v, state):
@@ -117,7 +200,7 @@
         out_shape=(out, out, out, jax.ShapeDtypeStruct(text_state.shape, BF16)),
         in_specs=[pl.BlockSpec((rows, width), lambda h: (0, 0)), w_spec, w_spec, w_spec, s_spec],
         out_specs=(o_spec, o_spec, o_spec, s_spec),
-        compiler_params=PARAMS,
+        compiler_params=pltpu.CompilerParams(vmem_limit_bytes=60 * 1024 * 1024),
         cost_estimate=cost(6 * rows * width * cols, 6 * width * cols, 3 * rows * cols),
         name="image_qkv",
     )(x, *weights, text_state)
@@ -149,27 +232,29 @@
     )(intra, q, state, gain)
 
 
-def mix_kernel(parts, has_before, meta, *refs):
+def mix_kernel(parts, has_before, count, meta, *refs):
     ins, (mix, *before, out) = refs[: len(parts)], refs[len(parts) :]
     head = meta[3]
     cols = mix.shape[3]
-    for r in range(mix.shape[0]):
+    for r in range(mix.shape[1]):
         total = before[0][:, r * cols : (r + 1) * cols] if has_before else 0.0
         for ref, offset in zip(ins, parts):
-            total = total + dot(ref[...], mix[r, head ^ offset])
+            group = head ^ offset
+            place = head ^ ((group >> 1) | ((group & 1) * (count // 2)))
+            total = total + dot(ref[...], mix[place, r])
         out[:, r * cols : (r + 1) * cols] = total.astype(out.dtype)
 
 
 def mix_part(meta, arrays, offsets, mix, before, dtype):
     rows, width = arrays[0].shape
-    ratio, _, _, cols = mix.shape
+    count, ratio, _, cols = mix.shape
     step = min(rows, 256)
     block = pl.BlockSpec((step, width), lambda i: (i, 0))
     out_block = pl.BlockSpec((step, ratio * cols), lambda i: (i, 0))
     whole = pl.BlockSpec(mix.shape, lambda i: (0, 0, 0, 0))
     extra = [] if before is None else [before]
     return pl.pallas_call(
-        functools.partial(mix_kernel, tuple(offsets), before is not None),
+        functools.partial(mix_kernel, tuple(offsets), before is not None, count),
         grid=(rows // step,),
         out_shape=jax.ShapeDtypeStruct((rows, ratio * cols), dtype),
         in_specs=[SMEM] + [block] * len(arrays) + [whole] + [out_block] * len(extra),
@@ -202,7 +287,9 @@
     part_rows = live_total // n_head
     n_pairs = n_ctx // 2
     core, parity = head & 1, ctx & 1
-    meta = jnp.stack([parity, core, ctx >> 1, head]).astype(jnp.int32)
+    span = 4
+    spot_in = ctx & (span - 1)
+    meta = jnp.stack([parity, core, ctx, head, spot_in]).astype(jnp.int32)
     flat = [(c, h) for c in range(n_ctx) for h in range(n_head)]
 
     def along(axis, count, mask):
@@ -213,43 +300,44 @@
     def index(c, h):
         return c * n_head + h
 
-    half = proj_in.shape[1] // 2
-    in_halves = jnp.stack([proj_in[:, :half], proj_in[:, half:]])
-    in_sends = jnp.broadcast_to(in_halves[None], (n_pairs,) + in_halves.shape).reshape(
-        (n_ctx,) + in_halves.shape[1:]
-    )
-    in_full = lax.all_to_all(in_sends, "ctx", 0, 0).reshape(enc_width, half)
+    ratio = n_ctx // n_head
+
+    def turned(h):
+        return (h >> 1) | ((h & 1) * (n_head // 2))
+
+    perm = [(index(c, h), index(c ^ (turned(h) * ratio), h)) for c, h in flat]
+    mix_own = lax.ppermute(mix_weight, both, perm)
+    perm = [(index(c, h), index(c, (c // ratio) ^ turned(h))) for c, h in flat]
+    mix_own = lax.ppermute(mix_own, both, perm)
+
+    part = proj_in.shape[1] // span
+    in_parts = proj_in.reshape(-1, span, part).transpose(1, 0, 2)
+    in_sends = jnp.broadcast_to(in_parts[None], (n_ctx // span,) + in_parts.shape).reshape(
+        (n_ctx,) + in_parts.shape[1:]
+    )
+    in_full = weighty(lax.all_to_all(in_sends, "ctx", 0, 0), 1e11, 4e8).reshape(enc_width, part)
 
     out_cols = proj_out.shape[1]
-    out_mine = lax.dynamic_slice(proj_out, (parity * half, 0), (half, out_cols))
-    out_next = along("ctx", n_ctx, 1)(
-        lax.dynamic_slice(proj_out, ((1 - parity) * half, 0), (half, out_cols))
-    )
-
-    ratio = n_ctx // n_head
-    perm = [(index(c, h), index((c % ratio) * n_head + h, c // ratio)) for c, h in flat]
-    mix_own = lax.ppermute(mix_weight, both, perm)
-
-    group_rows = lax.all_gather(enc_rows, "head", axis=0, tiled=True)
+
+    sources, swaps = [enc_rows], [0]
+    bit = n_head // 2
+    while bit:
+        sources = sources + [along("head", n_head, bit)(x) for x in sources]
+        swaps = swaps + [o ^ bit for o in swaps]
+        bit //= 2
     counts = row_counts[0]
     earlier = jnp.arange(n_head)[:, None] > jnp.arange(n_head)[None, :]
     starts = jnp.sum(jnp.where(earlier, counts[None, :], 0), axis=1)
     within = jnp.arange(capacity, dtype=jnp.int32)[None, :]
-    spot = jnp.where(within < counts[:, None], starts[:, None] + within, -1).reshape(-1)
-    wanted = core * core_rows + jnp.arange(core_rows, dtype=jnp.int32)
-    own_picks = (spot[None, :] == wanted[:, None]).astype(BF16)
-    own_rows = dot(own_picks, group_rows).astype(BF16)
-    pair_rows = jnp.stack([own_rows, along("ctx", n_ctx, 1)(own_rows)])
-    blocks = [pair_rows] + [along("ctx", n_ctx, 2 * k)(pair_rows) for k in range(1, n_pairs)]
-    core_part = jnp.concatenate(blocks).reshape(-1, enc_width)
-    other_part = along("head", n_head, 1)(core_part)
-
-    keep, send = projector(meta, core_part, other_part, in_full, out_mine, out_next)
-    ordered = order_rows(meta, keep, along("head", n_head, 1)(send), n_ctx)
-    received = lax.all_to_all(ordered.reshape(n_ctx * n_head, part_rows, out_cols), both, 0, 0)
-    received = received.reshape(n_pairs, 2, n_head // 2, 2, part_rows, out_cols)
-    summed = jnp.sum(received.astype(F32), axis=(1, 2)).astype(BF16)
-    img_part = summed.transpose(2, 0, 1, 3).reshape(part_rows, width)
+    spot = jnp.where(within < counts[:, None], starts[:, None] + within, -1)
+    owners = jnp.arange(n_head)[None, :] == (head ^ jnp.array(swaps, dtype=jnp.int32))[:, None]
+    swapped = jnp.sum(jnp.where(owners[:, :, None], spot[None], 0), axis=1)
+    own_rows = pick_rows(swapped.reshape(1, -1) - core * core_rows, sources, core_rows)
+
+    seconds = []
+    for m in range(span):
+        block = lax.dynamic_slice(proj_out, ((spot_in ^ m) * part, 0), (part, out_cols))
+        seconds.append(along("ctx", n_ctx, m)(block) if m else block)
 
     def norm(rows):
         widened = rows.astype(F32)
@@ -259,21 +347,53 @@
             * norm_gain
         ).astype(BF16)
 
-    image_rows = lax.all_gather(norm(img_part), "head", axis=0, tiled=True)
-
+    def spread(x, mask):
+        return jnp.concatenate([x, along("ctx", n_ctx, mask)(x)])
+
+    masks = [1 << n for n in reversed(range(n_ctx.bit_length() - 1))]
+    masks = masks[-1:] + masks[:-1]
+    offsets_ctx = [0]
+    for mask in masks:
+        offsets_ctx = offsets_ctx + [o ^ mask for o in offsets_ctx]
+    core_part = spread(own_rows, masks[0])
+    core_part, seconds = lax.optimization_barrier((core_part, seconds))
+    core_part = spread(core_part, masks[1])
+    core_part, mix_own = lax.optimization_barrier((core_part, mix_own))
+    for mask in masks[2:]:
+        core_part = spread(core_part, mask)
+    other_part = along("head", n_head, 1)(core_part)
+
+    keep, send = projector(meta, core_part, other_part, in_full, seconds)
+    ordered = order_rows(meta, keep, along("head", n_head, 1)(send), offsets_ctx)
+    ordered, qkv_weight, stream = lax.optimization_barrier((ordered, qkv_weight, stream))
     local_places = row_places[0] - ctx * shard_rows
-    picks = spot[None, :] == jnp.arange(live_total, dtype=jnp.int32)[:, None]
+    picks = spot.reshape(1, -1) == jnp.arange(live_total, dtype=jnp.int32)[:, None]
     places = jnp.sum(jnp.where(picks, local_places[None, :], 0), axis=1)
     put = jnp.arange(shard_rows, dtype=jnp.int32)[:, None] == places[None, :]
     is_text = jnp.logical_not(jnp.any(put, axis=1))[:, None]
     weights = [qkv_weight[:, i, :] for i in range(3)]
     text_rows = norm(stream)
+
     text_q, text_k, text_v = [
         jnp.where(is_text, jax.nn.silu(dot(text_rows, w)), 0.0).astype(BF16) for w in weights
     ]
     cols = text_q.shape[1]
     heads_dev = cols // HEAD_DIM
 
+    received = lax.all_to_all(
+        ordered.reshape(n_ctx * n_head, part_rows, span // 2 * out_cols), both, 0, 0
+    )
+
+    if out_cols % 128 == 0:
+        img_part = image_norm(received, norm_gain[None], n_ctx, span)
+    else:
+        received = received.reshape(
+            n_ctx // span, span, n_head // 2, 2, part_rows, span // 2, out_cols
+        )
+        summed = jnp.sum(received.astype(F32), axis=(1, 2)).astype(BF16)
+        img_part = norm(summed.transpose(2, 0, 3, 1, 4).reshape(part_rows, width))
+    image_rows = lax.all_gather(img_part, "head", axis=0, tiled=True)
+
     def split(x):
         return x.reshape(x.shape[0], heads_dev, HEAD_DIM)
 
@@ -305,10 +425,9 @@
     intra = intra.reshape(shard_rows, cols)
     heads_out = finish(intra, queries, prefix, head_gain[None])
 
-    mix_own, in_full = lax.optimization_barrier((mix_own, in_full))
     mix_full = lax.all_gather(mix_own, "ctx", axis=0)
     group_width, mix_cols = mix_weight.shape
-    mix_full = mix_full.reshape(ratio, n_head, group_width, mix_cols)
+    mix_full = mix_full.reshape(n_head, ratio, group_width, mix_cols)
     parts, offsets = [heads_out], [0]
     bit = n_head // 2
     while bit:
@@ -326,7 +445,8 @@
         )
     total = 0.0
     for part, offset in zip(parts, offsets):
-        group = lax.dynamic_index_in_dim(mix_full, head ^ offset, 1, keepdims=False)
+        spot = head ^ turned(head ^ offset)
+        group = lax.dynamic_index_in_dim(mix_full, spot, 0, keepdims=False)
         group = jnp.concatenate([group[r] for r in range(ratio)], axis=1)
         total = total + dot(part, group)
     return total.astype(BF16)

time: 209 us -> 184 us (0.88)
  waiting for transfers between devices: 72.4 us -> 58.6 us
  local copies, waits for them, and re-layouts: 26 us -> 14.6 us
  starting transfers between devices: 35.5 us -> 44.9 us
  blocking collectives: 15.5 us -> 7.37 us
  Pallas kernels: 16.5 us -> 19.9 us
  other arithmetic: 7.19 us -> 4.14 us
    ppermute x6 -> x11, waiting for transfers between devices: 42.6 us -> 27.9 us  [the longest x3 13.8 us: spread(): return jnp.concatenate([x, along('ctx', n_ctx, mask)(x)])]
    ppermute x6 -> x11, starting transfers between devices: 5.41 us -> 16.8 us  [the longest x1 4.88 us: on_device(): mix_own = lax.ppermute(mix_own, both, perm)]
    all_gather x2 -> x1, blocking collectives: 15.5 us -> 7.37 us  [on_device(): image_rows = lax.all_gather(img_part, 'head', axis=0, tiled=True)]
    unnamed x47 -> x43, local copies, waits for them, and re-layouts: 10.3 us -> 4.88 us
    convert_element_type x2 -> x0, local copies, waits for them, and re-layouts: 2.63 us -> none  [norm(): widened = rows.astype(F32)]
    squeeze x1, local copies, waits for them, and re-layouts: 6.09 us -> 3.78 us  [on_device(): weights = [qkv_weight[:, i, :] for i in range(3)]]
    ppermute x1, starting transfers between devices: 3.57 us -> 1.29 us  [on_device(): other_part = along('head', n_head, 1)(core_part)]
    pallas_call x2 -> x5, Pallas kernels: 5.4 us -> 6.86 us  [the longest x1 4.76 us: projector(): pl.pallas_call(functools.partial(projector_kernel, min(rows, 256), span),...]
  transfers between devices with their start and end apart: 16 -> 21, of which waited for: 6 -> 11; matrix products, arithmetic and copies ran while one was open for 21% -> 19% of each run, Pallas kernels for 7% -> 7%
where the time goes in v3:
time: 184 us
  waiting for transfers between devices  58.6 us (32%)
  starting transfers between devices  44.9 us (24%)
  matrix products  20.3 us (11%)
  Pallas kernels  19.9 us (11%)
  local copies, waits for them, and re-layouts  14.6 us (8%)
  between operations  13.8 us (8%)
  blocking collectives  7.37 us (4%)
  other arithmetic  4.14 us (2%)
    dot_general x6, matrix products, dot(): return jnp.dot(a, b, preferred_element_type=F32)  18 us
    ppermute x3, waiting for transfers between devices, spread(): return jnp.concatenate([x, along('ctx', n_ctx, mask)(x)])  13.8 us
    ppermute x3, waiting for transfers between devices, on_device(): seconds.append(along('ctx', n_ctx, m)(block) if m else block)  11.1 us
    all_to_all x1, waiting for transfers between devices, on_device(): lax.all_to_all(ordered.reshape(n_ctx * n_head, part_rows, span // 2 * out...  10.5 us
    ppermute x3, waiting for transfers between devices, on_device(): parts = parts + [along('head', n_head, bit)(p) for p in parts]  8.48 us
    all_gather x1, blocking collectives, on_device(): image_rows = lax.all_gather(img_part, 'head', axis=0, tiled=True)  7.37 us
    pallas_call x1, Pallas kernels, image_qkv(): pl.pallas_call(image_kernel, grid=(heads,), out_shape=(out, out, out, jax...  6.76 us
    all_to_all x1, waiting for transfers between devices, on_device(): lax.all_to_all(state.reshape(n_ctx, -1, HEAD_DIM), 'ctx', 0, 0).astype(F32)  6.48 us
  transfers between devices with their start and end apart: 21, of which 11 were waited for; matrix products, arithmetic and copies ran while one was open for 19% of the time, Pallas kernels for 7%

profile of v3, /device:TPU:1, one launch (start us, length us, event | category | flops | bytes accessed | tf_op | source)
XLA Modules:
  0.0 183.6 jit_solution(8642995077098538027)
XLA Ops:
  14.2 4.2 %collective-permute-start.8 = (bf16[512,384]{1,0:T(8,128)(2,1)}, bf16[512,384]{1,0:T(8,128)(2,1)S(1)}, u32[]{:S(2)}, u32[]{:S(2)}) collective-permute-start(bf16[512,384]{1,0:T(8,128)(2,1)} %param.20), channel_id=1, source_target_pairs={{0,0},{1,17},{2,10},{3,27},{4,4},{5,21},{6,14},{7,31},{8,8},{9,25}... | collective-permute-start | bytes 1179656 | tf_op jit(solution)/shard_map/ppermute | solution.py:309
  20.5 3.5 %all-to-all-start = ((bf16[8,128,384]{2,1,0:T(8,128)(2,1)}), bf16[8,128,384]{2,1,0:T(8,128)(2,1)S(1)}, u32[]{:S(2)}, u32[]{:S(2)}) async-start(bf16[8,128,384]{2,1,0:T(8,128)(2,1)} %bitcast.8), calls=%async_computation | async-start | bytes 1572864 | tf_op jit(solution)/shard_map/all_to_all | solution.py:318
  28.7 4.9 %collective-permute-start.9 = (bf16[512,384]{1,0:T(8,128)(2,1)S(1)}, bf16[512,384]{1,0:T(8,128)(2,1)S(1)}, u32[]{:S(2)}, u32[]{:S(2)}) collective-permute-start(bf16[512,384]{1,0:T(8,128)(2,1)S(1)} %collective-permute-done.8), channel_id=1, source_target_pairs={{0,0},{1,2},{2,1},{3,3},{4,4},{5,6},{6,5},{7,7},{8,9},{9,11},{10,8... | collective-permute-start | bytes 1179656 | tf_op jit(solution)/shard_map/ppermute | solution.py:311
  34.4 11.1 %collective-permute-done.6.refs_3_ = bf16[384,384]{1,0:T(8,128)(2,1)} collective-permute-done((bf16[384,384]{1,0:T(8,128)(2,1)S(1)}, bf16[384,384]{1,0:T(8,128)(2,1)}, u32[]{:S(2)}, u32[]{:S(2)}) %collective-permute-start.6) | collective-permute-done | bytes 294944 | tf_op jit(solution)/shard_map/ppermute | solution.py:340
  45.5 3.4 %collective-permute-start.7 = (bf16[64,1024]{1,0:T(8,128)(2,1)S(1)}, bf16[64,1024]{1,0:T(8,128)(2,1)S(1)}, u32[]{:S(2)}, u32[]{:S(2)}) collective-permute-start(bf16[64,1024]{1,0:T(8,128)(2,1)S(1)} %pad_maximum_fusion.1), channel_id=1, source_target_pairs={{0,16},{4,20},{8,24},{12,28},{16,0},{20,4},{24,8},{28,12},{1,17},{... | collective-permute-start | bytes 393224 | tf_op jit(solution)/shard_map/ppermute | solution.py:351
  48.9 6.3 %collective-permute-done.7 = bf16[64,1024]{1,0:T(8,128)(2,1)S(1)} collective-permute-done((bf16[64,1024]{1,0:T(8,128)(2,1)S(1)}, bf16[64,1024]{1,0:T(8,128)(2,1)S(1)}, u32[]{:S(2)}, u32[]{:S(2)}) %collective-permute-start.7) | collective-permute-done | bytes 131104 | tf_op jit(solution)/shard_map/ppermute | solution.py:351
  55.9 6.9 %collective-permute-done.10 = bf16[128,1024]{1,0:T(8,128)(2,1)S(1)} collective-permute-done((bf16[128,1024]{1,0:T(8,128)(2,1)S(1)}, bf16[128,1024]{1,0:T(8,128)(2,1)S(1)}, u32[]{:S(2)}, u32[]{:S(2)}) %collective-permute-start.10) | collective-permute-done | bytes 262176 | tf_op jit(solution)/shard_map/ppermute | solution.py:351
  66.4 4.8 %projector.1 = (bf16[512,768]{1,0:T(8,128)(2,1)}, bf16[512,768]{1,0:T(8,128)(2,1)}) custom-call(s32[5]{0:T(128)} %stack.23.meta, bf16[256,1024]{1,0:T(8,128)(2,1)} %copy-done.11, bf16[256,1024]{1,0:T(8,128)(2,1)} %copy-done.14, bf16[1024,384]{1,0:T(8,128)(2,1)} %bitcast.67, bf16[384,384]{1,0:T(8,128)(2,1)} %get-tuple-element.23.refs_0_, ...), custom_call_target="tpu_custom_call" | custom-call | flops 1006632960 | bytes 5000000 | tf_op jit(solution)/shard_map/projector/pallas_call | solution.py:81
  76.4 4.6 %all-to-all-start.1 = ((bf16[32,16,768]{2,1,0:T(8,128)(2,1)}), bf16[32,16,768]{2,1,0:T(8,128)(2,1)S(1)}, u32[]{:S(2)}, u32[]{:S(2)}) async-start(bf16[32,16,768]{2,1,0:T(8,128)(2,1)} %bitcast.11), calls=%async_computation.1 | async-start | bytes 1572864 | tf_op jit(solution)/shard_map/all_to_all | solution.py:383
  81.0 2.7 %fusion = f32[512]{0:T(512)S(1)} fusion(bf16[512,3072]{1,0:T(8,128)(2,1)} %param.14), kind=kLoop, calls=%fused_computation.2 | loop fusion | flops 4718080 | bytes 3147776 | tf_op jit(solution)/shard_map/reduce_sum | solution.py:346
  83.8 3.9 %select_convert_fusion.2 = bf16[512,512]{1,0:T(8,128)(2,1)S(1)} fusion(pred[512]{0:T(512)(128)(4,1)S(1)} %not.7, bf16[3072,3,512]{2,0,1:T(8,128)(2,1)} %param.18, bf16[512,3072]{1,0:T(8,128)(2,1)S(1)} %copy-done.7, f32[3072]{0:T(1024)S(1)} %copy-done.4, f32[512]{0:T(512)S(1)} %add_rsqrt_fusion), kind=kOutput, calls=%fused_computation.20 | convolution fusion | flops 1618477056 | bytes 6830592 | tf_op jit(solution)/shard_map/dot_general | solution.py:26
  88.0 5.0 %select_convert_fusion.3 = bf16[512,512]{1,0:T(8,128)(2,1)S(1)} fusion(pred[512]{0:T(512)(128)(4,1)S(1)} %not.7, bf16[3072,3,512]{2,0,1:T(8,128)(2,1)} %param.18, bf16[512,3072]{1,0:T(8,128)(2,1)} %param.14, f32[3072]{0:T(1024)S(1)} %copy-done.4, f32[512]{0:T(512)S(1)} %add_rsqrt_fusion), kind=kOutput, calls=%fused_computation.21 | convolution fusion | flops 1618477056 | bytes 6830592 | tf_op jit(solution)/shard_map/dot_general | solution.py:26
  94.0 4.8 %fusion.22 = f32[512,512]{1,0:T(8,128)} fusion(bf16[3072,3,512]{2,0,1:T(8,128)(2,1)} %param.18, bf16[512,3072]{1,0:T(8,128)(2,1)S(1)} %copy-done.8, f32[3072]{0:T(1024)S(1)} %copy-done.4, f32[512]{0:T(512)S(1)} %add_rsqrt_fusion), kind=kOutput, calls=%fused_computation.55 | convolution fusion | flops 1616904192 | bytes 7354368 | tf_op jit(solution)/shard_map/dot_general | solution.py:26
  98.8 3.8 %slice_bitcast_fusion.2 = (bf16[3072,512]{1,0:T(8,128)(2,1)}, bf16[3072,512]{1,0:T(8,128)(2,1)}, bf16[3072,512]{1,0:T(8,128)(2,1)}) fusion(bf16[3072,3,512]{2,0,1:T(8,128)(2,1)S(1)} %bitcast.63), kind=kLoop, calls=%fused_computation.8 | loop fusion | bytes 18874368 | tf_op jit(solution)/shard_map/squeeze | solution.py:374
  102.6 10.5 %all-to-all-done.1.got = bf16[32,16,768]{2,1,0:T(8,128)(2,1)S(1)} async-done(((bf16[32,16,768]{2,1,0:T(8,128)(2,1)}), bf16[32,16,768]{2,1,0:T(8,128)(2,1)S(1)}, u32[]{:S(2)}, u32[]{:S(2)}) %all-to-all-start.1) | async-done | bytes 786464 | tf_op jit(solution)/shard_map/all_to_all | solution.py:383
  113.4 7.4 %all_gather.9.x = bf16[64,3072]{1,0:T(8,128)(2,1)} all-gather(bf16[16,3072]{1,0:T(8,128)(2,1)S(1)} %image_norm.1), channel_id=1, replica_groups=mesh['ctx'=8,'head'=4] {'head'}, dimensions={0}, use_global_device_ids=true | all-gather | bytes 491520 | tf_op jit(solution)/shard_map/all_gather | solution.py:395
  120.7 6.8 %image_qkv.1 = (bf16[64,512]{1,0:T(8,128)(2,1)}, bf16[64,512]{1,0:T(8,128)(2,1)}, bf16[64,512]{1,0:T(8,128)(2,1)}, bf16[4,128,128]{2,1,0:T(8,128)(2,1)}) custom-call(bf16[64,3072]{1,0:T(8,128)(2,1)} %all_gather.9.x, bf16[3072,512]{1,0:T(8,128)(2,1)} %get-tuple-element.39.wq, bf16[3072,512]{1,0:T(8,128)(2,1)} %get-tuple-element.38.wk, ...), custom_call_target="tpu_custom_call" | custom-call | flops 603979776 | bytes 9437184 | tf_op jit(solution)/shard_map/image_qkv/pallas_call | solution.py:197
  130.5 3.4 %all-to-all-start.2 = ((bf16[8,64,128]{2,1,0:T(8,128)(2,1)}), bf16[8,64,128]{2,1,0:T(8,128)(2,1)S(1)}, u32[]{:S(2)}, u32[]{:S(2)}) async-start(bf16[8,64,128]{2,1,0:T(8,128)(2,1)} %bitcast.20), calls=%async_computation.2 | async-start | bytes 262144 | tf_op jit(solution)/shard_map/all_to_all | solution.py:405
  135.6 6.5 %all-to-all-done.2 = bf16[8,64,128]{2,1,0:T(8,128)(2,1)S(1)} async-done(((bf16[8,64,128]{2,1,0:T(8,128)(2,1)}), bf16[8,64,128]{2,1,0:T(8,128)(2,1)S(1)}, u32[]{:S(2)}, u32[]{:S(2)}) %all-to-all-start.2) | async-done | bytes 131104 | tf_op jit(solution)/shard_map/all_to_all | solution.py:405
  142.8 5.1 %all-to-all-start.3 = ((bf16[8,64,128]{2,1,0:T(8,128)(2,1)}), bf16[8,64,128]{2,1,0:T(8,128)(2,1)S(1)}, u32[]{:S(2)}, u32[]{:S(2)}) async-start(bf16[8,64,128]{2,1,0:T(8,128)(2,1)} %fusion.7), calls=%async_computation.3 | async-start | bytes 262144 | tf_op jit(solution)/shard_map/all_to_all | solution.py:407
  149.5 4.5 %all-to-all-done.3 = bf16[8,64,128]{2,1,0:T(8,128)(2,1)S(1)} async-done(((bf16[8,64,128]{2,1,0:T(8,128)(2,1)}), bf16[8,64,128]{2,1,0:T(8,128)(2,1)S(1)}, u32[]{:S(2)}, u32[]{:S(2)}) %all-to-all-start.3) | async-done | bytes 131104 | tf_op jit(solution)/shard_map/all_to_all | solution.py:407
  158.9 8.5 %collective-permute-done.13.refs_0_ = bf16[512,512]{1,0:T(8,128)(2,1)S(1)} collective-permute-done((bf16[512,512]{1,0:T(8,128)(2,1)S(1)}, bf16[512,512]{1,0:T(8,128)(2,1)S(1)}, u32[]{:S(2)}, u32[]{:S(2)}) %collective-permute-start.13) | collective-permute-done | bytes 524320 | tf_op jit(solution)/shard_map/ppermute | solution.py:434
  167.4 2.7 %collective-permute-start.14 = (bf16[512,512]{1,0:T(8,128)(2,1)S(1)}, bf16[512,512]{1,0:T(8,128)(2,1)S(1)}, u32[]{:S(2)}, u32[]{:S(2)}) collective-permute-start(bf16[512,512]{1,0:T(8,128)(2,1)S(1)} %collective-permute-done.13.refs_0_), channel_id=1, source_target_pairs={{0,1},{1,0},{2,3},{3,2},{4,5},{5,4},{6,7},{7,6},{8,9},{9,8},{10,11... | collective-permute-start | bytes 1572872 | tf_op jit(solution)/shard_map/ppermute | solution.py:434
  174.0 2.8 %mix_part.3 = bf16[512,768]{1,0:T(8,128)(2,1)} custom-call(s32[5]{0:T(128)S(1)} %copy-done.5, bf16[512,512]{1,0:T(8,128)(2,1)S(1)} %collective-permute-done.13.refs_0_, bf16[512,512]{1,0:T(8,128)(2,1)S(1)} %collective-permute-done.14.refs_1_, bf16[4,2,512,384]{3,2,1,0:T(8,128)(2,1)S(1)} %bitcast.58, f32[512,768]{1,0:T(8,128)S(1)} %mix_part.2.refs_3_), custom_call_target="tpu_custom_call" | custom-call | flops 805306368 | bytes 5000000 | tf_op jit(solution)/shard_map/mix_part/pallas_call | solution.py:256
  (110 shorter events, 42.0 us)
Async XLA Ops:
  6.5 17.9 %collective-permute-start = (bf16[64,1024]{1,0:T(8,128)(2,1)}, bf16[64,1024]{1,0:T(8,128)(2,1)S(1)}, u32[]{:S(2)}, u32[]{:S(2)}) collective-permute-start(bf16[64,1024]{1,0:T(8,128)(2,1)} %refs_0_.1), channel_id=1, source_target_pairs={{0,2},{1,3},{2,0},{3,1},{4,6},{5,7},{6,4},{7,5},{8,10},{9,11},{10,... | collective-permute-start | bytes 393224 | tf_op jit(solution)/shard_map/ppermute | solution.py:325
  8.6 18.2 %collective-permute-start.1 = (bf16[64,1024]{1,0:T(8,128)(2,1)}, bf16[64,1024]{1,0:T(8,128)(2,1)S(1)}, u32[]{:S(2)}, u32[]{:S(2)}) collective-permute-start(bf16[64,1024]{1,0:T(8,128)(2,1)} %refs_0_.1), channel_id=1, source_target_pairs={{0,1},{1,0},{2,3},{3,2},{4,5},{5,4},{6,7},{7,6},{8,9},{9,8},{10,11... | collective-permute-start | bytes 393224 | tf_op jit(solution)/shard_map/ppermute | solution.py:325
  9.5 14.8 %copy-start.17 = (s32[4]{0:T(128)S(1)}, s32[4]{0:T(128)}, u32[]{:S(2)}) copy-start(s32[4]{0:T(128)} %constant.49.clone) | copy-start | bytes 52
  9.5 18.6 %copy-start.3 = (bf16[64,1024]{1,0:T(8,128)(2,1)S(1)}, bf16[64,1024]{1,0:T(8,128)(2,1)}, u32[]{:S(2)}) copy-start(bf16[64,1024]{1,0:T(8,128)(2,1)} %refs_0_.1) | copy-start | bytes 393220
  11.6 22.7 %collective-permute-start.4 = (bf16[384,384]{1,0:T(8,128)(2,1)S(1)}, bf16[384,384]{1,0:T(8,128)(2,1)S(1)}, u32[]{:S(2)}, u32[]{:S(2)}) collective-permute-start(bf16[384,384]{1,0:T(8,128)(2,1)S(1)} %get-tuple-element.41), channel_id=1, source_target_pairs={{0,4},{4,0},{8,12},{12,8},{16,20},{20,16},{24,28},{28,24},{1,5},{5... | collective-permute-start | bytes 884744 | tf_op jit(solution)/shard_map/ppermute | solution.py:340
  12.9 21.5 %collective-permute-start.5 = (bf16[384,384]{1,0:T(8,128)(2,1)S(1)}, bf16[384,384]{1,0:T(8,128)(2,1)}, u32[]{:S(2)}, u32[]{:S(2)}) collective-permute-start(bf16[384,384]{1,0:T(8,128)(2,1)S(1)} %get-tuple-element.43), channel_id=1, source_target_pairs={{0,8},{4,12},{8,0},{12,4},{16,24},{20,28},{24,16},{28,20},{1,9},{5... | collective-permute-start | bytes 884744 | tf_op jit(solution)/shard_map/ppermute | solution.py:340
  14.2 14.6 %collective-permute-start.8 = (bf16[512,384]{1,0:T(8,128)(2,1)}, bf16[512,384]{1,0:T(8,128)(2,1)S(1)}, u32[]{:S(2)}, u32[]{:S(2)}) collective-permute-start(bf16[512,384]{1,0:T(8,128)(2,1)} %param.20), channel_id=1, source_target_pairs={{0,0},{1,17},{2,10},{3,27},{4,4},{5,21},{6,14},{7,31},{8,8},{9,25}... | collective-permute-start | bytes 1179656 | tf_op jit(solution)/shard_map/ppermute | solution.py:309
  20.5 43.6 %all-to-all-start = ((bf16[8,128,384]{2,1,0:T(8,128)(2,1)}), bf16[8,128,384]{2,1,0:T(8,128)(2,1)S(1)}, u32[]{:S(2)}, u32[]{:S(2)}) async-start(bf16[8,128,384]{2,1,0:T(8,128)(2,1)} %bitcast.8), calls=%async_computation | async-start | bytes 1572864 | tf_op jit(solution)/shard_map/all_to_all | solution.py:318
  24.0 146.0 %all-gather.3.cloned.1.call-start = ((), (), s32[]{:S(2)}) async-start(), calls=%async_computation.4 | async-start | bytes 3538944 | tf_op jit(solution)/shard_map/all_gather | solution.py:428
  24.5 21.0 %collective-permute-start.6 = (bf16[384,384]{1,0:T(8,128)(2,1)S(1)}, bf16[384,384]{1,0:T(8,128)(2,1)}, u32[]{:S(2)}, u32[]{:S(2)}) collective-permute-start(bf16[384,384]{1,0:T(8,128)(2,1)S(1)} %get-tuple-element.40), channel_id=1, source_target_pairs={{0,12},{4,8},{8,4},{12,0},{16,28},{20,24},{24,20},{28,16},{1,13},{... | collective-permute-start | bytes 884744 | tf_op jit(solution)/shard_map/ppermute | solution.py:340
  26.8 1.3 collective-permute-start.2
  28.4 5.9 %collective-permute-start.3 = (bf16[32,1024]{1,0:T(8,128)(2,1)S(1)}, bf16[32,1024]{1,0:T(8,128)(2,1)S(1)}, u32[]{:S(2)}, u32[]{:S(2)}) collective-permute-start(bf16[32,1024]{1,0:T(8,128)(2,1)S(1)} %pick_rows.1), channel_id=1, source_target_pairs={{0,4},{4,0},{8,12},{12,8},{16,20},{20,16},{24,28},{28,24},{1,5},{5... | collective-permute-start | bytes 196616 | tf_op jit(solution)/shard_map/ppermute | solution.py:351
  28.7 26.4 %collective-permute-start.9 = (bf16[512,384]{1,0:T(8,128)(2,1)S(1)}, bf16[512,384]{1,0:T(8,128)(2,1)S(1)}, u32[]{:S(2)}, u32[]{:S(2)}) collective-permute-start(bf16[512,384]{1,0:T(8,128)(2,1)S(1)} %collective-permute-done.8), channel_id=1, source_target_pairs={{0,0},{1,2},{2,1},{3,3},{4,4},{5,6},{6,5},{7,7},{8,9},{9,11},{10,8... | collective-permute-start | bytes 1179656 | tf_op jit(solution)/shard_map/ppermute | solution.py:311
  34.3 30.6 %copy-start.15 = (bf16[384,384]{1,0:T(8,128)(2,1)}, bf16[384,384]{1,0:T(8,128)(2,1)S(1)}, u32[]{:S(2)}) copy-start(bf16[384,384]{1,0:T(8,128)(2,1)S(1)} %collective-permute-done.4.refs_1_) | copy-start | bytes 884740
  45.5 9.6 %collective-permute-start.7 = (bf16[64,1024]{1,0:T(8,128)(2,1)S(1)}, bf16[64,1024]{1,0:T(8,128)(2,1)S(1)}, u32[]{:S(2)}, u32[]{:S(2)}) collective-permute-start(bf16[64,1024]{1,0:T(8,128)(2,1)S(1)} %pad_maximum_fusion.1), channel_id=1, source_target_pairs={{0,16},{4,20},{8,24},{12,28},{16,0},{20,4},{24,8},{28,12},{1,17},{... | collective-permute-start | bytes 393224 | tf_op jit(solution)/shard_map/ppermute | solution.py:351
  55.2 7.6 %collective-permute-start.10 = (bf16[128,1024]{1,0:T(8,128)(2,1)S(1)}, bf16[128,1024]{1,0:T(8,128)(2,1)S(1)}, u32[]{:S(2)}, u32[]{:S(2)}) collective-permute-start(bf16[128,1024]{1,0:T(8,128)(2,1)S(1)} %pad_maximum_fusion), channel_id=1, source_target_pairs={{0,8},{4,12},{8,0},{12,4},{16,24},{20,28},{24,16},{28,20},{1,9},{5... | collective-permute-start | bytes 786440 | tf_op jit(solution)/shard_map/ppermute | solution.py:351
  62.8 2.8 %collective-permute-start.11 = (bf16[256,1024]{1,0:T(8,128)(2,1)S(1)}, bf16[256,1024]{1,0:T(8,128)(2,1)S(1)}, u32[]{:S(2)}, u32[]{:S(2)}) collective-permute-start(bf16[256,1024]{1,0:T(8,128)(2,1)S(1)} %constant_dynamic-update-slice_fusion.own), channel_id=1, source_target_pairs={{0,1},{1,0},{2,3},{3,2},{4,5},{5,4},{6,7},{7,6},{8,9},{9,8},{10,11... | collective-permute-start | bytes 1572872 | tf_op jit(solution)/shard_map/ppermute | solution.py:364
  71.2 2.5 %collective-permute-start.12 = (bf16[512,768]{1,0:T(8,128)(2,1)}, bf16[512,768]{1,0:T(8,128)(2,1)S(1)}, u32[]{:S(2)}, u32[]{:S(2)}) collective-permute-start(bf16[512,768]{1,0:T(8,128)(2,1)} %get-tuple-element.28), channel_id=1, source_target_pairs={{0,1},{1,0},{2,3},{3,2},{4,5},{5,4},{6,7},{7,6},{8,9},{9,8},{10,11... | collective-permute-start | bytes 2359304 | tf_op jit(solution)/shard_map/ppermute | solution.py:367
  76.4 36.7 %all-to-all-start.1 = ((bf16[32,16,768]{2,1,0:T(8,128)(2,1)}), bf16[32,16,768]{2,1,0:T(8,128)(2,1)S(1)}, u32[]{:S(2)}, u32[]{:S(2)}) async-start(bf16[32,16,768]{2,1,0:T(8,128)(2,1)} %bitcast.11), calls=%async_computation.1 | async-start | bytes 1572864 | tf_op jit(solution)/shard_map/all_to_all | solution.py:383
  130.5 11.6 %all-to-all-start.2 = ((bf16[8,64,128]{2,1,0:T(8,128)(2,1)}), bf16[8,64,128]{2,1,0:T(8,128)(2,1)S(1)}, u32[]{:S(2)}, u32[]{:S(2)}) async-start(bf16[8,64,128]{2,1,0:T(8,128)(2,1)} %bitcast.20), calls=%async_computation.2 | async-start | bytes 262144 | tf_op jit(solution)/shard_map/all_to_all | solution.py:405
  142.8 11.3 %all-to-all-start.3 = ((bf16[8,64,128]{2,1,0:T(8,128)(2,1)}), bf16[8,64,128]{2,1,0:T(8,128)(2,1)S(1)}, u32[]{:S(2)}, u32[]{:S(2)}) async-start(bf16[8,64,128]{2,1,0:T(8,128)(2,1)} %fusion.7), calls=%async_computation.3 | async-start | bytes 262144 | tf_op jit(solution)/shard_map/all_to_all | solution.py:407
  155.6 11.7 %collective-permute-start.13 = (bf16[512,512]{1,0:T(8,128)(2,1)S(1)}, bf16[512,512]{1,0:T(8,128)(2,1)S(1)}, u32[]{:S(2)}, u32[]{:S(2)}) collective-permute-start(bf16[512,512]{1,0:T(8,128)(2,1)S(1)} %finish.1.refs_0_), channel_id=1, source_target_pairs={{0,2},{1,3},{2,0},{3,1},{4,6},{5,7},{6,4},{7,5},{8,10},{9,11},{10,... | collective-permute-start | bytes 1572872 | tf_op jit(solution)/shard_map/ppermute | solution.py:434
  156.9 13.2 %collective-permute-start.15 = (bf16[512,512]{1,0:T(8,128)(2,1)S(1)}, bf16[512,512]{1,0:T(8,128)(2,1)S(1)}, u32[]{:S(2)}, u32[]{:S(2)}) collective-permute-start(bf16[512,512]{1,0:T(8,128)(2,1)S(1)} %finish.1.refs_0_), channel_id=1, source_target_pairs={{0,1},{1,0},{2,3},{3,2},{4,5},{5,4},{6,7},{7,6},{8,9},{9,8},{10,11... | collective-permute-start | bytes 1572872 | tf_op jit(solution)/shard_map/ppermute | solution.py:434
  167.4 6.6 %collective-permute-start.14 = (bf16[512,512]{1,0:T(8,128)(2,1)S(1)}, bf16[512,512]{1,0:T(8,128)(2,1)S(1)}, u32[]{:S(2)}, u32[]{:S(2)}) collective-permute-start(bf16[512,512]{1,0:T(8,128)(2,1)S(1)} %collective-permute-done.13.refs_0_), channel_id=1, source_target_pairs={{0,1},{1,0},{2,3},{3,2},{4,5},{5,4},{6,7},{7,6},{8,9},{9,8},{10,11... | collective-permute-start | bytes 1572872 | tf_op jit(solution)/shard_map/ppermute | solution.py:434
  (18 other events, 105.5 us)
Sparse Core Ops, SparseCore 0:
  72.1 77.0 all-gather.2

commit v4 on v3

v4 whole, which is shorter than its diff:
```python
import functools

import jax
import jax.numpy as jnp
from jax import lax
from jax.experimental import pallas as pl
from jax.experimental.pallas import tpu as pltpu
from jax.sharding import PartitionSpec as P

HEAD_DIM = 128
F32 = jnp.float32
BF16 = jnp.bfloat16
VMEM_LIMIT = 20 * 1024 * 1024
VMEM = pl.BlockSpec(memory_space=pltpu.VMEM)
SMEM = pl.BlockSpec(memory_space=pltpu.SMEM)
ANYWHERE = pl.BlockSpec(memory_space=pl.ANY)
PARAMS = pltpu.CompilerParams(vmem_limit_bytes=VMEM_LIMIT)


def cost(flops, nbytes, transcendentals=0):
    return pl.CostEstimate(
        flops=int(flops), bytes_accessed=int(nbytes), transcendentals=int(transcendentals)
    )


def dot(a, b):
    return jnp.dot(a, b, preferred_element_type=F32)


def silu(x):
    return x * (1.0 / (1.0 + jnp.exp(-x)))


def nothing(*refs):
    pass


def weighty(arrays, flops, nbytes):
    anywhere = pl.BlockSpec(memory_space=pl.ANY)
    return pl.pallas_call(
        nothing,
        out_shape=[jax.ShapeDtypeStruct(x.shape, x.dtype) for x in arrays],
        in_specs=[anywhere] * len(arrays),
        out_specs=[anywhere] * len(arrays),
        input_output_aliases={i: i for i in range(len(arrays))},
        cost_estimate=cost(flops, nbytes),
        name="weighty",
    )(*arrays)


def spread_kernel(span, x, out):
    part = out.shape[2]
    for c in range(out.shape[0]):
        at = c % span * part
        out[c] = x[:, at : at + part]


def spread_units(x, n_ctx, span):
    rows, units = x.shape
    return pl.pallas_call(
        functools.partial(spread_kernel, span),
        out_shape=jax.ShapeDtypeStruct((n_ctx, rows, units // span), x.dtype),
        in_specs=[VMEM],
        out_specs=VMEM,
        compiler_params=PARAMS,
        cost_estimate=cost(0, 4 * x.size),
        name="spread_units",
    )(x)


def text_kernel(rows, keep, wq, wk, wv, out, state):
    step = min(rows.shape[0], 256)
    for i in range(rows.shape[0] // step):
        at = slice(i * step, (i + 1) * step)
        for n, w in enumerate((wq, wk, wv)):
            out[n, at, :] = (silu(dot(rows[at, :], w[...])) * keep[at, :]).astype(BF16)
    for h in range(state.shape[0]):
        cols = slice(h * HEAD_DIM, (h + 1) * HEAD_DIM)
        state[h] = lax.dot_general(
            out[1, :, cols], out[2, :, cols], (((0,), (0,)), ((), ())), preferred_element_type=F32
        )


def text_qkv(rows, keep, weights):
    count, width = rows.shape
    cols = weights[0].shape[1]
    heads = cols // HEAD_DIM
    return pl.pallas_call(
        text_kernel,
        out_shape=(
            jax.ShapeDtypeStruct((3, count, cols), BF16),
            jax.ShapeDtypeStruct((heads, HEAD_DIM, HEAD_DIM), F32),
        ),
        in_specs=[VMEM] * 5,
        out_specs=(VMEM, VMEM),
        compiler_params=PARAMS,
        cost_estimate=cost(6 * count * width * cols, 6 * width * cols, 3 * count * cols),
        name="text_qkv",
    )(rows, keep, *weights)


def projector_kernel(chunk, span, meta, own, other, first, *refs):
    seconds, (keep, send, w_keep, w_send) = refs[:span], refs[span:]
    cols = seconds[0].shape[1]
    same = meta[0] == meta[1]
    for m in range(0, span, 2):
        mine, near = seconds[m][...], seconds[m + 1][...]
        slot = (meta[4] ^ m) >> 1
        w_keep[slot] = jnp.where(same, mine, near)
        w_send[slot] = jnp.where(same, near, mine)
    rows = own.shape[0]

    def run(source, base):
        @pl.loop(0, rows // chunk)
        def _(i):
            at = pl.ds(pl.multiple_of(i * chunk, chunk), chunk)
            to = pl.ds(pl.multiple_of(base + i * chunk, chunk), chunk)
            pre = dot(source[at, :], first[...])
            hid = (0.5 * pre * (1.0 + lax.erf(pre * 0.7071067811865476))).astype(BF16)
            for n in range(span // 2):
                keep[to, n * cols : (n + 1) * cols] = dot(hid, w_keep[n]).astype(BF16)
                send[to, n * cols : (n + 1) * cols] = dot(hid, w_send[n]).astype(BF16)

    run(own, 0)
    run(other, rows)


def projector(meta, own, other, first, seconds):
    rows, width = own.shape
    units, cols = seconds[0].shape
    span = len(seconds)
    out = jax.ShapeDtypeStruct((2 * rows, span // 2 * cols), BF16)
    scratch = pltpu.VMEM((span // 2, units, cols), BF16)
    return pl.pallas_call(
        functools.partial(projector_kernel, min(rows, 256), span),
        out_shape=(out, out),
        in_specs=[SMEM] + [VMEM] * (3 + span),
        out_specs=(VMEM, VMEM),
        scratch_shapes=[scratch, scratch],
        compiler_params=pltpu.CompilerParams(vmem_limit_bytes=VMEM_LIMIT),
        cost_estimate=cost(4 * rows * units * (width + span * cols), 5e6, 2 * rows * units),
        name="projector",
    )(meta, own, other, first, *seconds)


def pick_kernel(spot, *refs):
    sources, out = refs[:-1], refs[-1]
    rows = out.shape[0]
    wanted = lax.broadcasted_iota(jnp.int32, (rows, spot.shape[1]), 0)
    at, total = 0, 0.0
    for ref in sources:
        count = ref.shape[0]
        picks = (spot[:, at : at + count] == wanted[:, at : at + count]).astype(F32).astype(BF16)
        total = total + dot(picks, ref[...])
        at += count
    out[...] = total.astype(BF16)


def pick_rows(spot, sources, rows):
    width = sources[0].shape[1]
    return pl.pallas_call(
        pick_kernel,
        out_shape=jax.ShapeDtypeStruct((rows, width), BF16),
        in_specs=[VMEM] * (1 + len(sources)),
        out_specs=VMEM,
        compiler_params=PARAMS,
        cost_estimate=cost(2 * rows * width * spot.shape[1], 2 * width * spot.shape[1]),
        name="pick_rows",
    )(spot, *sources)


def order_kernel(offsets, meta, keep, got, out):
    core, ctx = meta[1], meta[2]
    rows, count = out.shape[2], len(offsets)
    for i in range(2):
        for b, offset in enumerate(offsets):
            at = pl.ds((i * count + b) * rows, rows)
            there = pl.ds(((1 - i) * count + b) * rows, rows)
            total = keep[at, :].astype(F32) + got[there, :].astype(F32)
            out[ctx ^ offset, core ^ i] = total.astype(BF16)


def order_rows(meta, keep, got, offsets):
    rows, cols = keep.shape
    count = len(offsets)
    out = jax.ShapeDtypeStruct((count, 2, rows // count // 2, cols), BF16)
    return pl.pallas_call(
        functools.partial(order_kernel, tuple(offsets)),
        out_shape=out,
        in_specs=[SMEM, VMEM, VMEM],
        out_specs=VMEM,
        compiler_params=PARAMS,
        cost_estimate=cost(rows * cols, 6 * rows * cols),
        name="order_rows",
    )(meta, keep, got)


def image_norm_kernel(groups, span, heads, got, gain, out, total):
    wide = span // 2
    cols = got.shape[2] // wide
    square = 0.0
    for g in range(groups):
        for core in range(2):
            part = 0.0
            for s in range(span):
                for h in range(heads // 2):
                    part = part + got[((g * span + s) * heads) + 2 * h + core].astype(F32)
            part = part.astype(BF16).astype(F32)
            square = square + jnp.sum(part * part, axis=-1, keepdims=True)
            for n in range(wide):
                c = g * span + 2 * n + core
                total[:, c * cols : (c + 1) * cols] = part[:, n * cols : (n + 1) * cols]
    scale = lax.rsqrt(square / total.shape[1] + 1e-05)
    out[...] = (total[...] * scale * gain[...]).astype(BF16)


def image_norm(got, gain, n_ctx, span):
    devices, rows, _ = got.shape
    width = gain.shape[1]
    return pl.pallas_call(
        functools.partial(image_norm_kernel, n_ctx // span, span, devices // n_ctx),
        out_shape=jax.ShapeDtypeStruct((rows, width), BF16),
        in_specs=[VMEM, VMEM],
        out_specs=VMEM,
        scratch_shapes=[pltpu.VMEM((rows, width), F32)],
        compiler_params=PARAMS,
        cost_estimate=cost(4 * got.size, 2 * got.size),
        name="image_norm",
    )(got, gain)


def image_kernel(x, wq, wk, wv, text_state, out, state):
    rows = x[...]
    key = silu(dot(rows, wk[...])).astype(BF16)
    value = silu(dot(rows, wv[...])).astype(BF16)
    out[1] = key
    out[2] = value
    for h in range(state.shape[0]):
        cols = slice(h * HEAD_DIM, (h + 1) * HEAD_DIM)
        outer = lax.dot_general(
            key[:, cols], value[:, cols], (((0,), (0,)), ((), ())), preferred_element_type=F32
        )
        state[h] = (text_state[h] + outer).astype(BF16)
    out[0] = silu(dot(rows, wq[...])).astype(BF16)


def image_qkv(x, weights, text_state):
    rows, width = x.shape
    cols = weights[0].shape[1]
    return pl.pallas_call(
        image_kernel,
        out_shape=(
            jax.ShapeDtypeStruct((3, rows, cols), BF16),
            jax.ShapeDtypeStruct(text_state.shape, BF16),
        ),
        in_specs=[VMEM] * 5,
        out_specs=(VMEM, VMEM),
        compiler_params=PARAMS,
        cost_estimate=cost(6 * rows * width * cols, 6 * width * cols, 3 * rows * cols),
        name="image_qkv",
    )(x, *weights, text_state)


def finish_kernel(intra, q, state, gain, out):
    for h in range(state.shape[0]):
        cols = slice(h * HEAD_DIM, (h + 1) * HEAD_DIM)
        total = intra[:, cols] + dot(q[:, cols], state[h])
        scale = lax.rsqrt(jnp.mean(total * total, axis=-1, keepdims=True) + 1e-06)
        out[:, cols] = (total * scale * gain[:, cols]).astype(BF16)


def finish(intra, q, state, gain):
    rows, cols = q.shape
    return pl.pallas_call(
        finish_kernel,
        out_shape=jax.ShapeDtypeStruct((rows, cols), BF16),
        in_specs=[VMEM] * 4,
        out_specs=VMEM,
        compiler_params=PARAMS,
        cost_estimate=cost(2 * rows * cols * HEAD_DIM, 8 * rows * cols),
        name="finish",
    )(intra, q, state, gain)


def intra_kernel(text, image, put, q, out):
    where = put[...]
    for h in range(q.shape[1] // HEAD_DIM):
        at = slice(h * HEAD_DIM, (h + 1) * HEAD_DIM)
        queries, keys, values = [
            (text[n, :, at].astype(F32) + dot(where, image[n, :, at])).astype(BF16)
            for n in range(3)
        ]
        q[:, at] = queries
        scores = lax.dot_general(
            queries, keys, (((1,), (1,)), ((), ())), preferred_element_type=F32
        )
        rows = lax.broadcasted_iota(jnp.int32, scores.shape, 0)
        cols = lax.broadcasted_iota(jnp.int32, scores.shape, 1)
        scores = jnp.where(cols <= rows, scores, 0.0).astype(BF16)
        out[:, at] = dot(scores, values)


def intra_shard(text, image, put):
    _, rows, cols = text.shape
    return pl.pallas_call(
        intra_kernel,
        out_shape=(
            jax.ShapeDtypeStruct((rows, cols), BF16),
            jax.ShapeDtypeStruct((rows, cols), F32),
        ),
        in_specs=[VMEM] * 3,
        out_specs=(VMEM, VMEM),
        compiler_params=PARAMS,
        cost_estimate=cost(2e10, 4e7),
        name="intra_shard",
    )(text, image, put)


def turned(h, count):
    return (h >> 1) | ((h & 1) * (count // 2))


def mix_load_kernel(mix_offsets, meta, *refs):
    blocks, held, sems = refs[: len(mix_offsets)], refs[-2], refs[-1]
    ctx, head, ratio, count = meta[2], meta[3], meta[5], meta[6]
    base = ((head ^ turned(head, count)) * ratio) ^ ctx
    copies = []
    for n, offset in enumerate(mix_offsets):
        slot = base ^ offset
        copies.append(pltpu.make_async_copy(blocks[n], held.at[slot], sems.at[n]))
    for copy in copies:
        copy.start()
    for copy in copies:
        copy.wait()


def mix_load(meta, mix, mix_offsets):
    return pl.pallas_call(
        functools.partial(mix_load_kernel, tuple(mix_offsets)),
        out_shape=jax.ShapeDtypeStruct((len(mix),) + mix[0].shape, BF16),
        in_specs=[SMEM] + [ANYWHERE] * len(mix),
        out_specs=VMEM,
        scratch_shapes=[pltpu.SemaphoreType.DMA((len(mix),))],
        compiler_params=PARAMS,
        cost_estimate=cost(0, 4 * len(mix) * mix[0].size),
        name="mix_load",
    )(meta, *mix)


def mix_kernel(offsets, ratio, count, has_before, *refs):
    ins, (mix, *before, out) = refs[: len(offsets)], refs[len(offsets) :]
    cols = mix.shape[2]
    for r in range(ratio):
        to = slice(r * cols, (r + 1) * cols)
        total = before[0][:, to] if has_before else 0.0
        for ref, offset in zip(ins, offsets):
            total = total + dot(ref[...], mix[turned(offset, count) * ratio + r])
        out[:, to] = total.astype(out.dtype)


def mix_part(arrays, offsets, mix, ratio, count, before, dtype):
    rows, width = arrays[0].shape
    cols = mix.shape[2]
    extra = [] if before is None else [before]
    return pl.pallas_call(
        functools.partial(mix_kernel, tuple(offsets), ratio, count, before is not None),
        out_shape=jax.ShapeDtypeStruct((rows, ratio * cols), dtype),
        in_specs=[VMEM] * (len(arrays) + 1 + len(extra)),
        out_specs=VMEM,
        compiler_params=PARAMS,
        cost_estimate=cost(2 * rows * width * ratio * cols * len(arrays), 5e6),
        name="mix_part",
    )(*arrays, mix, *extra)


def on_device(
    enc_rows,
    row_counts,
    row_places,
    stream,
    norm_gain,
    proj_in,
    proj_out,
    qkv_weight,
    head_gain,
    mix_weight,
):
    both = ("ctx", "head")
    capacity, enc_width = enc_rows.shape
    shard_rows, width = stream.shape
    n_ctx, n_head = lax.axis_size("ctx"), lax.axis_size("head")
    ctx, head = lax.axis_index("ctx"), lax.axis_index("head")
    live_total = n_head * (capacity // 4)
    core_rows = live_total // 2
    part_rows = live_total // n_head
    n_pairs = n_ctx // 2
    core, parity = head & 1, ctx & 1
    span = 4
    spot_in = ctx & (span - 1)
    ratio = n_ctx // n_head
    meta = jnp.stack([parity, core, ctx, head, spot_in, ratio, n_head]).astype(jnp.int32)
    flat = [(c, h) for c in range(n_ctx) for h in range(n_head)]

    def along(axis, count, mask):
        return functools.partial(
            lax.ppermute, axis_name=axis, perm=[(i, i ^ mask) for i in range(count)]
        )

    def index(c, h):
        return c * n_head + h

    perm = [(index(c, h), index(c ^ (turned(h, n_head) * ratio), h)) for c, h in flat]
    mix_own = lax.ppermute(mix_weight, both, perm)

    part = proj_in.shape[1] // span
    if part % 128 == 0:
        in_sends = spread_units(proj_in, n_ctx, span)
    else:
        in_sends = jnp.stack([proj_in[:, c % span * part :][:, :part] for c in range(n_ctx)])
    out_cols = proj_out.shape[1]

    sources, swaps = [enc_rows], [0]
    bit = n_head // 2
    while bit:
        sources = sources + [along("head", n_head, bit)(x) for x in sources]
        swaps = swaps + [o ^ bit for o in swaps]
        bit //= 2
    counts = row_counts[0]
    earlier = jnp.arange(n_head)[:, None] > jnp.arange(n_head)[None, :]
    starts = jnp.sum(jnp.where(earlier, counts[None, :], 0), axis=1)
    within = jnp.arange(capacity, dtype=jnp.int32)[None, :]
    spot = jnp.where(within < counts[:, None], starts[:, None] + within, -1)
    owners = jnp.arange(n_head)[None, :] == (head ^ jnp.array(swaps, dtype=jnp.int32))[:, None]
    swapped = jnp.sum(jnp.where(owners[:, :, None], spot[None], 0), axis=1)
    own_rows = pick_rows(swapped.reshape(1, -1) - core * core_rows, sources, core_rows)
    own_rows, in_sends = lax.optimization_barrier((own_rows, in_sends))
    (in_full,) = weighty([lax.all_to_all(in_sends, "ctx", 0, 0)], 1e11, 4e8)
    in_full = in_full.reshape(enc_width, part)

    def norm(rows):
        widened = rows.astype(F32)
        return (
            widened
            * lax.rsqrt(jnp.mean(widened * widened, axis=-1, keepdims=True) + 1e-05)
            * norm_gain
        ).astype(BF16)

    def spread(x, mask):
        return jnp.concatenate([x, along("ctx", n_ctx, mask)(x)])

    masks = [1 << n for n in reversed(range(n_ctx.bit_length() - 1))]
    masks = masks[-1:] + masks[:-1]
    offsets_ctx = [0]
    for mask in masks:
        offsets_ctx = offsets_ctx + [o ^ mask for o in offsets_ctx]
    core_part, proj_out, stream, mix_own = lax.optimization_barrier(
        (spread(own_rows, masks[0]), proj_out, stream, mix_own)
    )
    perm = [(index(c, h), index(c, (c // ratio) ^ turned(h, n_head))) for c, h in flat]
    mix_own = lax.ppermute(mix_own, both, perm)
    text_rows = norm(stream)

    seconds = []
    for m in range(span):
        block = lax.dynamic_slice(proj_out, ((spot_in ^ m) * part, 0), (part, out_cols))
        seconds.append(along("ctx", n_ctx, m)(block) if m else block)
    seconds = weighty(seconds, 4e10, 1.6e8)

    core_part = spread(core_part, masks[1])
    core_part, mix_own, text_rows, qkv_weight = lax.optimization_barrier(
        (core_part, mix_own, text_rows, qkv_weight)
    )
    weights = [qkv_weight[:, i, :] for i in range(3)]
    for mask in masks[2:]:
        core_part = spread(core_part, mask)
    core_part, mix_own, weights = lax.optimization_barrier((core_part, mix_own, weights))
    other_part = along("head", n_head, 1)(core_part)

    mix_blocks = {0: mix_own}
    top = n_ctx // 2
    single = [o for o in range(1, top) if o & (o - 1) == 0]
    double = [o for o in range(1, top) if o not in single]
    late = [o for o in range(top + 1, n_ctx) if o & 1 == 0 or o == top + 1]
    last = [o for o in range(top + 1, n_ctx) if o not in late]

    def mix_start(stage):
        for offset in stage:
            mask = offset & -offset
            mix_blocks[offset] = along("ctx", n_ctx, mask)(mix_blocks[offset ^ mask])

    def mix_end(stage, beside):
        arrays, beside = lax.optimization_barrier(([mix_blocks[o] for o in stage], beside))
        mix_blocks.update(zip(stage, arrays))
        return beside

    mix_start(single)

    keep, send = projector(meta, core_part, other_part, in_full, seconds)
    ordered = order_rows(meta, keep, along("head", n_head, 1)(send), offsets_ctx)
    ordered, text_rows, weights = lax.optimization_barrier((ordered, text_rows, weights))
    local_places = row_places[0] - ctx * shard_rows
    picks = spot.reshape(1, -1) == jnp.arange(live_total, dtype=jnp.int32)[:, None]
    places = jnp.sum(jnp.where(picks, local_places[None, :], 0), axis=1)
    put = jnp.arange(shard_rows, dtype=jnp.int32)[:, None] == places[None, :]
    is_text = jnp.logical_not(jnp.any(put, axis=1))[:, None]

    text, text_state = mix_end(
        single, text_qkv(text_rows, is_text.astype(F32), weights)
    )
    mix_start(double)

    received = lax.all_to_all(
        ordered.reshape(n_ctx * n_head, part_rows, span // 2 * out_cols), both, 0, 0
    )
    (received,) = weighty([received], 2e11, 8e8)
    received, text = mix_end([0], (received, text))
    mix_start([top])

    if out_cols % 128 == 0:
        img_part = image_norm(received, norm_gain[None], n_ctx, span)
    else:
        received = received.reshape(
            n_ctx // span, span, n_head // 2, 2, part_rows, span // 2, out_cols
        )
        summed = jnp.sum(received.astype(F32), axis=(1, 2)).astype(BF16)
        img_part = norm(summed.transpose(2, 0, 3, 1, 4).reshape(part_rows, width))
    image_rows = lax.all_gather(img_part, "head", axis=0, tiled=True)

    image, state = image_qkv(image_rows, weights, text_state)
    state = mix_end([top] + double, state)
    mix_start(late)

    pieces = lax.all_to_all(state.reshape(n_ctx, -1, HEAD_DIM), "ctx", 0, 0).astype(F32)
    before = (jnp.cumsum(pieces, axis=0) - pieces).astype(BF16)
    before, put = lax.optimization_barrier((before, put.astype(BF16)))
    prefix = lax.all_to_all(before, "ctx", 0, 0).reshape(state.shape)

    queries, intra = mix_end(late, intra_shard(text, image, put))
    mix_start(last)
    heads_out = finish(intra, queries, prefix, head_gain[None])

    mix_cols = mix_weight.shape[1]
    near, near_offsets = [heads_out], [0]
    near.append(along("head", n_head, 1)(heads_out))
    near_offsets.append(1)
    far, far_offsets = [], []
    bit = n_head // 2
    sent, sent_offsets = [heads_out], [0]
    while bit > 1:
        sent = sent + [along("head", n_head, bit)(p) for p in sent]
        sent_offsets = sent_offsets + [o ^ bit for o in sent_offsets]
        bit //= 2
    near = mix_end(last, near)
    mix_offsets, mix_blocks = list(mix_blocks), list(mix_blocks.values())
    first = None
    if mix_cols % 128 == 0:
        mix_full = mix_load(meta, mix_blocks, mix_offsets)
        first = mix_part(near, near_offsets, mix_full, ratio, n_head, None, F32)
        sent, first = lax.optimization_barrier((sent, first))
    far = sent[1:] + [along("head", n_head, 1)(p) for p in sent[1:]]
    far_offsets = sent_offsets[1:] + [o ^ 1 for o in sent_offsets[1:]]
    if mix_cols % 128 == 0:
        return mix_part(far, far_offsets, mix_full, ratio, n_head, first, BF16)
    parts, offsets = near + far, near_offsets + far_offsets
    mix_full = jnp.stack([mix_blocks[mix_offsets.index(o)] for o in range(n_ctx)])
    total = 0.0
    for part, offset in zip(parts, offsets):
        spot = head ^ turned(head ^ offset, n_head)
        group = [
            lax.dynamic_index_in_dim(mix_full, (spot * ratio + r) ^ ctx, 0, keepdims=False)
            for r in range(ratio)
        ]
        total = total + dot(part, jnp.concatenate(group, axis=1))
    return total.astype(BF16)


def solution(mesh):
    in_specs = (
        P(("ctx", "head"), None),
        P("ctx", None),
        P("ctx", None),
        P("ctx", None),
        P(),
        P("ctx", "head"),
        P("head", "ctx"),
        P(None, None, "head"),
        P("head"),
        P("head", "ctx"),
    )
    out_specs = P("ctx", "head")
    return jax.shard_map(
        on_device, mesh=mesh, in_specs=in_specs, out_specs=out_specs, check_vma=False
    )
```

time: 184 us -> 172 us (0.935)
  local copies, waits for them, and re-layouts: 14.6 us -> 35.7 us
  matrix products: 20.3 us -> 0 us
  waiting for transfers between devices: 58.6 us -> 43.2 us
  between operations: 13.8 us -> 0.36 us
  other arithmetic: 4.14 us -> 11.9 us
  starting transfers between devices: 44.9 us -> 48.7 us
  Pallas kernels: 19.9 us -> 22.6 us
    unnamed x43 -> x80, local copies, waits for them, and re-layouts: 4.88 us -> 27.8 us
    dot_general x8 -> x0, matrix products: 20.3 us -> none  [the longest x6 18 us: dot(): return jnp.dot(a, b, preferred_element_type=F32)]
    all_to_all x1, waiting for transfers between devices: 10.5 us -> 0.01 us  [on_device(): lax.all_to_all(ordered.reshape(n_ctx * n_head, part_rows, span // 2 * out...]
    ppermute x3 -> x10, starting transfers between devices: 5.93 us -> 15.1 us  [the longest x7 8.65 us: mix_start(): mix_blocks[offset] = along('ctx', n_ctx, mask)(mix_blocks[offset ^ mask])]
    ppermute x3 -> x10, waiting for transfers between devices: 8.48 us -> 17 us  [the longest x7 15.5 us: mix_start(): mix_blocks[offset] = along('ctx', n_ctx, mask)(mix_blocks[offset ^ mask])]
    ppermute x3, waiting for transfers between devices: 11.1 us -> 6.46 us  [on_device(): seconds.append(along('ctx', n_ctx, m)(block) if m else block)]
    pallas_call x5 -> x11, Pallas kernels: 13.1 us -> 16.9 us  [the longest x1 5.64 us: text_qkv(): pl.pallas_call(text_kernel, out_shape=(jax.ShapeDtypeStruct((3, count, co...]
    convert_element_type x0 -> x3, other arithmetic: none -> 3.59 us  [the longest x1 2.87 us: norm(): return (widened * lax.rsqrt(jnp.mean(widened * widened, axis=-1, keepdims...]
  transfers between devices with their start and end apart: 21 -> 27, of which waited for: 11 -> 12; matrix products, arithmetic and copies ran while one was open for 19% -> 12% of each run, Pallas kernels for 7% -> 9%
where the time goes in v4:
time: 172 us; the launch traced here: 171 us
  starting transfers between devices  48.7 us (28%)
  waiting for transfers between devices  43.2 us (25%)
  local copies, waits for them, and re-layouts  35.7 us (21%)
  Pallas kernels  22.6 us (13%)
  other arithmetic  11.9 us (7%)
  blocking collectives  7.9 us (5%)
    unnamed x80, local copies, waits for them, and re-layouts  27.8 us
    ppermute x7, waiting for transfers between devices, mix_start(): mix_blocks[offset] = along('ctx', n_ctx, mask)(mix_blocks[offset ^ mask])  15.5 us
    ppermute x3, waiting for transfers between devices, spread(): return jnp.concatenate([x, along('ctx', n_ctx, mask)(x)])  11.1 us
    ppermute x7, starting transfers between devices, mix_start(): mix_blocks[offset] = along('ctx', n_ctx, mask)(mix_blocks[offset ^ mask])  8.65 us
    all_gather x1, blocking collectives, on_device(): image_rows = lax.all_gather(img_part, 'head', axis=0, tiled=True)  7.9 us
    ppermute x3, waiting for transfers between devices, on_device(): seconds.append(along('ctx', n_ctx, m)(block) if m else block)  6.46 us
    squeeze x1, local copies, waits for them, and re-layouts, on_device(): weights = [qkv_weight[:, i, :] for i in range(3)]  6.01 us
    pallas_call x1, Pallas kernels, text_qkv(): pl.pallas_call(text_kernel, out_shape=(jax.ShapeDtypeStruct((3, count, co...  5.64 us
  transfers between devices with their start and end apart: 27, of which 12 were waited for; matrix products, arithmetic and copies ran while one was open for 12% of the time, Pallas kernels for 9%

profile of v4, /device:TPU:1, one launch (start us, length us, event | category | flops | bytes accessed | tf_op | source)
XLA Modules:
  0.0 170.5 jit_solution(13321021844274457622)
XLA Ops:
  3.0 4.2 %collective-permute-start.4 = (bf16[512,384]{1,0:T(8,128)(2,1)}, bf16[512,384]{1,0:T(8,128)(2,1)S(1)}, u32[]{:S(2)}, u32[]{:S(2)}) collective-permute-start(bf16[512,384]{1,0:T(8,128)(2,1)} %param.20), channel_id=1, source_target_pairs={{0,0},{1,17},{2,10},{3,27},{4,4},{5,21},{6,14},{7,31},{8,8},{9,25}... | collective-permute-start | bytes 1179656 | tf_op jit(solution)/shard_map/ppermute | solution.py:413
  14.3 4.2 %all-to-all-start = ((bf16[8,128,384]{2,1,0:T(8,128)(2,1)}), bf16[8,128,384]{2,1,0:T(8,128)(2,1)}, u32[]{:S(2)}, u32[]{:S(2)}) async-start(bf16[8,128,384]{2,1,0:T(8,128)(2,1)} %spread_units.1), calls=%async_computation | async-start | bytes 1572864 | tf_op jit(solution)/shard_map/all_to_all | solution.py:437
  18.5 2.7 %fusion = f32[512]{0:T(512)S(1)} fusion(bf16[512,3072]{1,0:T(8,128)(2,1)} %param.14), kind=kLoop, calls=%fused_computation.2 | loop fusion | flops 4718080 | bytes 3147776 | tf_op jit(solution)/shard_map/reduce_sum | solution.py:444
  21.3 2.3 %collective-permute-start.5 = (bf16[64,1024]{1,0:T(8,128)(2,1)S(1)}, bf16[64,1024]{1,0:T(8,128)(2,1)S(1)}, u32[]{:S(2)}, u32[]{:S(2)}) collective-permute-start(bf16[64,1024]{1,0:T(8,128)(2,1)S(1)} %pad_maximum_fusion.2), channel_id=1, source_target_pairs={{0,16},{4,20},{8,24},{12,28},{16,0},{20,4},{24,8},{28,12},{1,17},{... | collective-permute-start | bytes 393224 | tf_op jit(solution)/shard_map/ppermute | solution.py:449
  23.6 4.4 %collective-permute-start.6 = (bf16[512,384]{1,0:T(8,128)(2,1)S(1)}, bf16[512,384]{1,0:T(8,128)(2,1)S(1)}, u32[]{:S(2)}, u32[]{:S(2)}) collective-permute-start(bf16[512,384]{1,0:T(8,128)(2,1)S(1)} %collective-permute-done.4), channel_id=1, source_target_pairs={{0,0},{1,2},{2,1},{3,3},{4,4},{5,6},{6,5},{7,7},{8,9},{9,11},{10,8... | collective-permute-start | bytes 1179656 | tf_op jit(solution)/shard_map/ppermute | solution.py:460
  28.8 2.4 %collective-permute-start.11 = (bf16[384,384]{1,0:T(8,128)(2,1)S(1)}, bf16[384,384]{1,0:T(8,128)(2,1)S(1)}, u32[]{:S(2)}, u32[]{:S(2)}) collective-permute-start(bf16[384,384]{1,0:T(8,128)(2,1)S(1)} %get-tuple-element.114), channel_id=1, source_target_pairs={{0,12},{4,8},{8,4},{12,0},{16,28},{20,24},{24,20},{28,16},{1,13},{... | collective-permute-start | bytes 884744 | tf_op jit(solution)/shard_map/ppermute | solution.py:466
  31.5 2.9 %fusion.2.rows = bf16[512,3072]{1,0:T(8,128)(2,1)} fusion(bf16[512,3072]{1,0:T(8,128)(2,1)S(1)} %copy-done.35, f32[3072]{0:T(1024)S(1)} %copy-done.20, f32[512]{0:T(512)S(1)} %add_rsqrt_fusion), kind=kLoop, calls=%fused_computation.4 | loop fusion | flops 6291456 | bytes 6305792 | tf_op jit(solution)/shard_map/convert_element_type | solution.py:446
  34.4 9.2 %collective-permute-done.5 = bf16[64,1024]{1,0:T(8,128)(2,1)S(1)} collective-permute-done((bf16[64,1024]{1,0:T(8,128)(2,1)S(1)}, bf16[64,1024]{1,0:T(8,128)(2,1)S(1)}, u32[]{:S(2)}, u32[]{:S(2)}) %collective-permute-start.5) | collective-permute-done | bytes 131104 | tf_op jit(solution)/shard_map/ppermute | solution.py:449
  44.3 6.5 %collective-permute-done.11.refs_3_ = bf16[384,384]{1,0:T(8,128)(2,1)S(1)} collective-permute-done((bf16[384,384]{1,0:T(8,128)(2,1)S(1)}, bf16[384,384]{1,0:T(8,128)(2,1)S(1)}, u32[]{:S(2)}, u32[]{:S(2)}) %collective-permute-start.11) | collective-permute-done | bytes 294944 | tf_op jit(solution)/shard_map/ppermute | solution.py:466
  51.6 6.0 %slice_bitcast_fusion = (bf16[3072,512]{1,0:T(8,128)(2,1)S(1)}, bf16[3072,512]{1,0:T(8,128)(2,1)}, bf16[3072,512]{1,0:T(8,128)(2,1)}) fusion(bf16[3072,3,512]{2,0,1:T(8,128)(2,1)} %param.18), kind=kLoop, calls=%fused_computation.5 | loop fusion | bytes 18874368 | tf_op jit(solution)/shard_map/squeeze | solution.py:473
  68.1 3.4 %projector.1 = (bf16[512,768]{1,0:T(8,128)(2,1)S(1)}, bf16[512,768]{1,0:T(8,128)(2,1)S(1)}) custom-call(s32[7]{0:T(128)S(1)} %stack.23.meta, bf16[256,1024]{1,0:T(8,128)(2,1)} %pad_maximum_fusion.own, bf16[256,1024]{1,0:T(8,128)(2,1)} %collective-permute-done.8.other, bf16[1024,384]{1,0:T(8,128)(2,1)} %bitcast.9.first, bf16[384,384]{1,0:T(8,128)(2,1)S(1)} %copy-done.13, ...), custom_call_target="tpu_custom_call" | custom-call | flops 1006632960 | bytes 5000000 | tf_op jit(solution)/shard_map/projector/pallas_call | solution.py:134
  75.4 3.2 %all-to-all-start.1 = ((bf16[32,16,768]{2,1,0:T(8,128)(2,1)}), bf16[32,16,768]{2,1,0:T(8,128)(2,1)}, u32[]{:S(2)}, u32[]{:S(2)}) async-start(bf16[32,16,768]{2,1,0:T(8,128)(2,1)} %bitcast.20), calls=%async_computation.1 | async-start | bytes 1572864 | tf_op jit(solution)/shard_map/all_to_all | solution.py:512
  89.8 5.6 %text_qkv.1 = (bf16[3,512,512]{2,1,0:T(8,128)(2,1)S(1)}, f32[4,128,128]{2,1,0:T(8,128)S(1)}) custom-call(bf16[512,3072]{1,0:T(8,128)(2,1)S(1)} %copy-done.5, f32[512,1]{1,0:T(8,128)S(1)} %copy-done.16, bf16[3072,512]{1,0:T(8,128)(2,1)S(1)} %copy-done.2, bf16[3072,512]{1,0:T(8,128)(2,1)S(1)} %copy-done, bf16[3072,512]{1,0:T(8,128)(2,1)S(1)} %get-tuple-element.83.wv), custom_call_target="tpu_custom_call" | custom-call | flops 4831838208 | bytes 9437184 | tf_op jit(solution)/shard_map/text_qkv/pallas_call | solution.py:88
  98.4 3.7 %collective-permute-done.14.refs_2_ = bf16[512,384]{1,0:T(8,128)(2,1)} collective-permute-done((bf16[512,384]{1,0:T(8,128)(2,1)S(1)}, bf16[512,384]{1,0:T(8,128)(2,1)}, u32[]{:S(2)}, u32[]{:S(2)}) %collective-permute-start.14) | collective-permute-done | bytes 393248 | tf_op jit(solution)/shard_map/ppermute | solution.py:489
  104.3 2.2 %collective-permute-start.15 = (bf16[512,384]{1,0:T(8,128)(2,1)S(1)}, bf16[512,384]{1,0:T(8,128)(2,1)S(1)}, u32[]{:S(2)}, u32[]{:S(2)}) collective-permute-start(bf16[512,384]{1,0:T(8,128)(2,1)S(1)} %copy-done.7), channel_id=1, source_target_pairs={{0,16},{4,20},{8,24},{12,28},{16,0},{20,4},{24,8},{28,12},{1,17},{... | collective-permute-start | bytes 1179656 | tf_op jit(solution)/shard_map/ppermute | solution.py:489
  107.9 7.9 %all_gather.3.x = bf16[64,3072]{1,0:T(8,128)(2,1)S(1)} all-gather(bf16[16,3072]{1,0:T(8,128)(2,1)S(1)} %image_norm.1), channel_id=1, replica_groups=mesh['ctx'=8,'head'=4] {'head'}, dimensions={0}, use_global_device_ids=true | all-gather | bytes 491520 | tf_op jit(solution)/shard_map/all_gather | solution.py:527
  125.4 3.4 %all-to-all-start.2 = ((bf16[8,64,128]{2,1,0:T(8,128)(2,1)}), bf16[8,64,128]{2,1,0:T(8,128)(2,1)S(1)}, u32[]{:S(2)}, u32[]{:S(2)}) async-start(bf16[8,64,128]{2,1,0:T(8,128)(2,1)} %bitcast.22), calls=%async_computation.2 | async-start | bytes 262144 | tf_op jit(solution)/shard_map/all_to_all | solution.py:533
  131.4 3.7 %all-to-all-done.2 = bf16[8,64,128]{2,1,0:T(8,128)(2,1)S(1)} async-done(((bf16[8,64,128]{2,1,0:T(8,128)(2,1)}), bf16[8,64,128]{2,1,0:T(8,128)(2,1)S(1)}, u32[]{:S(2)}, u32[]{:S(2)}) %all-to-all-start.2) | async-done | bytes 131104 | tf_op jit(solution)/shard_map/all_to_all | solution.py:533
  135.7 3.4 %all-to-all-start.3 = ((bf16[8,64,128]{2,1,0:T(8,128)(2,1)}), bf16[8,64,128]{2,1,0:T(8,128)(2,1)S(1)}, u32[]{:S(2)}, u32[]{:S(2)}) async-start(bf16[8,64,128]{2,1,0:T(8,128)(2,1)} %fusion.3), calls=%async_computation.3 | async-start | bytes 262144 | tf_op jit(solution)/shard_map/all_to_all | solution.py:536
  142.4 2.1 %intra_shard.1 = (bf16[512,512]{1,0:T(8,128)(2,1)S(1)}, f32[512,512]{1,0:T(8,128)S(1)}) custom-call(bf16[3,512,512]{2,1,0:T(8,128)(2,1)S(1)} %copy-done.34, bf16[3,64,512]{2,1,0:T(8,128)(2,1)S(1)} %copy-done.32, bf16[512,64]{1,0:T(8,128)(2,1)S(1)} %copy-done.17), custom_call_target="tpu_custom_call" | custom-call | flops 20000000000 | bytes 40000000 | tf_op jit(solution)/shard_map/intra_shard/pallas_call | solution.py:305
  146.1 4.0 %collective-permute-start.21 = (bf16[512,512]{1,0:T(8,128)(2,1)S(1)}, bf16[512,512]{1,0:T(8,128)(2,1)S(1)}, u32[]{:S(2)}, u32[]{:S(2)}) collective-permute-start(bf16[512,512]{1,0:T(8,128)(2,1)S(1)} %finish.1.refs_0_), channel_id=1, source_target_pairs={{0,1},{1,0},{2,3},{3,2},{4,5},{5,4},{6,7},{7,6},{8,9},{9,8},{10,11... | collective-permute-start | bytes 1572872 | tf_op jit(solution)/shard_map/ppermute | solution.py:544
  151.3 10.6 %collective-permute-done.20.refs_7_ = bf16[512,384]{1,0:T(8,128)(2,1)S(1)} collective-permute-done((bf16[512,384]{1,0:T(8,128)(2,1)}, bf16[512,384]{1,0:T(8,128)(2,1)S(1)}, u32[]{:S(2)}, u32[]{:S(2)}) %collective-permute-start.20) | collective-permute-done | bytes 393248 | tf_op jit(solution)/shard_map/ppermute | solution.py:489
  161.9 2.4 %mix_load.1.refs_2_ = bf16[8,512,384]{2,1,0:T(8,128)(2,1)S(1)} custom-call(s32[7]{0:T(128)S(1)} %copy-done.23, bf16[512,384]{1,0:T(8,128)(2,1)S(1)} %copy-done.7, bf16[512,384]{1,0:T(8,128)(2,1)S(1)} %copy-done.9, bf16[512,384]{1,0:T(8,128)(2,1)} %collective-permute-done.14.refs_2_, bf16[512,384]{1,0:T(8,128)(2,1)} %collective-permute-done.16.refs_3_, ...), custom_call_target="tpu_custom_call" | custom-call | bytes 6291456 | tf_op jit(solution)/shard_map/mix_load/pallas_call | solution.py:338
  168.4 2.1 %mix_part.3 = bf16[512,768]{1,0:T(8,128)(2,1)} custom-call(bf16[512,512]{1,0:T(8,128)(2,1)S(1)} %collective-permute-done.19.refs_0_, bf16[512,512]{1,0:T(8,128)(2,1)S(1)} %collective-permute-done.22.refs_1_, bf16[8,512,384]{2,1,0:T(8,128)(2,1)S(1)} %mix_load.1.refs_2_, f32[512,768]{1,0:T(8,128)S(1)} %mix_part.2.refs_3_), custom_call_target="tpu_custom_call" | custom-call | flops 805306368 | bytes 5000000 | tf_op jit(solution)/shard_map/mix_part/pallas_call | solution.py:365
  (149 shorter events, 67.7 us)
Async XLA Ops:
  0.0 9.6 %collective-permute-start = (bf16[64,1024]{1,0:T(8,128)(2,1)}, bf16[64,1024]{1,0:T(8,128)(2,1)S(1)}, u32[]{:S(2)}, u32[]{:S(2)}) collective-permute-start(bf16[64,1024]{1,0:T(8,128)(2,1)} %refs_0_.1), channel_id=1, source_target_pairs={{0,2},{1,3},{2,0},{3,1},{4,6},{5,7},{6,4},{7,5},{8,10},{9,11},{10,... | collective-permute-start | bytes 393224 | tf_op jit(solution)/shard_map/ppermute | solution.py:425
  2.0 9.6 %collective-permute-start.1 = (bf16[64,1024]{1,0:T(8,128)(2,1)}, bf16[64,1024]{1,0:T(8,128)(2,1)S(1)}, u32[]{:S(2)}, u32[]{:S(2)}) collective-permute-start(bf16[64,1024]{1,0:T(8,128)(2,1)} %refs_0_.1), channel_id=1, source_target_pairs={{0,1},{1,0},{2,3},{3,2},{4,5},{5,4},{6,7},{7,6},{8,9},{9,8},{10,11... | collective-permute-start | bytes 393224 | tf_op jit(solution)/shard_map/ppermute | solution.py:425
  3.0 15.5 %collective-permute-start.4 = (bf16[512,384]{1,0:T(8,128)(2,1)}, bf16[512,384]{1,0:T(8,128)(2,1)S(1)}, u32[]{:S(2)}, u32[]{:S(2)}) collective-permute-start(bf16[512,384]{1,0:T(8,128)(2,1)} %param.20), channel_id=1, source_target_pairs={{0,0},{1,17},{2,10},{3,27},{4,4},{5,21},{6,14},{7,31},{8,8},{9,25}... | collective-permute-start | bytes 1179656 | tf_op jit(solution)/shard_map/ppermute | solution.py:413
  12.9 5.6 %collective-permute-start.3 = (bf16[32,1024]{1,0:T(8,128)(2,1)S(1)}, bf16[32,1024]{1,0:T(8,128)(2,1)S(1)}, u32[]{:S(2)}, u32[]{:S(2)}) collective-permute-start(bf16[32,1024]{1,0:T(8,128)(2,1)S(1)} %pick_rows.1), channel_id=1, source_target_pairs={{0,4},{4,0},{8,12},{12,8},{16,20},{20,16},{24,28},{28,24},{1,5},{5... | collective-permute-start | bytes 196616 | tf_op jit(solution)/shard_map/ppermute | solution.py:449
  14.3 48.1 %all-to-all-start = ((bf16[8,128,384]{2,1,0:T(8,128)(2,1)}), bf16[8,128,384]{2,1,0:T(8,128)(2,1)}, u32[]{:S(2)}, u32[]{:S(2)}) async-start(bf16[8,128,384]{2,1,0:T(8,128)(2,1)} %spread_units.1), calls=%async_computation | async-start | bytes 1572864 | tf_op jit(solution)/shard_map/all_to_all | solution.py:437
  21.3 22.3 %collective-permute-start.5 = (bf16[64,1024]{1,0:T(8,128)(2,1)S(1)}, bf16[64,1024]{1,0:T(8,128)(2,1)S(1)}, u32[]{:S(2)}, u32[]{:S(2)}) collective-permute-start(bf16[64,1024]{1,0:T(8,128)(2,1)S(1)} %pad_maximum_fusion.2), channel_id=1, source_target_pairs={{0,16},{4,20},{8,24},{12,28},{16,0},{20,4},{24,8},{28,12},{1,17},{... | collective-permute-start | bytes 393224 | tf_op jit(solution)/shard_map/ppermute | solution.py:449
  23.6 28.0 %collective-permute-start.6 = (bf16[512,384]{1,0:T(8,128)(2,1)S(1)}, bf16[512,384]{1,0:T(8,128)(2,1)S(1)}, u32[]{:S(2)}, u32[]{:S(2)}) collective-permute-start(bf16[512,384]{1,0:T(8,128)(2,1)S(1)} %collective-permute-done.4), channel_id=1, source_target_pairs={{0,0},{1,2},{2,1},{3,3},{4,4},{5,6},{6,5},{7,7},{8,9},{9,11},{10,8... | collective-permute-start | bytes 1179656 | tf_op jit(solution)/shard_map/ppermute | solution.py:460
  28.8 15.5 %collective-permute-start.10 = (bf16[384,384]{1,0:T(8,128)(2,1)S(1)}, bf16[384,384]{1,0:T(8,128)(2,1)S(1)}, u32[]{:S(2)}, u32[]{:S(2)}) collective-permute-start(bf16[384,384]{1,0:T(8,128)(2,1)S(1)} %get-tuple-element.115), channel_id=1, source_target_pairs={{0,8},{4,12},{8,0},{12,4},{16,24},{20,28},{24,16},{28,20},{1,9},{5... | collective-permute-start | bytes 884744 | tf_op jit(solution)/shard_map/ppermute | solution.py:466
  28.8 21.9 %collective-permute-start.11 = (bf16[384,384]{1,0:T(8,128)(2,1)S(1)}, bf16[384,384]{1,0:T(8,128)(2,1)S(1)}, u32[]{:S(2)}, u32[]{:S(2)}) collective-permute-start(bf16[384,384]{1,0:T(8,128)(2,1)S(1)} %get-tuple-element.114), channel_id=1, source_target_pairs={{0,12},{4,8},{8,4},{12,0},{16,28},{20,24},{24,20},{28,16},{1,13},{... | collective-permute-start | bytes 884744 | tf_op jit(solution)/shard_map/ppermute | solution.py:466
  31.2 19.6 %collective-permute-start.9 = (bf16[384,384]{1,0:T(8,128)(2,1)S(1)}, bf16[384,384]{1,0:T(8,128)(2,1)S(1)}, u32[]{:S(2)}, u32[]{:S(2)}) collective-permute-start(bf16[384,384]{1,0:T(8,128)(2,1)S(1)} %get-tuple-element.116), channel_id=1, source_target_pairs={{0,4},{4,0},{8,12},{12,8},{16,20},{20,16},{24,28},{28,24},{1,5},{5... | collective-permute-start | bytes 884744 | tf_op jit(solution)/shard_map/ppermute | solution.py:466
  51.6 7.9 %collective-permute-start.7 = (bf16[128,1024]{1,0:T(8,128)(2,1)}, bf16[128,1024]{1,0:T(8,128)(2,1)S(1)}, u32[]{:S(2)}, u32[]{:S(2)}) collective-permute-start(bf16[128,1024]{1,0:T(8,128)(2,1)} %pad_maximum_fusion.1), channel_id=1, source_target_pairs={{0,8},{4,12},{8,0},{12,4},{16,24},{20,28},{24,16},{28,20},{1,9},{5... | collective-permute-start | bytes 786440 | tf_op jit(solution)/shard_map/ppermute | solution.py:449
  61.3 2.9 %collective-permute-start.8 = (bf16[256,1024]{1,0:T(8,128)(2,1)}, bf16[256,1024]{1,0:T(8,128)(2,1)}, u32[]{:S(2)}, u32[]{:S(2)}) collective-permute-start(bf16[256,1024]{1,0:T(8,128)(2,1)} %pad_maximum_fusion.own), channel_id=1, source_target_pairs={{0,1},{1,0},{2,3},{3,2},{4,5},{5,4},{6,7},{7,6},{8,9},{9,8},{10,11... | collective-permute-start | bytes 1572872 | tf_op jit(solution)/shard_map/ppermute | solution.py:477
  75.4 27.9 %all-to-all-start.1 = ((bf16[32,16,768]{2,1,0:T(8,128)(2,1)}), bf16[32,16,768]{2,1,0:T(8,128)(2,1)}, u32[]{:S(2)}, u32[]{:S(2)}) async-start(bf16[32,16,768]{2,1,0:T(8,128)(2,1)} %bitcast.20), calls=%async_computation.1 | async-start | bytes 1572864 | tf_op jit(solution)/shard_map/all_to_all | solution.py:512
  80.5 17.2 %collective-permute-start.13 = (bf16[512,384]{1,0:T(8,128)(2,1)S(1)}, bf16[512,384]{1,0:T(8,128)(2,1)S(1)}, u32[]{:S(2)}, u32[]{:S(2)}) collective-permute-start(bf16[512,384]{1,0:T(8,128)(2,1)S(1)} %collective-permute-done.6.refs_0_), channel_id=1, source_target_pairs={{0,4},{4,0},{8,12},{12,8},{16,20},{20,16},{24,28},{28,24},{1,5},{5... | collective-permute-start | bytes 1179656 | tf_op jit(solution)/shard_map/ppermute | solution.py:489
  81.9 20.2 %collective-permute-start.14 = (bf16[512,384]{1,0:T(8,128)(2,1)S(1)}, bf16[512,384]{1,0:T(8,128)(2,1)}, u32[]{:S(2)}, u32[]{:S(2)}) collective-permute-start(bf16[512,384]{1,0:T(8,128)(2,1)S(1)} %collective-permute-done.6.refs_0_), channel_id=1, source_target_pairs={{0,8},{4,12},{8,0},{12,4},{16,24},{20,28},{24,16},{28,20},{1,9},{5... | collective-permute-start | bytes 1179656 | tf_op jit(solution)/shard_map/ppermute | solution.py:489
  102.1 21.7 %collective-permute-start.16 = (bf16[512,384]{1,0:T(8,128)(2,1)}, bf16[512,384]{1,0:T(8,128)(2,1)}, u32[]{:S(2)}, u32[]{:S(2)}) collective-permute-start(bf16[512,384]{1,0:T(8,128)(2,1)} %collective-permute-done.14.refs_2_), channel_id=1, source_target_pairs={{0,4},{4,0},{8,12},{12,8},{16,20},{20,16},{24,28},{28,24},{1,5},{5... | collective-permute-start | bytes 1179656 | tf_op jit(solution)/shard_map/ppermute | solution.py:489
  104.3 20.3 %collective-permute-start.15 = (bf16[512,384]{1,0:T(8,128)(2,1)S(1)}, bf16[512,384]{1,0:T(8,128)(2,1)S(1)}, u32[]{:S(2)}, u32[]{:S(2)}) collective-permute-start(bf16[512,384]{1,0:T(8,128)(2,1)S(1)} %copy-done.7), channel_id=1, source_target_pairs={{0,16},{4,20},{8,24},{12,28},{16,0},{20,4},{24,8},{28,12},{1,17},{... | collective-permute-start | bytes 1179656 | tf_op jit(solution)/shard_map/ppermute | solution.py:489
  125.4 9.6 %all-to-all-start.2 = ((bf16[8,64,128]{2,1,0:T(8,128)(2,1)}), bf16[8,64,128]{2,1,0:T(8,128)(2,1)S(1)}, u32[]{:S(2)}, u32[]{:S(2)}) async-start(bf16[8,64,128]{2,1,0:T(8,128)(2,1)} %bitcast.22), calls=%async_computation.2 | async-start | bytes 262144 | tf_op jit(solution)/shard_map/all_to_all | solution.py:533
  128.8 15.6 %collective-permute-start.17 = (bf16[512,384]{1,0:T(8,128)(2,1)}, bf16[512,384]{1,0:T(8,128)(2,1)S(1)}, u32[]{:S(2)}, u32[]{:S(2)}) collective-permute-start(bf16[512,384]{1,0:T(8,128)(2,1)} %copy-done.10), channel_id=1, source_target_pairs={{0,4},{4,0},{8,12},{12,8},{16,20},{20,16},{24,28},{28,24},{1,5},{5... | collective-permute-start | bytes 1179656 | tf_op jit(solution)/shard_map/ppermute | solution.py:489
  130.2 14.3 %collective-permute-start.18 = (bf16[512,384]{1,0:T(8,128)(2,1)}, bf16[512,384]{1,0:T(8,128)(2,1)}, u32[]{:S(2)}, u32[]{:S(2)}) collective-permute-start(bf16[512,384]{1,0:T(8,128)(2,1)} %copy-done.10), channel_id=1, source_target_pairs={{0,8},{4,12},{8,0},{12,4},{16,24},{20,28},{24,16},{28,20},{1,9},{5... | collective-permute-start | bytes 1179656 | tf_op jit(solution)/shard_map/ppermute | solution.py:489
  135.7 9.8 %all-to-all-start.3 = ((bf16[8,64,128]{2,1,0:T(8,128)(2,1)}), bf16[8,64,128]{2,1,0:T(8,128)(2,1)S(1)}, u32[]{:S(2)}, u32[]{:S(2)}) async-start(bf16[8,64,128]{2,1,0:T(8,128)(2,1)} %fusion.3), calls=%async_computation.3 | async-start | bytes 262144 | tf_op jit(solution)/shard_map/all_to_all | solution.py:536
  146.1 15.8 %collective-permute-start.21 = (bf16[512,512]{1,0:T(8,128)(2,1)S(1)}, bf16[512,512]{1,0:T(8,128)(2,1)S(1)}, u32[]{:S(2)}, u32[]{:S(2)}) collective-permute-start(bf16[512,512]{1,0:T(8,128)(2,1)S(1)} %finish.1.refs_0_), channel_id=1, source_target_pairs={{0,1},{1,0},{2,3},{3,2},{4,5},{5,4},{6,7},{7,6},{8,9},{9,8},{10,11... | collective-permute-start | bytes 1572872 | tf_op jit(solution)/shard_map/ppermute | solution.py:544
  150.1 15.5 %collective-permute-start.19 = (bf16[512,512]{1,0:T(8,128)(2,1)S(1)}, bf16[512,512]{1,0:T(8,128)(2,1)S(1)}, u32[]{:S(2)}, u32[]{:S(2)}) collective-permute-start(bf16[512,512]{1,0:T(8,128)(2,1)S(1)} %finish.1.refs_0_), channel_id=1, source_target_pairs={{0,2},{1,3},{2,0},{3,1},{4,6},{5,7},{6,4},{7,5},{8,10},{9,11},{10,... | collective-permute-start | bytes 1572872 | tf_op jit(solution)/shard_map/ppermute | solution.py:550
  151.3 10.6 %collective-permute-start.20 = (bf16[512,384]{1,0:T(8,128)(2,1)}, bf16[512,384]{1,0:T(8,128)(2,1)S(1)}, u32[]{:S(2)}, u32[]{:S(2)}) collective-permute-start(bf16[512,384]{1,0:T(8,128)(2,1)} %collective-permute-done.18.refs_6_), channel_id=1, source_target_pairs={{0,4},{4,0},{8,12},{12,8},{16,20},{20,16},{24,28},{28,24},{1,5},{5... | collective-permute-start | bytes 1179656 | tf_op jit(solution)/shard_map/ppermute | solution.py:489
  (43 other events, 264.7 us)

commit v5 on v4

--- a/solution.py
+++ b/solution.py
@@ -14,7 +14,9 @@
 VMEM = pl.BlockSpec(memory_space=pltpu.VMEM)
 SMEM = pl.BlockSpec(memory_space=pltpu.SMEM)
 ANYWHERE = pl.BlockSpec(memory_space=pl.ANY)
+HBM = pl.BlockSpec(memory_space=pltpu.HBM)
 PARAMS = pltpu.CompilerParams(vmem_limit_bytes=VMEM_LIMIT)
+FETCHING = pltpu.CompilerParams(vmem_limit_bytes=56 * 1024 * 1024)
 
 
 def cost(flops, nbytes, transcendentals=0):
@@ -99,48 +101,66 @@
     )(rows, keep, *weights)
 
 
-def projector_kernel(chunk, span, meta, own, other, first, *refs):
-    seconds, (keep, send, w_keep, w_send) = refs[:span], refs[span:]
-    cols = seconds[0].shape[1]
+def projector_kernel(chunk, span, pieces, meta, *refs):
+    sources, refs = refs[:pieces], refs[pieces:]
+    first_hbm, refs = refs[0], refs[1:]
+    seconds_hbm, refs = refs[:span], refs[span:]
+    keep, send, held, first, seconds, w_keep, w_send, sems = refs
+    count = sources[0].shape[0]
+    copies = [pltpu.make_async_copy(first_hbm, first, sems.at[0])]
+    for n, source in enumerate(sources):
+        to = held.at[n * count : (n + 1) * count, :]
+        copies.append(pltpu.make_async_copy(source, to, sems.at[1 + n]))
+    for m in range(span):
+        copies.append(
+            pltpu.make_async_copy(seconds_hbm[m], seconds.at[m], sems.at[1 + pieces + m])
+        )
+    for copy in copies:
+        copy.start()
+    for copy in copies:
+        copy.wait()
+    cols = seconds.shape[2]
     same = meta[0] == meta[1]
     for m in range(0, span, 2):
-        mine, near = seconds[m][...], seconds[m + 1][...]
+        mine, near = seconds[m], seconds[m + 1]
         slot = (meta[4] ^ m) >> 1
         w_keep[slot] = jnp.where(same, mine, near)
         w_send[slot] = jnp.where(same, near, mine)
-    rows = own.shape[0]
-
-    def run(source, base):
-        @pl.loop(0, rows // chunk)
-        def _(i):
-            at = pl.ds(pl.multiple_of(i * chunk, chunk), chunk)
-            to = pl.ds(pl.multiple_of(base + i * chunk, chunk), chunk)
-            pre = dot(source[at, :], first[...])
-            hid = (0.5 * pre * (1.0 + lax.erf(pre * 0.7071067811865476))).astype(BF16)
-            for n in range(span // 2):
-                keep[to, n * cols : (n + 1) * cols] = dot(hid, w_keep[n]).astype(BF16)
-                send[to, n * cols : (n + 1) * cols] = dot(hid, w_send[n]).astype(BF16)
-
-    run(own, 0)
-    run(other, rows)
-
-
-def projector(meta, own, other, first, seconds):
-    rows, width = own.shape
+
+    @pl.loop(0, held.shape[0] // chunk)
+    def _(i):
+        at = pl.ds(pl.multiple_of(i * chunk, chunk), chunk)
+        pre = dot(held[at, :], first[...])
+        hid = (0.5 * pre * (1.0 + lax.erf(pre * 0.7071067811865476))).astype(BF16)
+        for n in range(span // 2):
+            keep[at, n * cols : (n + 1) * cols] = dot(hid, w_keep[n]).astype(BF16)
+            send[at, n * cols : (n + 1) * cols] = dot(hid, w_send[n]).astype(BF16)
+
+
+def projector(meta, sources, first, seconds):
+    rows, width = sources[0].shape
+    rows = rows * len(sources)
     units, cols = seconds[0].shape
     span = len(seconds)
-    out = jax.ShapeDtypeStruct((2 * rows, span // 2 * cols), BF16)
-    scratch = pltpu.VMEM((span // 2, units, cols), BF16)
-    return pl.pallas_call(
-        functools.partial(projector_kernel, min(rows, 256), span),
+    out = jax.ShapeDtypeStruct((rows, span // 2 * cols), BF16)
+    side = pltpu.VMEM((span // 2, units, cols), BF16)
+    return pl.pallas_call(
+        functools.partial(projector_kernel, min(rows, 256), span, len(sources)),
         out_shape=(out, out),
-        in_specs=[SMEM] + [VMEM] * (3 + span),
+        in_specs=[SMEM] + [HBM] * (len(sources) + 1 + span),
         out_specs=(VMEM, VMEM),
-        scratch_shapes=[scratch, scratch],
-        compiler_params=pltpu.CompilerParams(vmem_limit_bytes=VMEM_LIMIT),
-        cost_estimate=cost(4 * rows * units * (width + span * cols), 5e6, 2 * rows * units),
+        scratch_shapes=[
+            pltpu.VMEM((rows, width), BF16),
+            pltpu.VMEM((width, units), BF16),
+            pltpu.VMEM((span, units, cols), BF16),
+            side,
+            side,
+            pltpu.SemaphoreType.DMA((1 + len(sources) + span,)),
+        ],
+        compiler_params=FETCHING,
+        cost_estimate=cost(2 * rows * units * (width + span * cols), 5e6, rows * units),
         name="projector",
-    )(meta, own, other, first, *seconds)
+    )(meta, *sources, first, *seconds)
 
 
 def pick_kernel(spot, *refs):
@@ -229,33 +249,50 @@
     )(got, gain)
 
 
-def image_kernel(x, wq, wk, wv, text_state, out, state):
+def image_kernel(steps, x, wq, wk, wv, text_state, out, state, held, sems):
     rows = x[...]
-    key = silu(dot(rows, wk[...])).astype(BF16)
-    value = silu(dot(rows, wv[...])).astype(BF16)
-    out[1] = key
-    out[2] = value
+    depth = x.shape[1] // steps
+    order = ((1, wk), (2, wv), (0, wq))
+
+    def copy(n, w, i):
+        at = slice(i * depth, (i + 1) * depth)
+        return pltpu.make_async_copy(w.at[at, :], held.at[n, at, :], sems.at[n * steps + i])
+
+    for n, w in order:
+        for i in range(steps):
+            copy(n, w, i).start()
+    for n, w in order:
+        total = 0.0
+        for i in range(steps):
+            copy(n, w, i).wait()
+            at = slice(i * depth, (i + 1) * depth)
+            total = total + dot(rows[:, at], held[n, at, :])
+        out[n] = silu(total).astype(BF16)
     for h in range(state.shape[0]):
         cols = slice(h * HEAD_DIM, (h + 1) * HEAD_DIM)
         outer = lax.dot_general(
-            key[:, cols], value[:, cols], (((0,), (0,)), ((), ())), preferred_element_type=F32
+            out[1, :, cols], out[2, :, cols], (((0,), (0,)), ((), ())), preferred_element_type=F32
         )
         state[h] = (text_state[h] + outer).astype(BF16)
-    out[0] = silu(dot(rows, wq[...])).astype(BF16)
 
 
 def image_qkv(x, weights, text_state):
     rows, width = x.shape
     cols = weights[0].shape[1]
-    return pl.pallas_call(
-        image_kernel,
+    steps = 4 if width % 1024 == 0 else 1
+    return pl.pallas_call(
+        functools.partial(image_kernel, steps),
         out_shape=(
             jax.ShapeDtypeStruct((3, rows, cols), BF16),
             jax.ShapeDtypeStruct(text_state.shape, BF16),
         ),
-        in_specs=[VMEM] * 5,
+        in_specs=[VMEM] + [HBM] * 3 + [VMEM],
         out_specs=(VMEM, VMEM),
-        compiler_params=PARAMS,
+        scratch_shapes=[
+            pltpu.VMEM((3, width, cols), BF16),
+            pltpu.SemaphoreType.DMA((3 * steps,)),
+        ],
+        compiler_params=FETCHING,
         cost_estimate=cost(6 * rows * width * cols, 6 * width * cols, 3 * rows * cols),
         name="image_qkv",
     )(x, *weights, text_state)
@@ -338,7 +375,7 @@
     return pl.pallas_call(
         functools.partial(mix_load_kernel, tuple(mix_offsets)),
         out_shape=jax.ShapeDtypeStruct((len(mix),) + mix[0].shape, BF16),
-        in_specs=[SMEM] + [ANYWHERE] * len(mix),
+        in_specs=[SMEM] + [HBM] * len(mix),
         out_specs=VMEM,
         scratch_shapes=[pltpu.SemaphoreType.DMA((len(mix),))],
         compiler_params=PARAMS,
@@ -395,7 +432,7 @@
     part_rows = live_total // n_head
     n_pairs = n_ctx // 2
     core, parity = head & 1, ctx & 1
-    span = 4
+    span = 2
     spot_in = ctx & (span - 1)
     ratio = n_ctx // n_head
     meta = jnp.stack([parity, core, ctx, head, spot_in, ratio, n_head]).astype(jnp.int32)
@@ -449,32 +486,38 @@
         return jnp.concatenate([x, along("ctx", n_ctx, mask)(x)])
 
     masks = [1 << n for n in reversed(range(n_ctx.bit_length() - 1))]
-    masks = masks[-1:] + masks[:-1]
     offsets_ctx = [0]
     for mask in masks:
         offsets_ctx = offsets_ctx + [o ^ mask for o in offsets_ctx]
-    core_part, proj_out, stream, mix_own = lax.optimization_barrier(
-        (spread(own_rows, masks[0]), proj_out, stream, mix_own)
+    core_part, proj_out, mix_own, stream, qkv_weight = lax.optimization_barrier(
+        (spread(own_rows, masks[0]), proj_out, mix_own, stream, qkv_weight)
     )
     perm = [(index(c, h), index(c, (c // ratio) ^ turned(h, n_head))) for c, h in flat]
     mix_own = lax.ppermute(mix_own, both, perm)
-    text_rows = norm(stream)
 
     seconds = []
     for m in range(span):
         block = lax.dynamic_slice(proj_out, ((spot_in ^ m) * part, 0), (part, out_cols))
-        seconds.append(along("ctx", n_ctx, m)(block) if m else block)
-    seconds = weighty(seconds, 4e10, 1.6e8)
+        seconds.append(block)
+    seconds = [along("ctx", n_ctx, m)(x) if m else x for m, x in enumerate(seconds)]
+    seconds = weighty(seconds, 1e10, 4e7)
+    text_rows = norm(stream)
+    weights = [qkv_weight[:, i, :] for i in range(3)]
+    local_places = row_places[0] - ctx * shard_rows
+    picks = spot.reshape(1, -1) == jnp.arange(live_total, dtype=jnp.int32)[:, None]
+    places = jnp.sum(jnp.where(picks, local_places[None, :], 0), axis=1)
+    put = jnp.arange(shard_rows, dtype=jnp.int32)[:, None] == places[None, :]
+    is_text = jnp.logical_not(jnp.any(put, axis=1))[:, None]
+
+    text, text_state = text_qkv(text_rows, is_text.astype(F32), weights)
 
     core_part = spread(core_part, masks[1])
-    core_part, mix_own, text_rows, qkv_weight = lax.optimization_barrier(
-        (core_part, mix_own, text_rows, qkv_weight)
-    )
-    weights = [qkv_weight[:, i, :] for i in range(3)]
-    for mask in masks[2:]:
+    core_part, mix_own, text = lax.optimization_barrier((core_part, mix_own, text))
+    for mask in masks[2:-1]:
         core_part = spread(core_part, mask)
-    core_part, mix_own, weights = lax.optimization_barrier((core_part, mix_own, weights))
-    other_part = along("head", n_head, 1)(core_part)
+    core_parts = [core_part, along("ctx", n_ctx, masks[-1])(core_part)]
+    other_parts = [along("head", n_head, 1)(x) for x in core_parts]
+    core_parts, mix_own = lax.optimization_barrier((core_parts, mix_own))
 
     mix_blocks = {0: mix_own}
     top = n_ctx // 2
@@ -495,26 +538,15 @@
 
     mix_start(single)
 
-    keep, send = projector(meta, core_part, other_part, in_full, seconds)
+    keep, send = projector(meta, core_parts + other_parts, in_full, seconds)
     ordered = order_rows(meta, keep, along("head", n_head, 1)(send), offsets_ctx)
-    ordered, text_rows, weights = lax.optimization_barrier((ordered, text_rows, weights))
-    local_places = row_places[0] - ctx * shard_rows
-    picks = spot.reshape(1, -1) == jnp.arange(live_total, dtype=jnp.int32)[:, None]
-    places = jnp.sum(jnp.where(picks, local_places[None, :], 0), axis=1)
-    put = jnp.arange(shard_rows, dtype=jnp.int32)[:, None] == places[None, :]
-    is_text = jnp.logical_not(jnp.any(put, axis=1))[:, None]
-
-    text, text_state = mix_end(
-        single, text_qkv(text_rows, is_text.astype(F32), weights)
-    )
-    mix_start(double)
+    ordered, mix_blocks[0] = lax.optimization_barrier((ordered, mix_blocks[0]))
+    mix_start([top])
 
     received = lax.all_to_all(
         ordered.reshape(n_ctx * n_head, part_rows, span // 2 * out_cols), both, 0, 0
     )
     (received,) = weighty([received], 2e11, 8e8)
-    received, text = mix_end([0], (received, text))
-    mix_start([top])
 
     if out_cols % 128 == 0:
         img_part = image_norm(received, norm_gain[None], n_ctx, span)
@@ -526,8 +558,10 @@
         img_part = norm(summed.transpose(2, 0, 3, 1, 4).reshape(part_rows, width))
     image_rows = lax.all_gather(img_part, "head", axis=0, tiled=True)
 
+    image_rows = mix_end(single, image_rows)
+    mix_start(double)
     image, state = image_qkv(image_rows, weights, text_state)
-    state = mix_end([top] + double, state)
+    state = mix_end([top], state)
     mix_start(late)
 
     pieces = lax.all_to_all(state.reshape(n_ctx, -1, HEAD_DIM), "ctx", 0, 0).astype(F32)
@@ -535,7 +569,7 @@
     before, put = lax.optimization_barrier((before, put.astype(BF16)))
     prefix = lax.all_to_all(before, "ctx", 0, 0).reshape(state.shape)
 
-    queries, intra = mix_end(late, intra_shard(text, image, put))
+    queries, intra = mix_end(double + late, intra_shard(text, image, put))
     mix_start(last)
     heads_out = finish(intra, queries, prefix, head_gain[None])
 
@@ -550,13 +584,12 @@
         sent = sent + [along("head", n_head, bit)(p) for p in sent]
         sent_offsets = sent_offsets + [o ^ bit for o in sent_offsets]
         bit //= 2
-    near = mix_end(last, near)
+    near, sent = mix_end(last, (near, sent))
     mix_offsets, mix_blocks = list(mix_blocks), list(mix_blocks.values())
     first = None
     if mix_cols % 128 == 0:
         mix_full = mix_load(meta, mix_blocks, mix_offsets)
         first = mix_part(near, near_offsets, mix_full, ratio, n_head, None, F32)
-        sent, first = lax.optimization_barrier((sent, first))
     far = sent[1:] + [along("head", n_head, 1)(p) for p in sent[1:]]
     far_offsets = sent_offsets[1:] + [o ^ 1 for o in sent_offsets[1:]]
     if mix_cols % 128 == 0:

time: 172 us -> 157 us (0.913)
  local copies, waits for them, and re-layouts: 35.7 us -> 18.5 us
  Pallas kernels: 22.6 us -> 28.6 us
  other arithmetic: 11.9 us -> 5.94 us
  waiting for transfers between devices: 43.2 us -> 47.1 us
    unnamed x80 -> x50, local copies, waits for them, and re-layouts: 27.8 us -> 12.4 us
    all_to_all x1, waiting for transfers between devices: 0.01 us -> 7.89 us  [on_device(): lax.all_to_all(ordered.reshape(n_ctx * n_head, part_rows, span // 2 * out...]
    pallas_call x2, Pallas kernels: 5.36 us -> 11.9 us  [the longest x1 6.01 us: projector(): pl.pallas_call(functools.partial(projector_kernel, min(rows, 256), span,...]
    ppermute x3 -> x2, waiting for transfers between devices: 11.1 us -> 6.98 us  [spread(): return jnp.concatenate([x, along('ctx', n_ctx, mask)(x)])]
    all_to_all x1, starting transfers between devices: 3.25 us -> 5.8 us  [on_device(): lax.all_to_all(ordered.reshape(n_ctx * n_head, part_rows, span // 2 * out...]
    concatenate x3 -> x2, other arithmetic: 2.49 us -> 0.03 us  [spread(): return jnp.concatenate([x, along('ctx', n_ctx, mask)(x)])]
    ppermute x1, starting transfers between devices: 4.02 us -> 1.69 us  [on_device(): near.append(along('head', n_head, 1)(heads_out))]
    reduce_sum x1, other arithmetic: 2.73 us -> 0.69 us  [norm(): jnp.mean(widened * widened, axis=-1, keepdims=True) + 1e-05]
  transfers between devices with their start and end apart: 27 -> 26, of which waited for: 12 -> 11; matrix products, arithmetic and copies ran while one was open for 12% -> 8% of each run, Pallas kernels for 9% -> 12%
where the time goes in v5:
time: 157 us; the launch traced here: 156 us
  starting transfers between devices  48.1 us (31%)
  waiting for transfers between devices  47.1 us (30%)
  Pallas kernels  28.6 us (18%)
  local copies, waits for them, and re-layouts  18.5 us (12%)
  blocking collectives  7.24 us (5%)
  other arithmetic  5.94 us (4%)
    ppermute x7, waiting for transfers between devices, mix_start(): mix_blocks[offset] = along('ctx', n_ctx, mask)(mix_blocks[offset ^ mask])  17.4 us
    unnamed x50, local copies, waits for them, and re-layouts  12.4 us
    ppermute x7, starting transfers between devices, mix_start(): mix_blocks[offset] = along('ctx', n_ctx, mask)(mix_blocks[offset ^ mask])  8.67 us
    all_to_all x1, waiting for transfers between devices, on_device(): lax.all_to_all(ordered.reshape(n_ctx * n_head, part_rows, span // 2 * out...  7.89 us
    all_gather x1, blocking collectives, on_device(): image_rows = lax.all_gather(img_part, 'head', axis=0, tiled=True)  7.24 us
    ppermute x2, waiting for transfers between devices, spread(): return jnp.concatenate([x, along('ctx', n_ctx, mask)(x)])  6.98 us
    pallas_call x1, Pallas kernels, projector(): pl.pallas_call(functools.partial(projector_kernel, min(rows, 256), span,...  6.01 us
    pallas_call x1, Pallas kernels, image_qkv(): pl.pallas_call(functools.partial(image_kernel, steps), out_shape=(jax.Sha...  5.88 us
  transfers between devices with their start and end apart: 26, of which 11 were waited for; matrix products, arithmetic and copies ran while one was open for 8% of the time, Pallas kernels for 12%

profile of v5, /device:TPU:1, one launch (start us, length us, event | category | flops | bytes accessed | tf_op | source)
XLA Modules:
  0.0 155.9 jit_solution(10558838573716950719)
XLA Ops:
  0.0 2.0 %collective-permute-start = (bf16[64,1024]{1,0:T(8,128)(2,1)}, bf16[64,1024]{1,0:T(8,128)(2,1)S(1)}, u32[]{:S(2)}, u32[]{:S(2)}) collective-permute-start(bf16[64,1024]{1,0:T(8,128)(2,1)} %refs_0_.1), channel_id=1, source_target_pairs={{0,2},{1,3},{2,0},{3,1},{4,6},{5,7},{6,4},{7,5},{8,10},{9,11},{10,... | collective-permute-start | bytes 393224 | tf_op jit(solution)/shard_map/ppermute | solution.py:462
  3.0 4.2 %collective-permute-start.4 = (bf16[512,384]{1,0:T(8,128)(2,1)}, bf16[512,384]{1,0:T(8,128)(2,1)S(1)}, u32[]{:S(2)}, u32[]{:S(2)}) collective-permute-start(bf16[512,384]{1,0:T(8,128)(2,1)} %param.20), channel_id=1, source_target_pairs={{0,0},{1,17},{2,10},{3,27},{4,4},{5,21},{6,14},{7,31},{8,8},{9,25}... | collective-permute-start | bytes 1179656 | tf_op jit(solution)/shard_map/ppermute | solution.py:450
  15.2 5.6 %all-to-all-start = ((bf16[8,128,768]{2,1,0:T(8,128)(2,1)}), bf16[8,128,768]{2,1,0:T(8,128)(2,1)S(1)}, u32[]{:S(2)}, u32[]{:S(2)}) async-start(bf16[8,128,768]{2,1,0:T(8,128)(2,1)} %spread_units.1), calls=%async_computation | async-start | bytes 3145728 | tf_op jit(solution)/shard_map/all_to_all | solution.py:474
  20.8 4.3 %slice_bitcast_fusion = (bf16[3072,512]{1,0:T(8,128)(2,1)S(1)}, bf16[3072,512]{1,0:T(8,128)(2,1)S(1)}, bf16[3072,512]{1,0:T(8,128)(2,1)S(1)}) fusion(bf16[3072,3,512]{2,0,1:T(8,128)(2,1)} %param.18), kind=kLoop, calls=%fused_computation.5 | loop fusion | bytes 18874368 | tf_op jit(solution)/shard_map/squeeze | solution.py:505
  26.6 3.6 %collective-permute-start.6 = (bf16[512,384]{1,0:T(8,128)(2,1)S(1)}, bf16[512,384]{1,0:T(8,128)(2,1)}, u32[]{:S(2)}, u32[]{:S(2)}) collective-permute-start(bf16[512,384]{1,0:T(8,128)(2,1)S(1)} %collective-permute-done.4), channel_id=1, source_target_pairs={{0,0},{1,2},{2,1},{3,3},{4,4},{5,6},{6,5},{7,7},{8,9},{9,11},{10,8... | collective-permute-start | bytes 1179656 | tf_op jit(solution)/shard_map/ppermute | solution.py:496
  34.4 5.7 %text_qkv.1 = (bf16[3,512,512]{2,1,0:T(8,128)(2,1)S(1)}, f32[4,128,128]{2,1,0:T(8,128)S(1)}) custom-call(bf16[512,3072]{1,0:T(8,128)(2,1)S(1)} %fusion.2.rows, f32[512,1]{1,0:T(8,128)S(1)} %copy.17.keep, bf16[3072,512]{1,0:T(8,128)(2,1)S(1)} %get-tuple-element.89.wq, bf16[3072,512]{1,0:T(8,128)(2,1)S(1)} %get-tuple-element.88.wk, ...), custom_call_target="tpu_custom_call" | custom-call | flops 4831838208 | bytes 9437184 | tf_op jit(solution)/shard_map/text_qkv/pallas_call | solution.py:90
  41.9 7.0 %collective-permute-done.5 = bf16[64,1024]{1,0:T(8,128)(2,1)S(1)} collective-permute-done((bf16[64,1024]{1,0:T(8,128)(2,1)S(1)}, bf16[64,1024]{1,0:T(8,128)(2,1)S(1)}, u32[]{:S(2)}, u32[]{:S(2)}) %collective-permute-start.5) | collective-permute-done | bytes 131104 | tf_op jit(solution)/shard_map/ppermute | solution.py:486
  49.6 2.2 %collective-permute-start.10 = (bf16[128,1024]{1,0:T(8,128)(2,1)S(1)}, bf16[128,1024]{1,0:T(8,128)(2,1)S(1)}, u32[]{:S(2)}, u32[]{:S(2)}) collective-permute-start(bf16[128,1024]{1,0:T(8,128)(2,1)S(1)} %pad_maximum_fusion.refs_0_), channel_id=1, source_target_pairs={{0,1},{1,0},{2,3},{3,2},{4,5},{5,4},{6,7},{7,6},{8,9},{9,8},{10,11... | collective-permute-start | bytes 786440 | tf_op jit(solution)/shard_map/ppermute | solution.py:519
  51.9 2.5 %collective-permute-done.12.refs_1_ = bf16[768,384]{1,0:T(8,128)(2,1)S(1)} collective-permute-done((bf16[768,384]{1,0:T(8,128)(2,1)S(1)}, bf16[768,384]{1,0:T(8,128)(2,1)S(1)}, u32[]{:S(2)}, u32[]{:S(2)}) %collective-permute-start.12) | collective-permute-done | bytes 589856 | tf_op jit(solution)/shard_map/ppermute | solution.py:502
  55.2 4.8 %collective-permute-done.7.refs_1_ = bf16[128,1024]{1,0:T(8,128)(2,1)S(1)} collective-permute-done((bf16[128,1024]{1,0:T(8,128)(2,1)S(1)}, bf16[128,1024]{1,0:T(8,128)(2,1)S(1)}, u32[]{:S(2)}, u32[]{:S(2)}) %collective-permute-start.7) | collective-permute-done | bytes 262176 | tf_op jit(solution)/shard_map/ppermute | solution.py:518
  62.4 6.0 %projector.1 = (bf16[512,384]{1,0:T(8,128)(2,1)}, bf16[512,384]{1,0:T(8,128)(2,1)}) custom-call(s32[7]{0:T(128)} %stack.20.meta, bf16[128,1024]{1,0:T(8,128)(2,1)} %copy-done.20, bf16[128,1024]{1,0:T(8,128)(2,1)} %copy-done.22, bf16[128,1024]{1,0:T(8,128)(2,1)} %copy-done.23, bf16[128,1024]{1,0:T(8,128)(2,1)} %copy-done.24, bf16[1024,768]{1,0:T(8,128)(2,1)} %bitcast.22, ...), custom_call_target="tpu_custom_call" | custom-call | flops 1409286144 | bytes 5000000 | tf_op jit(solution)/shard_map/projector/pallas_call | solution.py:147
  72.8 5.8 %all-to-all-start.1 = ((bf16[32,16,384]{2,1,0:T(8,128)(2,1)}), bf16[32,16,384]{2,1,0:T(8,128)(2,1)S(1)}, u32[]{:S(2)}, u32[]{:S(2)}) async-start(bf16[32,16,384]{2,1,0:T(8,128)(2,1)} %bitcast.11), calls=%async_computation.1 | async-start | bytes 786432 | tf_op jit(solution)/shard_map/all_to_all | solution.py:546
  81.3 2.2 %collective-permute-start.15 = (bf16[512,384]{1,0:T(8,128)(2,1)}, bf16[512,384]{1,0:T(8,128)(2,1)}, u32[]{:S(2)}, u32[]{:S(2)}) collective-permute-start(bf16[512,384]{1,0:T(8,128)(2,1)} %collective-permute-done.6.refs_0_), channel_id=1, source_target_pairs={{0,16},{4,20},{8,24},{12,28},{16,0},{20,4},{24,8},{28,12},{1,17},{... | collective-permute-start | bytes 1179656 | tf_op jit(solution)/shard_map/ppermute | solution.py:532
  83.4 7.9 %all-to-all-done.1.refs_0_ = bf16[32,16,384]{2,1,0:T(8,128)(2,1)S(1)} async-done(((bf16[32,16,384]{2,1,0:T(8,128)(2,1)}), bf16[32,16,384]{2,1,0:T(8,128)(2,1)S(1)}, u32[]{:S(2)}, u32[]{:S(2)}) %all-to-all-start.1) | async-done | bytes 393248 | tf_op jit(solution)/shard_map/all_to_all | solution.py:546
  93.9 7.2 %all_gather.3.x = bf16[64,3072]{1,0:T(8,128)(2,1)} all-gather(bf16[16,3072]{1,0:T(8,128)(2,1)S(1)} %image_norm.1), channel_id=1, replica_groups=mesh['ctx'=8,'head'=4] {'head'}, dimensions={0}, use_global_device_ids=true | all-gather | bytes 491520 | tf_op jit(solution)/shard_map/all_gather | solution.py:559
  103.1 5.9 %image_qkv.1 = (bf16[3,64,512]{2,1,0:T(8,128)(2,1)}, bf16[4,128,128]{2,1,0:T(8,128)(2,1)}) custom-call(bf16[64,3072]{1,0:T(8,128)(2,1)} %all_gather.3.x, bf16[3072,512]{1,0:T(8,128)(2,1)} %copy-done.2, bf16[3072,512]{1,0:T(8,128)(2,1)} %copy-done.1, bf16[3072,512]{1,0:T(8,128)(2,1)} %copy-done, f32[4,128,128]{2,1,0:T(8,128)} %copy-done.7), custom_call_target="tpu_custom_call" | custom-call | flops 603979776 | bytes 9437184 | tf_op jit(solution)/shard_map/image_qkv/pallas_call | solution.py:283
  109.0 3.6 %all-to-all-start.2 = ((bf16[8,64,128]{2,1,0:T(8,128)(2,1)}), bf16[8,64,128]{2,1,0:T(8,128)(2,1)S(1)}, u32[]{:S(2)}, u32[]{:S(2)}) async-start(bf16[8,64,128]{2,1,0:T(8,128)(2,1)} %bitcast.23), calls=%async_computation.2 | async-start | bytes 262144 | tf_op jit(solution)/shard_map/all_to_all | solution.py:567
  115.5 3.5 %all-to-all-done.2 = bf16[8,64,128]{2,1,0:T(8,128)(2,1)S(1)} async-done(((bf16[8,64,128]{2,1,0:T(8,128)(2,1)}), bf16[8,64,128]{2,1,0:T(8,128)(2,1)S(1)}, u32[]{:S(2)}, u32[]{:S(2)}) %all-to-all-start.2) | async-done | bytes 131104 | tf_op jit(solution)/shard_map/all_to_all | solution.py:567
  119.7 3.4 %all-to-all-start.3 = ((bf16[8,64,128]{2,1,0:T(8,128)(2,1)}), bf16[8,64,128]{2,1,0:T(8,128)(2,1)S(1)}, u32[]{:S(2)}, u32[]{:S(2)}) async-start(bf16[8,64,128]{2,1,0:T(8,128)(2,1)} %fusion.3), calls=%async_computation.3 | async-start | bytes 262144 | tf_op jit(solution)/shard_map/all_to_all | solution.py:570
  125.4 2.0 %intra_shard.1 = (bf16[512,512]{1,0:T(8,128)(2,1)S(1)}, f32[512,512]{1,0:T(8,128)S(1)}) custom-call(bf16[3,512,512]{2,1,0:T(8,128)(2,1)S(1)} %copy-done.16, bf16[3,64,512]{2,1,0:T(8,128)(2,1)S(1)} %copy-done.14, bf16[512,64]{1,0:T(8,128)(2,1)S(1)} %get-tuple-element.73.put), custom_call_target="tpu_custom_call" | custom-call | flops 20000000000 | bytes 40000000 | tf_op jit(solution)/shard_map/intra_shard/pallas_call | solution.py:342
  127.5 6.1 %collective-permute-done.14.refs_4_ = bf16[512,384]{1,0:T(8,128)(2,1)S(1)} collective-permute-done((bf16[512,384]{1,0:T(8,128)(2,1)}, bf16[512,384]{1,0:T(8,128)(2,1)S(1)}, u32[]{:S(2)}, u32[]{:S(2)}) %collective-permute-start.14) | collective-permute-done | bytes 393248 | tf_op jit(solution)/shard_map/ppermute | solution.py:532
  138.3 9.4 %collective-permute-done.18.refs_7_ = bf16[512,384]{1,0:T(8,128)(2,1)S(1)} collective-permute-done((bf16[512,384]{1,0:T(8,128)(2,1)S(1)}, bf16[512,384]{1,0:T(8,128)(2,1)S(1)}, u32[]{:S(2)}, u32[]{:S(2)}) %collective-permute-start.18) | collective-permute-done | bytes 393248 | tf_op jit(solution)/shard_map/ppermute | solution.py:532
  150.5 2.0 %mix_load.1.refs_2_ = bf16[8,512,384]{2,1,0:T(8,128)(2,1)S(1)} custom-call(s32[7]{0:T(128)S(1)} %copy-done.12, bf16[512,384]{1,0:T(8,128)(2,1)} %collective-permute-done.6.refs_0_, bf16[512,384]{1,0:T(8,128)(2,1)} %collective-permute-done.8.refs_1_, bf16[512,384]{1,0:T(8,128)(2,1)} %collective-permute-done.9.refs_2_, ...), custom_call_target="tpu_custom_call" | custom-call | bytes 6291456 | tf_op jit(solution)/shard_map/mix_load/pallas_call | solution.py:375
  153.8 2.1 %mix_part.3 = bf16[512,768]{1,0:T(8,128)(2,1)} custom-call(bf16[512,512]{1,0:T(8,128)(2,1)S(1)} %collective-permute-done.20.refs_0_, bf16[512,512]{1,0:T(8,128)(2,1)S(1)} %collective-permute-done.21.refs_1_, bf16[8,512,384]{2,1,0:T(8,128)(2,1)S(1)} %mix_load.1.refs_2_, f32[512,768]{1,0:T(8,128)S(1)} %mix_part.2.refs_3_), custom_call_target="tpu_custom_call" | custom-call | flops 805306368 | bytes 5000000 | tf_op jit(solution)/shard_map/mix_part/pallas_call | solution.py:402
  (116 shorter events, 46.5 us)
Async XLA Ops:
  0.0 10.6 %collective-permute-start = (bf16[64,1024]{1,0:T(8,128)(2,1)}, bf16[64,1024]{1,0:T(8,128)(2,1)S(1)}, u32[]{:S(2)}, u32[]{:S(2)}) collective-permute-start(bf16[64,1024]{1,0:T(8,128)(2,1)} %refs_0_.1), channel_id=1, source_target_pairs={{0,2},{1,3},{2,0},{3,1},{4,6},{5,7},{6,4},{7,5},{8,10},{9,11},{10,... | collective-permute-start | bytes 393224 | tf_op jit(solution)/shard_map/ppermute | solution.py:462
  2.0 11.0 %collective-permute-start.1 = (bf16[64,1024]{1,0:T(8,128)(2,1)}, bf16[64,1024]{1,0:T(8,128)(2,1)S(1)}, u32[]{:S(2)}, u32[]{:S(2)}) collective-permute-start(bf16[64,1024]{1,0:T(8,128)(2,1)} %refs_0_.1), channel_id=1, source_target_pairs={{0,1},{1,0},{2,3},{3,2},{4,5},{5,4},{6,7},{7,6},{8,9},{9,8},{10,11... | collective-permute-start | bytes 393224 | tf_op jit(solution)/shard_map/ppermute | solution.py:462
  3.0 17.8 %collective-permute-start.4 = (bf16[512,384]{1,0:T(8,128)(2,1)}, bf16[512,384]{1,0:T(8,128)(2,1)S(1)}, u32[]{:S(2)}, u32[]{:S(2)}) collective-permute-start(bf16[512,384]{1,0:T(8,128)(2,1)} %param.20), channel_id=1, source_target_pairs={{0,0},{1,17},{2,10},{3,27},{4,4},{5,21},{6,14},{7,31},{8,8},{9,25}... | collective-permute-start | bytes 1179656 | tf_op jit(solution)/shard_map/ppermute | solution.py:450
  10.6 2.5 %collective-permute-start.2 = (bf16[64,1024]{1,0:T(8,128)(2,1)S(1)}, bf16[64,1024]{1,0:T(8,128)(2,1)S(1)}, u32[]{:S(2)}, u32[]{:S(2)}) collective-permute-start(bf16[64,1024]{1,0:T(8,128)(2,1)S(1)} %collective-permute-done.refs_1_), channel_id=1, source_target_pairs={{0,1},{1,0},{2,3},{3,2},{4,5},{5,4},{6,7},{7,6},{8,9},{9,8},{10,11... | collective-permute-start | bytes 393224 | tf_op jit(solution)/shard_map/ppermute | solution.py:462
  14.3 6.4 %collective-permute-start.3 = (bf16[32,1024]{1,0:T(8,128)(2,1)S(1)}, bf16[32,1024]{1,0:T(8,128)(2,1)S(1)}, u32[]{:S(2)}, u32[]{:S(2)}) collective-permute-start(bf16[32,1024]{1,0:T(8,128)(2,1)S(1)} %pick_rows.1), channel_id=1, source_target_pairs={{0,16},{4,20},{8,24},{12,28},{16,0},{20,4},{24,8},{28,12},{1,17},{... | collective-permute-start | bytes 196616 | tf_op jit(solution)/shard_map/ppermute | solution.py:486
  15.2 45.2 %all-to-all-start = ((bf16[8,128,768]{2,1,0:T(8,128)(2,1)}), bf16[8,128,768]{2,1,0:T(8,128)(2,1)S(1)}, u32[]{:S(2)}, u32[]{:S(2)}) async-start(bf16[8,128,768]{2,1,0:T(8,128)(2,1)} %spread_units.1), calls=%async_computation | async-start | bytes 3145728 | tf_op jit(solution)/shard_map/all_to_all | solution.py:474
  25.1 23.8 %collective-permute-start.5 = (bf16[64,1024]{1,0:T(8,128)(2,1)S(1)}, bf16[64,1024]{1,0:T(8,128)(2,1)S(1)}, u32[]{:S(2)}, u32[]{:S(2)}) collective-permute-start(bf16[64,1024]{1,0:T(8,128)(2,1)S(1)} %pad_maximum_fusion.1), channel_id=1, source_target_pairs={{0,8},{4,12},{8,0},{12,4},{16,24},{20,28},{24,16},{28,20},{1,9},{5... | collective-permute-start | bytes 393224 | tf_op jit(solution)/shard_map/ppermute | solution.py:486
  26.6 22.3 %collective-permute-start.6 = (bf16[512,384]{1,0:T(8,128)(2,1)S(1)}, bf16[512,384]{1,0:T(8,128)(2,1)}, u32[]{:S(2)}, u32[]{:S(2)}) collective-permute-start(bf16[512,384]{1,0:T(8,128)(2,1)S(1)} %collective-permute-done.4), channel_id=1, source_target_pairs={{0,0},{1,2},{2,1},{3,3},{4,4},{5,6},{6,5},{7,7},{8,9},{9,11},{10,8... | collective-permute-start | bytes 1179656 | tf_op jit(solution)/shard_map/ppermute | solution.py:496
  31.2 23.1 %collective-permute-start.12 = (bf16[768,384]{1,0:T(8,128)(2,1)S(1)}, bf16[768,384]{1,0:T(8,128)(2,1)S(1)}, u32[]{:S(2)}, u32[]{:S(2)}) collective-permute-start(bf16[768,384]{1,0:T(8,128)(2,1)S(1)} %get-tuple-element.90), channel_id=1, source_target_pairs={{0,4},{4,0},{8,12},{12,8},{16,20},{20,16},{24,28},{28,24},{1,5},{5... | collective-permute-start | bytes 1769480 | tf_op jit(solution)/shard_map/ppermute | solution.py:502
  48.9 11.0 %collective-permute-start.7 = (bf16[128,1024]{1,0:T(8,128)(2,1)S(1)}, bf16[128,1024]{1,0:T(8,128)(2,1)S(1)}, u32[]{:S(2)}, u32[]{:S(2)}) collective-permute-start(bf16[128,1024]{1,0:T(8,128)(2,1)S(1)} %pad_maximum_fusion.refs_0_), channel_id=1, source_target_pairs={{0,4},{4,0},{8,12},{12,8},{16,20},{20,16},{24,28},{28,24},{1,5},{5... | collective-permute-start | bytes 786440 | tf_op jit(solution)/shard_map/ppermute | solution.py:518
  49.6 12.0 %collective-permute-start.10 = (bf16[128,1024]{1,0:T(8,128)(2,1)S(1)}, bf16[128,1024]{1,0:T(8,128)(2,1)S(1)}, u32[]{:S(2)}, u32[]{:S(2)}) collective-permute-start(bf16[128,1024]{1,0:T(8,128)(2,1)S(1)} %pad_maximum_fusion.refs_0_), channel_id=1, source_target_pairs={{0,1},{1,0},{2,3},{3,2},{4,5},{5,4},{6,7},{7,6},{8,9},{9,8},{10,11... | collective-permute-start | bytes 786440 | tf_op jit(solution)/shard_map/ppermute | solution.py:519
  72.8 18.5 %all-to-all-start.1 = ((bf16[32,16,384]{2,1,0:T(8,128)(2,1)}), bf16[32,16,384]{2,1,0:T(8,128)(2,1)S(1)}, u32[]{:S(2)}, u32[]{:S(2)}) async-start(bf16[32,16,384]{2,1,0:T(8,128)(2,1)} %bitcast.11), calls=%async_computation.1 | async-start | bytes 786432 | tf_op jit(solution)/shard_map/all_to_all | solution.py:546
  78.6 22.6 %collective-permute-start.8 = (bf16[512,384]{1,0:T(8,128)(2,1)}, bf16[512,384]{1,0:T(8,128)(2,1)}, u32[]{:S(2)}, u32[]{:S(2)}) collective-permute-start(bf16[512,384]{1,0:T(8,128)(2,1)} %collective-permute-done.6.refs_0_), channel_id=1, source_target_pairs={{0,4},{4,0},{8,12},{12,8},{16,20},{20,16},{24,28},{28,24},{1,5},{5... | collective-permute-start | bytes 1179656 | tf_op jit(solution)/shard_map/ppermute | solution.py:532
  80.1 23.0 %collective-permute-start.9 = (bf16[512,384]{1,0:T(8,128)(2,1)}, bf16[512,384]{1,0:T(8,128)(2,1)}, u32[]{:S(2)}, u32[]{:S(2)}) collective-permute-start(bf16[512,384]{1,0:T(8,128)(2,1)} %collective-permute-done.6.refs_0_), channel_id=1, source_target_pairs={{0,8},{4,12},{8,0},{12,4},{16,24},{20,28},{24,16},{28,20},{1,9},{5... | collective-permute-start | bytes 1179656 | tf_op jit(solution)/shard_map/ppermute | solution.py:532
  81.3 27.7 %collective-permute-start.15 = (bf16[512,384]{1,0:T(8,128)(2,1)}, bf16[512,384]{1,0:T(8,128)(2,1)}, u32[]{:S(2)}, u32[]{:S(2)}) collective-permute-start(bf16[512,384]{1,0:T(8,128)(2,1)} %collective-permute-done.6.refs_0_), channel_id=1, source_target_pairs={{0,16},{4,20},{8,24},{12,28},{16,0},{20,4},{24,8},{28,12},{1,17},{... | collective-permute-start | bytes 1179656 | tf_op jit(solution)/shard_map/ppermute | solution.py:532
  109.0 10.0 %all-to-all-start.2 = ((bf16[8,64,128]{2,1,0:T(8,128)(2,1)}), bf16[8,64,128]{2,1,0:T(8,128)(2,1)S(1)}, u32[]{:S(2)}, u32[]{:S(2)}) async-start(bf16[8,64,128]{2,1,0:T(8,128)(2,1)} %bitcast.23), calls=%async_computation.2 | async-start | bytes 262144 | tf_op jit(solution)/shard_map/all_to_all | solution.py:567
  112.6 14.9 %collective-permute-start.16 = (bf16[512,384]{1,0:T(8,128)(2,1)}, bf16[512,384]{1,0:T(8,128)(2,1)S(1)}, u32[]{:S(2)}, u32[]{:S(2)}) collective-permute-start(bf16[512,384]{1,0:T(8,128)(2,1)} %collective-permute-done.15.refs_3_), channel_id=1, source_target_pairs={{0,4},{4,0},{8,12},{12,8},{16,20},{20,16},{24,28},{28,24},{1,5},{5... | collective-permute-start | bytes 1179656 | tf_op jit(solution)/shard_map/ppermute | solution.py:532
  114.1 13.4 %collective-permute-start.17 = (bf16[512,384]{1,0:T(8,128)(2,1)}, bf16[512,384]{1,0:T(8,128)(2,1)S(1)}, u32[]{:S(2)}, u32[]{:S(2)}) collective-permute-start(bf16[512,384]{1,0:T(8,128)(2,1)} %collective-permute-done.15.refs_3_), channel_id=1, source_target_pairs={{0,8},{4,12},{8,0},{12,4},{16,24},{20,28},{24,16},{28,20},{1,9},{5... | collective-permute-start | bytes 1179656 | tf_op jit(solution)/shard_map/ppermute | solution.py:532
  115.2 18.3 %collective-permute-start.14 = (bf16[512,384]{1,0:T(8,128)(2,1)}, bf16[512,384]{1,0:T(8,128)(2,1)S(1)}, u32[]{:S(2)}, u32[]{:S(2)}) collective-permute-start(bf16[512,384]{1,0:T(8,128)(2,1)} %collective-permute-done.9.refs_2_), channel_id=1, source_target_pairs={{0,4},{4,0},{8,12},{12,8},{16,20},{20,16},{24,28},{28,24},{1,5},{5... | collective-permute-start | bytes 1179656 | tf_op jit(solution)/shard_map/ppermute | solution.py:532
  119.7 14.2 %all-to-all-start.3 = ((bf16[8,64,128]{2,1,0:T(8,128)(2,1)}), bf16[8,64,128]{2,1,0:T(8,128)(2,1)S(1)}, u32[]{:S(2)}, u32[]{:S(2)}) async-start(bf16[8,64,128]{2,1,0:T(8,128)(2,1)} %fusion.3), calls=%async_computation.3 | async-start | bytes 262144 | tf_op jit(solution)/shard_map/all_to_all | solution.py:570
  134.5 13.3 %collective-permute-start.19 = (bf16[512,512]{1,0:T(8,128)(2,1)S(1)}, bf16[512,512]{1,0:T(8,128)(2,1)S(1)}, u32[]{:S(2)}, u32[]{:S(2)}) collective-permute-start(bf16[512,512]{1,0:T(8,128)(2,1)S(1)} %finish.1.refs_0_), channel_id=1, source_target_pairs={{0,1},{1,0},{2,3},{3,2},{4,5},{5,4},{6,7},{7,6},{8,9},{9,8},{10,11... | collective-permute-start | bytes 1572872 | tf_op jit(solution)/shard_map/ppermute | solution.py:578
  136.2 13.5 %collective-permute-start.20 = (bf16[512,512]{1,0:T(8,128)(2,1)S(1)}, bf16[512,512]{1,0:T(8,128)(2,1)S(1)}, u32[]{:S(2)}, u32[]{:S(2)}) collective-permute-start(bf16[512,512]{1,0:T(8,128)(2,1)S(1)} %finish.1.refs_0_), channel_id=1, source_target_pairs={{0,2},{1,3},{2,0},{3,1},{4,6},{5,7},{6,4},{7,5},{8,10},{9,11},{10,... | collective-permute-start | bytes 1572872 | tf_op jit(solution)/shard_map/ppermute | solution.py:584
  137.4 10.4 %collective-permute-start.18 = (bf16[512,384]{1,0:T(8,128)(2,1)S(1)}, bf16[512,384]{1,0:T(8,128)(2,1)S(1)}, u32[]{:S(2)}, u32[]{:S(2)}) collective-permute-start(bf16[512,384]{1,0:T(8,128)(2,1)S(1)} %collective-permute-done.17.refs_6_), channel_id=1, source_target_pairs={{0,4},{4,0},{8,12},{12,8},{16,20},{20,16},{24,28},{28,24},{1,5},{5... | collective-permute-start | bytes 1179656 | tf_op jit(solution)/shard_map/ppermute | solution.py:532
  149.7 4.1 %collective-permute-start.21 = (bf16[512,512]{1,0:T(8,128)(2,1)S(1)}, bf16[512,512]{1,0:T(8,128)(2,1)S(1)}, u32[]{:S(2)}, u32[]{:S(2)}) collective-permute-start(bf16[512,512]{1,0:T(8,128)(2,1)S(1)} %collective-permute-done.20.refs_0_), channel_id=1, source_target_pairs={{0,1},{1,0},{2,3},{3,2},{4,5},{5,4},{6,7},{7,6},{8,9},{9,8},{10,11... | collective-permute-start | bytes 1572872 | tf_op jit(solution)/shard_map/ppermute | solution.py:593
  (27 other events, 124.2 us)

commit v6 on v5

--- a/solution.py
+++ b/solution.py
@@ -528,7 +528,7 @@
 
     def mix_start(stage):
         for offset in stage:
-            mask = offset & -offset
+            mask = 1 << offset.bit_length() - 1 if offset in double else offset & -offset
             mix_blocks[offset] = along("ctx", n_ctx, mask)(mix_blocks[offset ^ mask])
 
     def mix_end(stage, beside):
@@ -558,10 +558,8 @@
         img_part = norm(summed.transpose(2, 0, 3, 1, 4).reshape(part_rows, width))
     image_rows = lax.all_gather(img_part, "head", axis=0, tiled=True)
 
-    image_rows = mix_end(single, image_rows)
-    mix_start(double)
     image, state = image_qkv(image_rows, weights, text_state)
-    state = mix_end([top], state)
+    state = mix_end([top] + single, state)
     mix_start(late)
 
     pieces = lax.all_to_all(state.reshape(n_ctx, -1, HEAD_DIM), "ctx", 0, 0).astype(F32)
@@ -569,8 +567,8 @@
     before, put = lax.optimization_barrier((before, put.astype(BF16)))
     prefix = lax.all_to_all(before, "ctx", 0, 0).reshape(state.shape)
 
-    queries, intra = mix_end(double + late, intra_shard(text, image, put))
-    mix_start(last)
+    queries, intra = mix_end(late, intra_shard(text, image, put))
+    mix_start(double + last)
     heads_out = finish(intra, queries, prefix, head_gain[None])
 
     mix_cols = mix_weight.shape[1]
@@ -584,7 +582,7 @@
         sent = sent + [along("head", n_head, bit)(p) for p in sent]
         sent_offsets = sent_offsets + [o ^ bit for o in sent_offsets]
         bit //= 2
-    near, sent = mix_end(last, (near, sent))
+    near, sent = mix_end(double + last, (near, sent))
     mix_offsets, mix_blocks = list(mix_blocks), list(mix_blocks.values())
     first = None
     if mix_cols % 128 == 0:

time: 157 us -> 152 us (0.968)
  waiting for transfers between devices: 47.1 us -> 40.9 us
    ppermute x7, waiting for transfers between devices: 17.4 us -> 9.9 us  [mix_start(): mix_blocks[offset] = along('ctx', n_ctx, mask)(mix_blocks[offset ^ mask])]
    ppermute x1, starting transfers between devices: 1.69 us -> 3.77 us  [on_device(): near.append(along('head', n_head, 1)(heads_out))]
  transfers between devices with their start and end apart: 26 -> 26, of which waited for: 11 -> 10; matrix products, arithmetic and copies ran while one was open for 8% -> 8% of each run, Pallas kernels for 12% -> 12%
where the time goes in v6:
time: 152 us; the launch traced here: 151 us
  starting transfers between devices  49.1 us (32%)
  waiting for transfers between devices  40.9 us (27%)
  Pallas kernels  28.7 us (19%)
  local copies, waits for them, and re-layouts  18.7 us (12%)
  blocking collectives  7.24 us (5%)
  other arithmetic  5.94 us (4%)
    unnamed x50, local copies, waits for them, and re-layouts  12.4 us
    ppermute x7, waiting for transfers between devices, mix_start(): mix_blocks[offset] = along('ctx', n_ctx, mask)(mix_blocks[offset ^ mask])  9.9 us
    ppermute x7, starting transfers between devices, mix_start(): mix_blocks[offset] = along('ctx', n_ctx, mask)(mix_blocks[offset ^ mask])  8.19 us
    all_to_all x1, waiting for transfers between devices, on_device(): lax.all_to_all(ordered.reshape(n_ctx * n_head, part_rows, span // 2 * out...  7.89 us
    all_gather x1, blocking collectives, on_device(): image_rows = lax.all_gather(img_part, 'head', axis=0, tiled=True)  7.24 us
    ppermute x2, waiting for transfers between devices, spread(): return jnp.concatenate([x, along('ctx', n_ctx, mask)(x)])  6.83 us
    pallas_call x1, Pallas kernels, projector(): pl.pallas_call(functools.partial(projector_kernel, min(rows, 256), span,...  6.01 us
    pallas_call x1, Pallas kernels, image_qkv(): pl.pallas_call(functools.partial(image_kernel, steps), out_shape=(jax.Sha...  5.88 us
  transfers between devices with their start and end apart: 26, of which 10 were waited for; matrix products, arithmetic and copies ran while one was open for 8% of the time, Pallas kernels for 12%

profile of v6, /device:TPU:1, one launch (start us, length us, event | category | flops | bytes accessed | tf_op | source)
XLA Modules:
  0.0 150.9 jit_solution(7499369077579803177)
XLA Ops:
  0.0 2.0 %collective-permute-start = (bf16[64,1024]{1,0:T(8,128)(2,1)}, bf16[64,1024]{1,0:T(8,128)(2,1)S(1)}, u32[]{:S(2)}, u32[]{:S(2)}) collective-permute-start(bf16[64,1024]{1,0:T(8,128)(2,1)} %refs_0_.1), channel_id=1, source_target_pairs={{0,2},{1,3},{2,0},{3,1},{4,6},{5,7},{6,4},{7,5},{8,10},{9,11},{10,... | collective-permute-start | bytes 393224 | tf_op jit(solution)/shard_map/ppermute | solution.py:462
  3.0 4.2 %collective-permute-start.4 = (bf16[512,384]{1,0:T(8,128)(2,1)}, bf16[512,384]{1,0:T(8,128)(2,1)S(1)}, u32[]{:S(2)}, u32[]{:S(2)}) collective-permute-start(bf16[512,384]{1,0:T(8,128)(2,1)} %param.20), channel_id=1, source_target_pairs={{0,0},{1,17},{2,10},{3,27},{4,4},{5,21},{6,14},{7,31},{8,8},{9,25}... | collective-permute-start | bytes 1179656 | tf_op jit(solution)/shard_map/ppermute | solution.py:450
  15.2 5.6 %all-to-all-start = ((bf16[8,128,768]{2,1,0:T(8,128)(2,1)}), bf16[8,128,768]{2,1,0:T(8,128)(2,1)S(1)}, u32[]{:S(2)}, u32[]{:S(2)}) async-start(bf16[8,128,768]{2,1,0:T(8,128)(2,1)} %spread_units.1), calls=%async_computation | async-start | bytes 3145728 | tf_op jit(solution)/shard_map/all_to_all | solution.py:474
  22.3 3.6 %collective-permute-start.6 = (bf16[512,384]{1,0:T(8,128)(2,1)S(1)}, bf16[512,384]{1,0:T(8,128)(2,1)}, u32[]{:S(2)}, u32[]{:S(2)}) collective-permute-start(bf16[512,384]{1,0:T(8,128)(2,1)S(1)} %collective-permute-done.4), channel_id=1, source_target_pairs={{0,0},{1,2},{2,1},{3,3},{4,4},{5,6},{6,5},{7,7},{8,9},{9,11},{10,8... | collective-permute-start | bytes 1179656 | tf_op jit(solution)/shard_map/ppermute | solution.py:496
  26.0 4.3 %slice_bitcast_fusion = (bf16[3072,512]{1,0:T(8,128)(2,1)S(1)}, bf16[3072,512]{1,0:T(8,128)(2,1)S(1)}, bf16[3072,512]{1,0:T(8,128)(2,1)S(1)}) fusion(bf16[3072,3,512]{2,0,1:T(8,128)(2,1)} %param.18), kind=kLoop, calls=%fused_computation.5 | loop fusion | bytes 18874368 | tf_op jit(solution)/shard_map/squeeze | solution.py:505
  34.5 5.7 %text_qkv.1 = (bf16[3,512,512]{2,1,0:T(8,128)(2,1)S(1)}, f32[4,128,128]{2,1,0:T(8,128)S(1)}) custom-call(bf16[512,3072]{1,0:T(8,128)(2,1)S(1)} %fusion.2.rows, f32[512,1]{1,0:T(8,128)S(1)} %copy.17.keep, bf16[3072,512]{1,0:T(8,128)(2,1)S(1)} %get-tuple-element.87.wq, bf16[3072,512]{1,0:T(8,128)(2,1)S(1)} %get-tuple-element.86.wk, ...), custom_call_target="tpu_custom_call" | custom-call | flops 4831838208 | bytes 9437184 | tf_op jit(solution)/shard_map/text_qkv/pallas_call | solution.py:90
  42.1 6.8 %collective-permute-done.5 = bf16[64,1024]{1,0:T(8,128)(2,1)S(1)} collective-permute-done((bf16[64,1024]{1,0:T(8,128)(2,1)S(1)}, bf16[64,1024]{1,0:T(8,128)(2,1)S(1)}, u32[]{:S(2)}, u32[]{:S(2)}) %collective-permute-start.5) | collective-permute-done | bytes 131104 | tf_op jit(solution)/shard_map/ppermute | solution.py:486
  49.6 2.2 %collective-permute-start.8 = (bf16[128,1024]{1,0:T(8,128)(2,1)S(1)}, bf16[128,1024]{1,0:T(8,128)(2,1)S(1)}, u32[]{:S(2)}, u32[]{:S(2)}) collective-permute-start(bf16[128,1024]{1,0:T(8,128)(2,1)S(1)} %pad_maximum_fusion.refs_0_), channel_id=1, source_target_pairs={{0,1},{1,0},{2,3},{3,2},{4,5},{5,4},{6,7},{7,6},{8,9},{9,8},{10,11... | collective-permute-start | bytes 786440 | tf_op jit(solution)/shard_map/ppermute | solution.py:519
  51.9 2.6 %collective-permute-done.10.refs_1_ = bf16[768,384]{1,0:T(8,128)(2,1)S(1)} collective-permute-done((bf16[768,384]{1,0:T(8,128)(2,1)S(1)}, bf16[768,384]{1,0:T(8,128)(2,1)S(1)}, u32[]{:S(2)}, u32[]{:S(2)}) %collective-permute-start.10) | collective-permute-done | bytes 589856 | tf_op jit(solution)/shard_map/ppermute | solution.py:502
  55.3 4.6 %collective-permute-done.7.refs_1_ = bf16[128,1024]{1,0:T(8,128)(2,1)S(1)} collective-permute-done((bf16[128,1024]{1,0:T(8,128)(2,1)S(1)}, bf16[128,1024]{1,0:T(8,128)(2,1)S(1)}, u32[]{:S(2)}, u32[]{:S(2)}) %collective-permute-start.7) | collective-permute-done | bytes 262176 | tf_op jit(solution)/shard_map/ppermute | solution.py:518
  62.3 6.0 %projector.1 = (bf16[512,384]{1,0:T(8,128)(2,1)}, bf16[512,384]{1,0:T(8,128)(2,1)}) custom-call(s32[7]{0:T(128)} %stack.20.meta, bf16[128,1024]{1,0:T(8,128)(2,1)} %copy-done.20, bf16[128,1024]{1,0:T(8,128)(2,1)} %copy-done.22, bf16[128,1024]{1,0:T(8,128)(2,1)} %copy-done.23, bf16[128,1024]{1,0:T(8,128)(2,1)} %copy-done.24, bf16[1024,768]{1,0:T(8,128)(2,1)} %bitcast.22, ...), custom_call_target="tpu_custom_call" | custom-call | flops 1409286144 | bytes 5000000 | tf_op jit(solution)/shard_map/projector/pallas_call | solution.py:147
  72.7 5.2 %all-to-all-start.1 = ((bf16[32,16,384]{2,1,0:T(8,128)(2,1)}), bf16[32,16,384]{2,1,0:T(8,128)(2,1)S(1)}, u32[]{:S(2)}, u32[]{:S(2)}) async-start(bf16[32,16,384]{2,1,0:T(8,128)(2,1)} %bitcast.11), calls=%async_computation.1 | async-start | bytes 786432 | tf_op jit(solution)/shard_map/all_to_all | solution.py:546
  80.6 2.2 %collective-permute-start.12 = (bf16[512,384]{1,0:T(8,128)(2,1)}, bf16[512,384]{1,0:T(8,128)(2,1)}, u32[]{:S(2)}, u32[]{:S(2)}) collective-permute-start(bf16[512,384]{1,0:T(8,128)(2,1)} %collective-permute-done.6.refs_0_), channel_id=1, source_target_pairs={{0,16},{4,20},{8,24},{12,28},{16,0},{20,4},{24,8},{28,12},{1,17},{... | collective-permute-start | bytes 1179656 | tf_op jit(solution)/shard_map/ppermute | solution.py:532
  82.7 7.9 %all-to-all-done.1.refs_0_ = bf16[32,16,384]{2,1,0:T(8,128)(2,1)S(1)} async-done(((bf16[32,16,384]{2,1,0:T(8,128)(2,1)}), bf16[32,16,384]{2,1,0:T(8,128)(2,1)S(1)}, u32[]{:S(2)}, u32[]{:S(2)}) %all-to-all-start.1) | async-done | bytes 393248 | tf_op jit(solution)/shard_map/all_to_all | solution.py:546
  93.2 7.2 %all_gather.3.x = bf16[64,3072]{1,0:T(8,128)(2,1)} all-gather(bf16[16,3072]{1,0:T(8,128)(2,1)S(1)} %image_norm.1), channel_id=1, replica_groups=mesh['ctx'=8,'head'=4] {'head'}, dimensions={0}, use_global_device_ids=true | all-gather | bytes 491520 | tf_op jit(solution)/shard_map/all_gather | solution.py:559
  100.5 5.9 %image_qkv.1 = (bf16[3,64,512]{2,1,0:T(8,128)(2,1)}, bf16[4,128,128]{2,1,0:T(8,128)(2,1)}) custom-call(bf16[64,3072]{1,0:T(8,128)(2,1)} %all_gather.3.x, bf16[3072,512]{1,0:T(8,128)(2,1)} %copy-done.2, bf16[3072,512]{1,0:T(8,128)(2,1)} %copy-done.1, bf16[3072,512]{1,0:T(8,128)(2,1)} %copy-done, f32[4,128,128]{2,1,0:T(8,128)} %copy-done.7), custom_call_target="tpu_custom_call" | custom-call | flops 603979776 | bytes 9437184 | tf_op jit(solution)/shard_map/image_qkv/pallas_call | solution.py:283
  106.5 3.7 %all-to-all-start.2 = ((bf16[8,64,128]{2,1,0:T(8,128)(2,1)}), bf16[8,64,128]{2,1,0:T(8,128)(2,1)S(1)}, u32[]{:S(2)}, u32[]{:S(2)}) async-start(bf16[8,64,128]{2,1,0:T(8,128)(2,1)} %bitcast.23), calls=%async_computation.2 | async-start | bytes 262144 | tf_op jit(solution)/shard_map/all_to_all | solution.py:565
  112.8 3.8 %all-to-all-done.2 = bf16[8,64,128]{2,1,0:T(8,128)(2,1)S(1)} async-done(((bf16[8,64,128]{2,1,0:T(8,128)(2,1)}), bf16[8,64,128]{2,1,0:T(8,128)(2,1)S(1)}, u32[]{:S(2)}, u32[]{:S(2)}) %all-to-all-start.2) | async-done | bytes 131104 | tf_op jit(solution)/shard_map/all_to_all | solution.py:565
  117.3 3.4 %all-to-all-start.3 = ((bf16[8,64,128]{2,1,0:T(8,128)(2,1)}), bf16[8,64,128]{2,1,0:T(8,128)(2,1)S(1)}, u32[]{:S(2)}, u32[]{:S(2)}) async-start(bf16[8,64,128]{2,1,0:T(8,128)(2,1)} %fusion.3), calls=%async_computation.3 | async-start | bytes 262144 | tf_op jit(solution)/shard_map/all_to_all | solution.py:568
  123.0 2.1 %intra_shard.1 = (bf16[512,512]{1,0:T(8,128)(2,1)S(1)}, f32[512,512]{1,0:T(8,128)S(1)}) custom-call(bf16[3,512,512]{2,1,0:T(8,128)(2,1)S(1)} %copy-done.16, bf16[3,64,512]{2,1,0:T(8,128)(2,1)S(1)} %copy-done.14, bf16[512,64]{1,0:T(8,128)(2,1)S(1)} %get-tuple-element.71.put), custom_call_target="tpu_custom_call" | custom-call | flops 20000000000 | bytes 40000000 | tf_op jit(solution)/shard_map/intra_shard/pallas_call | solution.py:342
  127.4 3.8 %collective-permute-start.19 = (bf16[512,512]{1,0:T(8,128)(2,1)S(1)}, bf16[512,512]{1,0:T(8,128)(2,1)S(1)}, u32[]{:S(2)}, u32[]{:S(2)}) collective-permute-start(bf16[512,512]{1,0:T(8,128)(2,1)S(1)} %finish.1.refs_0_), channel_id=1, source_target_pairs={{0,1},{1,0},{2,3},{3,2},{4,5},{5,4},{6,7},{7,6},{8,9},{9,8},{10,11... | collective-permute-start | bytes 1572872 | tf_op jit(solution)/shard_map/ppermute | solution.py:576
  133.1 9.8 %collective-permute-done.15.refs_6_ = bf16[512,384]{1,0:T(8,128)(2,1)S(1)} collective-permute-done((bf16[512,384]{1,0:T(8,128)(2,1)}, bf16[512,384]{1,0:T(8,128)(2,1)S(1)}, u32[]{:S(2)}, u32[]{:S(2)}) %collective-permute-start.15) | collective-permute-done | bytes 393248 | tf_op jit(solution)/shard_map/ppermute | solution.py:532
  145.5 2.0 %mix_load.1.refs_2_ = bf16[8,512,384]{2,1,0:T(8,128)(2,1)S(1)} custom-call(s32[7]{0:T(128)S(1)} %copy-done.12, bf16[512,384]{1,0:T(8,128)(2,1)} %collective-permute-done.6.refs_0_, bf16[512,384]{1,0:T(8,128)(2,1)} %collective-permute-done.13.refs_1_, bf16[512,384]{1,0:T(8,128)(2,1)} %collective-permute-done.14.refs_2_, ...), custom_call_target="tpu_custom_call" | custom-call | bytes 6291456 | tf_op jit(solution)/shard_map/mix_load/pallas_call | solution.py:375
  148.8 2.1 %mix_part.3 = bf16[512,768]{1,0:T(8,128)(2,1)} custom-call(bf16[512,512]{1,0:T(8,128)(2,1)S(1)} %collective-permute-done.20.refs_0_, bf16[512,512]{1,0:T(8,128)(2,1)S(1)} %collective-permute-done.21.refs_1_, bf16[8,512,384]{2,1,0:T(8,128)(2,1)S(1)} %mix_load.1.refs_2_, f32[512,768]{1,0:T(8,128)S(1)} %mix_part.2.refs_3_), custom_call_target="tpu_custom_call" | custom-call | flops 805306368 | bytes 5000000 | tf_op jit(solution)/shard_map/mix_part/pallas_call | solution.py:402
  (116 shorter events, 43.9 us)
Async XLA Ops:
  0.0 10.6 %collective-permute-start = (bf16[64,1024]{1,0:T(8,128)(2,1)}, bf16[64,1024]{1,0:T(8,128)(2,1)S(1)}, u32[]{:S(2)}, u32[]{:S(2)}) collective-permute-start(bf16[64,1024]{1,0:T(8,128)(2,1)} %refs_0_.1), channel_id=1, source_target_pairs={{0,2},{1,3},{2,0},{3,1},{4,6},{5,7},{6,4},{7,5},{8,10},{9,11},{10,... | collective-permute-start | bytes 393224 | tf_op jit(solution)/shard_map/ppermute | solution.py:462
  2.0 11.1 %collective-permute-start.1 = (bf16[64,1024]{1,0:T(8,128)(2,1)}, bf16[64,1024]{1,0:T(8,128)(2,1)S(1)}, u32[]{:S(2)}, u32[]{:S(2)}) collective-permute-start(bf16[64,1024]{1,0:T(8,128)(2,1)} %refs_0_.1), channel_id=1, source_target_pairs={{0,1},{1,0},{2,3},{3,2},{4,5},{5,4},{6,7},{7,6},{8,9},{9,8},{10,11... | collective-permute-start | bytes 393224 | tf_op jit(solution)/shard_map/ppermute | solution.py:462
  3.0 17.8 %collective-permute-start.4 = (bf16[512,384]{1,0:T(8,128)(2,1)}, bf16[512,384]{1,0:T(8,128)(2,1)S(1)}, u32[]{:S(2)}, u32[]{:S(2)}) collective-permute-start(bf16[512,384]{1,0:T(8,128)(2,1)} %param.20), channel_id=1, source_target_pairs={{0,0},{1,17},{2,10},{3,27},{4,4},{5,21},{6,14},{7,31},{8,8},{9,25}... | collective-permute-start | bytes 1179656 | tf_op jit(solution)/shard_map/ppermute | solution.py:450
  10.6 2.5 %collective-permute-start.2 = (bf16[64,1024]{1,0:T(8,128)(2,1)S(1)}, bf16[64,1024]{1,0:T(8,128)(2,1)S(1)}, u32[]{:S(2)}, u32[]{:S(2)}) collective-permute-start(bf16[64,1024]{1,0:T(8,128)(2,1)S(1)} %collective-permute-done.refs_1_), channel_id=1, source_target_pairs={{0,1},{1,0},{2,3},{3,2},{4,5},{5,4},{6,7},{7,6},{8,9},{9,8},{10,11... | collective-permute-start | bytes 393224 | tf_op jit(solution)/shard_map/ppermute | solution.py:462
  14.3 6.4 %collective-permute-start.3 = (bf16[32,1024]{1,0:T(8,128)(2,1)S(1)}, bf16[32,1024]{1,0:T(8,128)(2,1)S(1)}, u32[]{:S(2)}, u32[]{:S(2)}) collective-permute-start(bf16[32,1024]{1,0:T(8,128)(2,1)S(1)} %pick_rows.1), channel_id=1, source_target_pairs={{0,16},{4,20},{8,24},{12,28},{16,0},{20,4},{24,8},{28,12},{1,17},{... | collective-permute-start | bytes 196616 | tf_op jit(solution)/shard_map/ppermute | solution.py:486
  15.2 45.1 %all-to-all-start = ((bf16[8,128,768]{2,1,0:T(8,128)(2,1)}), bf16[8,128,768]{2,1,0:T(8,128)(2,1)S(1)}, u32[]{:S(2)}, u32[]{:S(2)}) async-start(bf16[8,128,768]{2,1,0:T(8,128)(2,1)} %spread_units.1), calls=%async_computation | async-start | bytes 3145728 | tf_op jit(solution)/shard_map/all_to_all | solution.py:474
  20.8 28.1 %collective-permute-start.5 = (bf16[64,1024]{1,0:T(8,128)(2,1)S(1)}, bf16[64,1024]{1,0:T(8,128)(2,1)S(1)}, u32[]{:S(2)}, u32[]{:S(2)}) collective-permute-start(bf16[64,1024]{1,0:T(8,128)(2,1)S(1)} %pad_maximum_fusion.1), channel_id=1, source_target_pairs={{0,8},{4,12},{8,0},{12,4},{16,24},{20,28},{24,16},{28,20},{1,9},{5... | collective-permute-start | bytes 393224 | tf_op jit(solution)/shard_map/ppermute | solution.py:486
  22.3 26.7 %collective-permute-start.6 = (bf16[512,384]{1,0:T(8,128)(2,1)S(1)}, bf16[512,384]{1,0:T(8,128)(2,1)}, u32[]{:S(2)}, u32[]{:S(2)}) collective-permute-start(bf16[512,384]{1,0:T(8,128)(2,1)S(1)} %collective-permute-done.4), channel_id=1, source_target_pairs={{0,0},{1,2},{2,1},{3,3},{4,4},{5,6},{6,5},{7,7},{8,9},{9,11},{10,8... | collective-permute-start | bytes 1179656 | tf_op jit(solution)/shard_map/ppermute | solution.py:496
  31.4 23.0 %collective-permute-start.10 = (bf16[768,384]{1,0:T(8,128)(2,1)S(1)}, bf16[768,384]{1,0:T(8,128)(2,1)S(1)}, u32[]{:S(2)}, u32[]{:S(2)}) collective-permute-start(bf16[768,384]{1,0:T(8,128)(2,1)S(1)} %get-tuple-element.88), channel_id=1, source_target_pairs={{0,4},{4,0},{8,12},{12,8},{16,20},{20,16},{24,28},{28,24},{1,5},{5... | collective-permute-start | bytes 1769480 | tf_op jit(solution)/shard_map/ppermute | solution.py:502
  48.9 10.9 %collective-permute-start.7 = (bf16[128,1024]{1,0:T(8,128)(2,1)S(1)}, bf16[128,1024]{1,0:T(8,128)(2,1)S(1)}, u32[]{:S(2)}, u32[]{:S(2)}) collective-permute-start(bf16[128,1024]{1,0:T(8,128)(2,1)S(1)} %pad_maximum_fusion.refs_0_), channel_id=1, source_target_pairs={{0,4},{4,0},{8,12},{12,8},{16,20},{20,16},{24,28},{28,24},{1,5},{5... | collective-permute-start | bytes 786440 | tf_op jit(solution)/shard_map/ppermute | solution.py:518
  49.6 11.9 %collective-permute-start.8 = (bf16[128,1024]{1,0:T(8,128)(2,1)S(1)}, bf16[128,1024]{1,0:T(8,128)(2,1)S(1)}, u32[]{:S(2)}, u32[]{:S(2)}) collective-permute-start(bf16[128,1024]{1,0:T(8,128)(2,1)S(1)} %pad_maximum_fusion.refs_0_), channel_id=1, source_target_pairs={{0,1},{1,0},{2,3},{3,2},{4,5},{5,4},{6,7},{7,6},{8,9},{9,8},{10,11... | collective-permute-start | bytes 786440 | tf_op jit(solution)/shard_map/ppermute | solution.py:519
  72.7 17.9 %all-to-all-start.1 = ((bf16[32,16,384]{2,1,0:T(8,128)(2,1)}), bf16[32,16,384]{2,1,0:T(8,128)(2,1)S(1)}, u32[]{:S(2)}, u32[]{:S(2)}) async-start(bf16[32,16,384]{2,1,0:T(8,128)(2,1)} %bitcast.11), calls=%async_computation.1 | async-start | bytes 786432 | tf_op jit(solution)/shard_map/all_to_all | solution.py:546
  77.9 28.5 %collective-permute-start.13 = (bf16[512,384]{1,0:T(8,128)(2,1)}, bf16[512,384]{1,0:T(8,128)(2,1)}, u32[]{:S(2)}, u32[]{:S(2)}) collective-permute-start(bf16[512,384]{1,0:T(8,128)(2,1)} %collective-permute-done.6.refs_0_), channel_id=1, source_target_pairs={{0,4},{4,0},{8,12},{12,8},{16,20},{20,16},{24,28},{28,24},{1,5},{5... | collective-permute-start | bytes 1179656 | tf_op jit(solution)/shard_map/ppermute | solution.py:532
  79.4 27.0 %collective-permute-start.14 = (bf16[512,384]{1,0:T(8,128)(2,1)}, bf16[512,384]{1,0:T(8,128)(2,1)}, u32[]{:S(2)}, u32[]{:S(2)}) collective-permute-start(bf16[512,384]{1,0:T(8,128)(2,1)} %collective-permute-done.6.refs_0_), channel_id=1, source_target_pairs={{0,8},{4,12},{8,0},{12,4},{16,24},{20,28},{24,16},{28,20},{1,9},{5... | collective-permute-start | bytes 1179656 | tf_op jit(solution)/shard_map/ppermute | solution.py:532
  80.6 25.9 %collective-permute-start.12 = (bf16[512,384]{1,0:T(8,128)(2,1)}, bf16[512,384]{1,0:T(8,128)(2,1)}, u32[]{:S(2)}, u32[]{:S(2)}) collective-permute-start(bf16[512,384]{1,0:T(8,128)(2,1)} %collective-permute-done.6.refs_0_), channel_id=1, source_target_pairs={{0,16},{4,20},{8,24},{12,28},{16,0},{20,4},{24,8},{28,12},{1,17},{... | collective-permute-start | bytes 1179656 | tf_op jit(solution)/shard_map/ppermute | solution.py:532
  106.5 10.1 %all-to-all-start.2 = ((bf16[8,64,128]{2,1,0:T(8,128)(2,1)}), bf16[8,64,128]{2,1,0:T(8,128)(2,1)S(1)}, u32[]{:S(2)}, u32[]{:S(2)}) async-start(bf16[8,64,128]{2,1,0:T(8,128)(2,1)} %bitcast.23), calls=%async_computation.2 | async-start | bytes 262144 | tf_op jit(solution)/shard_map/all_to_all | solution.py:565
  110.2 14.9 %collective-permute-start.16 = (bf16[512,384]{1,0:T(8,128)(2,1)}, bf16[512,384]{1,0:T(8,128)(2,1)S(1)}, u32[]{:S(2)}, u32[]{:S(2)}) collective-permute-start(bf16[512,384]{1,0:T(8,128)(2,1)} %collective-permute-done.12.refs_3_), channel_id=1, source_target_pairs={{0,4},{4,0},{8,12},{12,8},{16,20},{20,16},{24,28},{28,24},{1,5},{5... | collective-permute-start | bytes 1179656 | tf_op jit(solution)/shard_map/ppermute | solution.py:532
  111.6 13.4 %collective-permute-start.17 = (bf16[512,384]{1,0:T(8,128)(2,1)}, bf16[512,384]{1,0:T(8,128)(2,1)S(1)}, u32[]{:S(2)}, u32[]{:S(2)}) collective-permute-start(bf16[512,384]{1,0:T(8,128)(2,1)} %collective-permute-done.12.refs_3_), channel_id=1, source_target_pairs={{0,8},{4,12},{8,0},{12,4},{16,24},{20,28},{24,16},{28,20},{1,9},{5... | collective-permute-start | bytes 1179656 | tf_op jit(solution)/shard_map/ppermute | solution.py:532
  117.3 9.6 %all-to-all-start.3 = ((bf16[8,64,128]{2,1,0:T(8,128)(2,1)}), bf16[8,64,128]{2,1,0:T(8,128)(2,1)S(1)}, u32[]{:S(2)}, u32[]{:S(2)}) async-start(bf16[8,64,128]{2,1,0:T(8,128)(2,1)} %fusion.3), calls=%async_computation.3 | async-start | bytes 262144 | tf_op jit(solution)/shard_map/all_to_all | solution.py:568
  127.4 15.5 %collective-permute-start.19 = (bf16[512,512]{1,0:T(8,128)(2,1)S(1)}, bf16[512,512]{1,0:T(8,128)(2,1)S(1)}, u32[]{:S(2)}, u32[]{:S(2)}) collective-permute-start(bf16[512,512]{1,0:T(8,128)(2,1)S(1)} %finish.1.refs_0_), channel_id=1, source_target_pairs={{0,1},{1,0},{2,3},{3,2},{4,5},{5,4},{6,7},{7,6},{8,9},{9,8},{10,11... | collective-permute-start | bytes 1572872 | tf_op jit(solution)/shard_map/ppermute | solution.py:576
  131.2 13.5 %collective-permute-start.20 = (bf16[512,512]{1,0:T(8,128)(2,1)S(1)}, bf16[512,512]{1,0:T(8,128)(2,1)S(1)}, u32[]{:S(2)}, u32[]{:S(2)}) collective-permute-start(bf16[512,512]{1,0:T(8,128)(2,1)S(1)} %finish.1.refs_0_), channel_id=1, source_target_pairs={{0,2},{1,3},{2,0},{3,1},{4,6},{5,7},{6,4},{7,5},{8,10},{9,11},{10,... | collective-permute-start | bytes 1572872 | tf_op jit(solution)/shard_map/ppermute | solution.py:582
  132.4 10.6 %collective-permute-start.15 = (bf16[512,384]{1,0:T(8,128)(2,1)}, bf16[512,384]{1,0:T(8,128)(2,1)S(1)}, u32[]{:S(2)}, u32[]{:S(2)}) collective-permute-start(bf16[512,384]{1,0:T(8,128)(2,1)} %collective-permute-done.13.refs_1_), channel_id=1, source_target_pairs={{0,8},{4,12},{8,0},{12,4},{16,24},{20,28},{24,16},{28,20},{1,9},{5... | collective-permute-start | bytes 1179656 | tf_op jit(solution)/shard_map/ppermute | solution.py:532
  132.4 10.6 %collective-permute-start.18 = (bf16[512,384]{1,0:T(8,128)(2,1)S(1)}, bf16[512,384]{1,0:T(8,128)(2,1)S(1)}, u32[]{:S(2)}, u32[]{:S(2)}) collective-permute-start(bf16[512,384]{1,0:T(8,128)(2,1)S(1)} %collective-permute-done.17.refs_5_), channel_id=1, source_target_pairs={{0,4},{4,0},{8,12},{12,8},{16,20},{20,16},{24,28},{28,24},{1,5},{5... | collective-permute-start | bytes 1179656 | tf_op jit(solution)/shard_map/ppermute | solution.py:532
  144.7 4.1 %collective-permute-start.21 = (bf16[512,512]{1,0:T(8,128)(2,1)S(1)}, bf16[512,512]{1,0:T(8,128)(2,1)S(1)}, u32[]{:S(2)}, u32[]{:S(2)}) collective-permute-start(bf16[512,512]{1,0:T(8,128)(2,1)S(1)} %collective-permute-done.20.refs_0_), channel_id=1, source_target_pairs={{0,1},{1,0},{2,3},{3,2},{4,5},{5,4},{6,7},{7,6},{8,9},{9,8},{10,11... | collective-permute-start | bytes 1572872 | tf_op jit(solution)/shard_map/ppermute | solution.py:591
  (27 other events, 91.9 us)

commit v7 on v6

--- a/solution.py
+++ b/solution.py
@@ -50,11 +50,16 @@
     )(*arrays)
 
 
-def spread_kernel(span, x, out):
+def spread_kernel(span, x, out, sems):
     part = out.shape[2]
+    copies = []
     for c in range(out.shape[0]):
         at = c % span * part
-        out[c] = x[:, at : at + part]
+        copies.append(pltpu.make_async_copy(x.at[:, at : at + part], out.at[c], sems.at[c]))
+    for copy in copies:
+        copy.start()
+    for copy in copies:
+        copy.wait()
 
 
 def spread_units(x, n_ctx, span):
@@ -62,8 +67,9 @@
     return pl.pallas_call(
         functools.partial(spread_kernel, span),
         out_shape=jax.ShapeDtypeStruct((n_ctx, rows, units // span), x.dtype),
-        in_specs=[VMEM],
-        out_specs=VMEM,
+        in_specs=[HBM],
+        out_specs=HBM,
+        scratch_shapes=[pltpu.SemaphoreType.DMA((n_ctx,))],
         compiler_params=PARAMS,
         cost_estimate=cost(0, 4 * x.size),
         name="spread_units",
@@ -249,7 +255,7 @@
     )(got, gain)
 
 
-def image_kernel(steps, x, wq, wk, wv, text_state, out, state, held, sems):
+def image_kernel(steps, x, wq, wk, wv, text_hbm, out, state, held, text_state, sems):
     rows = x[...]
     depth = x.shape[1] // steps
     order = ((1, wk), (2, wv), (0, wq))
@@ -261,6 +267,8 @@
     for n, w in order:
         for i in range(steps):
             copy(n, w, i).start()
+    text = pltpu.make_async_copy(text_hbm, text_state, sems.at[3 * steps])
+    text.start()
     for n, w in order:
         total = 0.0
         for i in range(steps):
@@ -268,6 +276,7 @@
             at = slice(i * depth, (i + 1) * depth)
             total = total + dot(rows[:, at], held[n, at, :])
         out[n] = silu(total).astype(BF16)
+    text.wait()
     for h in range(state.shape[0]):
         cols = slice(h * HEAD_DIM, (h + 1) * HEAD_DIM)
         outer = lax.dot_general(
@@ -286,11 +295,12 @@
             jax.ShapeDtypeStruct((3, rows, cols), BF16),
             jax.ShapeDtypeStruct(text_state.shape, BF16),
         ),
-        in_specs=[VMEM] + [HBM] * 3 + [VMEM],
+        in_specs=[VMEM] + [HBM] * 4,
         out_specs=(VMEM, VMEM),
         scratch_shapes=[
             pltpu.VMEM((3, width, cols), BF16),
-            pltpu.SemaphoreType.DMA((3 * steps,)),
+            pltpu.VMEM(text_state.shape, F32),
+            pltpu.SemaphoreType.DMA((3 * steps + 1,)),
         ],
         compiler_params=FETCHING,
         cost_estimate=cost(6 * rows * width * cols, 6 * width * cols, 3 * rows * cols),

time: 152 us -> 152 us (level)
  transfers between devices with their start and end apart: 26 -> 26, of which waited for: 10 -> 9; matrix products, arithmetic and copies ran while one was open for 8% -> 8% of each run, Pallas kernels for 12% -> 12%
where the time goes in v7:
time: 152 us; the launch traced here: 151 us
  starting transfers between devices  49.1 us (32%)
  waiting for transfers between devices  40.8 us (27%)
  Pallas kernels  28.7 us (19%)
  local copies, waits for them, and re-layouts  18.7 us (12%)
  blocking collectives  7.24 us (5%)
  other arithmetic  5.94 us (4%)
    unnamed x50, local copies, waits for them, and re-layouts  12.4 us
    ppermute x7, waiting for transfers between devices, mix_start(): mix_blocks[offset] = along('ctx', n_ctx, mask)(mix_blocks[offset ^ mask])  9.84 us
    ppermute x7, starting transfers between devices, mix_start(): mix_blocks[offset] = along('ctx', n_ctx, mask)(mix_blocks[offset ^ mask])  8.19 us
    all_to_all x1, waiting for transfers between devices, on_device(): lax.all_to_all(ordered.reshape(n_ctx * n_head, part_rows, span // 2 * out...  7.89 us
    all_gather x1, blocking collectives, on_device(): image_rows = lax.all_gather(img_part, 'head', axis=0, tiled=True)  7.24 us
    ppermute x2, waiting for transfers between devices, spread(): return jnp.concatenate([x, along('ctx', n_ctx, mask)(x)])  6.83 us
    pallas_call x1, Pallas kernels, projector(): pl.pallas_call(functools.partial(projector_kernel, min(rows, 256), span,...  6.01 us
    pallas_call x1, Pallas kernels, image_qkv(): pl.pallas_call(functools.partial(image_kernel, steps), out_shape=(jax.Sha...  5.95 us
  transfers between devices with their start and end apart: 26, of which 9 were waited for; matrix products, arithmetic and copies ran while one was open for 8% of the time, Pallas kernels for 12%

profile of v7, /device:TPU:1, one launch (start us, length us, event | category | flops | bytes accessed | tf_op | source)
XLA Modules:
  0.0 150.9 jit_solution(8940128196185354890)
XLA Ops:
  0.0 2.0 %collective-permute-start = (bf16[64,1024]{1,0:T(8,128)(2,1)}, bf16[64,1024]{1,0:T(8,128)(2,1)S(1)}, u32[]{:S(2)}, u32[]{:S(2)}) collective-permute-start(bf16[64,1024]{1,0:T(8,128)(2,1)} %refs_0_.1), channel_id=1, source_target_pairs={{0,2},{1,3},{2,0},{3,1},{4,6},{5,7},{6,4},{7,5},{8,10},{9,11},{10,... | collective-permute-start | bytes 393224 | tf_op jit(solution)/shard_map/ppermute | solution.py:472
  3.0 4.2 %collective-permute-start.4 = (bf16[512,384]{1,0:T(8,128)(2,1)}, bf16[512,384]{1,0:T(8,128)(2,1)S(1)}, u32[]{:S(2)}, u32[]{:S(2)}) collective-permute-start(bf16[512,384]{1,0:T(8,128)(2,1)} %param.20), channel_id=1, source_target_pairs={{0,0},{1,17},{2,10},{3,27},{4,4},{5,21},{6,14},{7,31},{8,8},{9,25}... | collective-permute-start | bytes 1179656 | tf_op jit(solution)/shard_map/ppermute | solution.py:460
  15.2 5.6 %all-to-all-start = ((bf16[8,128,768]{2,1,0:T(8,128)(2,1)}), bf16[8,128,768]{2,1,0:T(8,128)(2,1)S(1)}, u32[]{:S(2)}, u32[]{:S(2)}) async-start(bf16[8,128,768]{2,1,0:T(8,128)(2,1)} %spread_units.1), calls=%async_computation | async-start | bytes 3145728 | tf_op jit(solution)/shard_map/all_to_all | solution.py:484
  22.3 3.6 %collective-permute-start.6 = (bf16[512,384]{1,0:T(8,128)(2,1)S(1)}, bf16[512,384]{1,0:T(8,128)(2,1)}, u32[]{:S(2)}, u32[]{:S(2)}) collective-permute-start(bf16[512,384]{1,0:T(8,128)(2,1)S(1)} %collective-permute-done.4), channel_id=1, source_target_pairs={{0,0},{1,2},{2,1},{3,3},{4,4},{5,6},{6,5},{7,7},{8,9},{9,11},{10,8... | collective-permute-start | bytes 1179656 | tf_op jit(solution)/shard_map/ppermute | solution.py:506
  25.9 4.3 %slice_bitcast_fusion = (bf16[3072,512]{1,0:T(8,128)(2,1)S(1)}, bf16[3072,512]{1,0:T(8,128)(2,1)S(1)}, bf16[3072,512]{1,0:T(8,128)(2,1)S(1)}) fusion(bf16[3072,3,512]{2,0,1:T(8,128)(2,1)} %param.18), kind=kLoop, calls=%fused_computation.5 | loop fusion | bytes 18874368 | tf_op jit(solution)/shard_map/squeeze | solution.py:515
  34.5 5.7 %text_qkv.1 = (bf16[3,512,512]{2,1,0:T(8,128)(2,1)S(1)}, f32[4,128,128]{2,1,0:T(8,128)S(1)}) custom-call(bf16[512,3072]{1,0:T(8,128)(2,1)S(1)} %fusion.2.rows, f32[512,1]{1,0:T(8,128)S(1)} %copy.17.keep, bf16[3072,512]{1,0:T(8,128)(2,1)S(1)} %get-tuple-element.87.wq, bf16[3072,512]{1,0:T(8,128)(2,1)S(1)} %get-tuple-element.86.wk, ...), custom_call_target="tpu_custom_call" | custom-call | flops 4831838208 | bytes 9437184 | tf_op jit(solution)/shard_map/text_qkv/pallas_call | solution.py:96
  42.1 6.8 %collective-permute-done.5 = bf16[64,1024]{1,0:T(8,128)(2,1)S(1)} collective-permute-done((bf16[64,1024]{1,0:T(8,128)(2,1)S(1)}, bf16[64,1024]{1,0:T(8,128)(2,1)S(1)}, u32[]{:S(2)}, u32[]{:S(2)}) %collective-permute-start.5) | collective-permute-done | bytes 131104 | tf_op jit(solution)/shard_map/ppermute | solution.py:496
  49.6 2.2 %collective-permute-start.8 = (bf16[128,1024]{1,0:T(8,128)(2,1)S(1)}, bf16[128,1024]{1,0:T(8,128)(2,1)S(1)}, u32[]{:S(2)}, u32[]{:S(2)}) collective-permute-start(bf16[128,1024]{1,0:T(8,128)(2,1)S(1)} %pad_maximum_fusion.refs_0_), channel_id=1, source_target_pairs={{0,1},{1,0},{2,3},{3,2},{4,5},{5,4},{6,7},{7,6},{8,9},{9,8},{10,11... | collective-permute-start | bytes 786440 | tf_op jit(solution)/shard_map/ppermute | solution.py:529
  51.8 2.6 %collective-permute-done.10.refs_1_ = bf16[768,384]{1,0:T(8,128)(2,1)S(1)} collective-permute-done((bf16[768,384]{1,0:T(8,128)(2,1)S(1)}, bf16[768,384]{1,0:T(8,128)(2,1)S(1)}, u32[]{:S(2)}, u32[]{:S(2)}) %collective-permute-start.10) | collective-permute-done | bytes 589856 | tf_op jit(solution)/shard_map/ppermute | solution.py:512
  55.2 4.6 %collective-permute-done.7.refs_1_ = bf16[128,1024]{1,0:T(8,128)(2,1)S(1)} collective-permute-done((bf16[128,1024]{1,0:T(8,128)(2,1)S(1)}, bf16[128,1024]{1,0:T(8,128)(2,1)S(1)}, u32[]{:S(2)}, u32[]{:S(2)}) %collective-permute-start.7) | collective-permute-done | bytes 262176 | tf_op jit(solution)/shard_map/ppermute | solution.py:528
  62.3 6.0 %projector.1 = (bf16[512,384]{1,0:T(8,128)(2,1)}, bf16[512,384]{1,0:T(8,128)(2,1)}) custom-call(s32[7]{0:T(128)} %stack.20.meta, bf16[128,1024]{1,0:T(8,128)(2,1)} %copy-done.20, bf16[128,1024]{1,0:T(8,128)(2,1)} %copy-done.22, bf16[128,1024]{1,0:T(8,128)(2,1)} %copy-done.23, bf16[128,1024]{1,0:T(8,128)(2,1)} %copy-done.24, bf16[1024,768]{1,0:T(8,128)(2,1)} %bitcast.22, ...), custom_call_target="tpu_custom_call" | custom-call | flops 1409286144 | bytes 5000000 | tf_op jit(solution)/shard_map/projector/pallas_call | solution.py:153
  72.7 5.2 %all-to-all-start.1 = ((bf16[32,16,384]{2,1,0:T(8,128)(2,1)}), bf16[32,16,384]{2,1,0:T(8,128)(2,1)S(1)}, u32[]{:S(2)}, u32[]{:S(2)}) async-start(bf16[32,16,384]{2,1,0:T(8,128)(2,1)} %bitcast.11), calls=%async_computation.1 | async-start | bytes 786432 | tf_op jit(solution)/shard_map/all_to_all | solution.py:556
  80.5 2.2 %collective-permute-start.12 = (bf16[512,384]{1,0:T(8,128)(2,1)}, bf16[512,384]{1,0:T(8,128)(2,1)}, u32[]{:S(2)}, u32[]{:S(2)}) collective-permute-start(bf16[512,384]{1,0:T(8,128)(2,1)} %collective-permute-done.6.refs_0_), channel_id=1, source_target_pairs={{0,16},{4,20},{8,24},{12,28},{16,0},{20,4},{24,8},{28,12},{1,17},{... | collective-permute-start | bytes 1179656 | tf_op jit(solution)/shard_map/ppermute | solution.py:542
  82.7 7.9 %all-to-all-done.1.refs_0_ = bf16[32,16,384]{2,1,0:T(8,128)(2,1)S(1)} async-done(((bf16[32,16,384]{2,1,0:T(8,128)(2,1)}), bf16[32,16,384]{2,1,0:T(8,128)(2,1)S(1)}, u32[]{:S(2)}, u32[]{:S(2)}) %all-to-all-start.1) | async-done | bytes 393248 | tf_op jit(solution)/shard_map/all_to_all | solution.py:556
  93.2 7.2 %all_gather.3.x = bf16[64,3072]{1,0:T(8,128)(2,1)} all-gather(bf16[16,3072]{1,0:T(8,128)(2,1)S(1)} %image_norm.1), channel_id=1, replica_groups=mesh['ctx'=8,'head'=4] {'head'}, dimensions={0}, use_global_device_ids=true | all-gather | bytes 491520 | tf_op jit(solution)/shard_map/all_gather | solution.py:569
  100.5 6.0 %image_qkv.1 = (bf16[3,64,512]{2,1,0:T(8,128)(2,1)}, bf16[4,128,128]{2,1,0:T(8,128)(2,1)}) custom-call(bf16[64,3072]{1,0:T(8,128)(2,1)} %all_gather.3.x, bf16[3072,512]{1,0:T(8,128)(2,1)} %copy-done.2, bf16[3072,512]{1,0:T(8,128)(2,1)} %copy-done.1, bf16[3072,512]{1,0:T(8,128)(2,1)} %copy-done, f32[4,128,128]{2,1,0:T(8,128)} %copy-done.7), custom_call_target="tpu_custom_call" | custom-call | flops 603979776 | bytes 9437184 | tf_op jit(solution)/shard_map/image_qkv/pallas_call | solution.py:292
  106.5 3.7 %all-to-all-start.2 = ((bf16[8,64,128]{2,1,0:T(8,128)(2,1)}), bf16[8,64,128]{2,1,0:T(8,128)(2,1)S(1)}, u32[]{:S(2)}, u32[]{:S(2)}) async-start(bf16[8,64,128]{2,1,0:T(8,128)(2,1)} %bitcast.23), calls=%async_computation.2 | async-start | bytes 262144 | tf_op jit(solution)/shard_map/all_to_all | solution.py:575
  112.8 3.8 %all-to-all-done.2 = bf16[8,64,128]{2,1,0:T(8,128)(2,1)S(1)} async-done(((bf16[8,64,128]{2,1,0:T(8,128)(2,1)}), bf16[8,64,128]{2,1,0:T(8,128)(2,1)S(1)}, u32[]{:S(2)}, u32[]{:S(2)}) %all-to-all-start.2) | async-done | bytes 131104 | tf_op jit(solution)/shard_map/all_to_all | solution.py:575
  117.2 3.4 %all-to-all-start.3 = ((bf16[8,64,128]{2,1,0:T(8,128)(2,1)}), bf16[8,64,128]{2,1,0:T(8,128)(2,1)S(1)}, u32[]{:S(2)}, u32[]{:S(2)}) async-start(bf16[8,64,128]{2,1,0:T(8,128)(2,1)} %fusion.3), calls=%async_computation.3 | async-start | bytes 262144 | tf_op jit(solution)/shard_map/all_to_all | solution.py:578
  123.0 2.1 %intra_shard.1 = (bf16[512,512]{1,0:T(8,128)(2,1)S(1)}, f32[512,512]{1,0:T(8,128)S(1)}) custom-call(bf16[3,512,512]{2,1,0:T(8,128)(2,1)S(1)} %copy-done.16, bf16[3,64,512]{2,1,0:T(8,128)(2,1)S(1)} %copy-done.14, bf16[512,64]{1,0:T(8,128)(2,1)S(1)} %get-tuple-element.71.put), custom_call_target="tpu_custom_call" | custom-call | flops 20000000000 | bytes 40000000 | tf_op jit(solution)/shard_map/intra_shard/pallas_call | solution.py:352
  127.4 3.8 %collective-permute-start.19 = (bf16[512,512]{1,0:T(8,128)(2,1)S(1)}, bf16[512,512]{1,0:T(8,128)(2,1)S(1)}, u32[]{:S(2)}, u32[]{:S(2)}) collective-permute-start(bf16[512,512]{1,0:T(8,128)(2,1)S(1)} %finish.1.refs_0_), channel_id=1, source_target_pairs={{0,1},{1,0},{2,3},{3,2},{4,5},{5,4},{6,7},{7,6},{8,9},{9,8},{10,11... | collective-permute-start | bytes 1572872 | tf_op jit(solution)/shard_map/ppermute | solution.py:586
  133.1 9.8 %collective-permute-done.15.refs_6_ = bf16[512,384]{1,0:T(8,128)(2,1)S(1)} collective-permute-done((bf16[512,384]{1,0:T(8,128)(2,1)}, bf16[512,384]{1,0:T(8,128)(2,1)S(1)}, u32[]{:S(2)}, u32[]{:S(2)}) %collective-permute-start.15) | collective-permute-done | bytes 393248 | tf_op jit(solution)/shard_map/ppermute | solution.py:542
  145.5 2.0 %mix_load.1.refs_2_ = bf16[8,512,384]{2,1,0:T(8,128)(2,1)S(1)} custom-call(s32[7]{0:T(128)S(1)} %copy-done.12, bf16[512,384]{1,0:T(8,128)(2,1)} %collective-permute-done.6.refs_0_, bf16[512,384]{1,0:T(8,128)(2,1)} %collective-permute-done.13.refs_1_, bf16[512,384]{1,0:T(8,128)(2,1)} %collective-permute-done.14.refs_2_, ...), custom_call_target="tpu_custom_call" | custom-call | bytes 6291456 | tf_op jit(solution)/shard_map/mix_load/pallas_call | solution.py:385
  148.8 2.1 %mix_part.3 = bf16[512,768]{1,0:T(8,128)(2,1)} custom-call(bf16[512,512]{1,0:T(8,128)(2,1)S(1)} %collective-permute-done.20.refs_0_, bf16[512,512]{1,0:T(8,128)(2,1)S(1)} %collective-permute-done.21.refs_1_, bf16[8,512,384]{2,1,0:T(8,128)(2,1)S(1)} %mix_load.1.refs_2_, f32[512,768]{1,0:T(8,128)S(1)} %mix_part.2.refs_3_), custom_call_target="tpu_custom_call" | custom-call | flops 805306368 | bytes 5000000 | tf_op jit(solution)/shard_map/mix_part/pallas_call | solution.py:412
  (116 shorter events, 43.8 us)
Async XLA Ops:
  0.0 10.6 %collective-permute-start = (bf16[64,1024]{1,0:T(8,128)(2,1)}, bf16[64,1024]{1,0:T(8,128)(2,1)S(1)}, u32[]{:S(2)}, u32[]{:S(2)}) collective-permute-start(bf16[64,1024]{1,0:T(8,128)(2,1)} %refs_0_.1), channel_id=1, source_target_pairs={{0,2},{1,3},{2,0},{3,1},{4,6},{5,7},{6,4},{7,5},{8,10},{9,11},{10,... | collective-permute-start | bytes 393224 | tf_op jit(solution)/shard_map/ppermute | solution.py:472
  2.0 11.0 %collective-permute-start.1 = (bf16[64,1024]{1,0:T(8,128)(2,1)}, bf16[64,1024]{1,0:T(8,128)(2,1)S(1)}, u32[]{:S(2)}, u32[]{:S(2)}) collective-permute-start(bf16[64,1024]{1,0:T(8,128)(2,1)} %refs_0_.1), channel_id=1, source_target_pairs={{0,1},{1,0},{2,3},{3,2},{4,5},{5,4},{6,7},{7,6},{8,9},{9,8},{10,11... | collective-permute-start | bytes 393224 | tf_op jit(solution)/shard_map/ppermute | solution.py:472
  3.0 17.8 %collective-permute-start.4 = (bf16[512,384]{1,0:T(8,128)(2,1)}, bf16[512,384]{1,0:T(8,128)(2,1)S(1)}, u32[]{:S(2)}, u32[]{:S(2)}) collective-permute-start(bf16[512,384]{1,0:T(8,128)(2,1)} %param.20), channel_id=1, source_target_pairs={{0,0},{1,17},{2,10},{3,27},{4,4},{5,21},{6,14},{7,31},{8,8},{9,25}... | collective-permute-start | bytes 1179656 | tf_op jit(solution)/shard_map/ppermute | solution.py:460
  10.6 2.5 %collective-permute-start.2 = (bf16[64,1024]{1,0:T(8,128)(2,1)S(1)}, bf16[64,1024]{1,0:T(8,128)(2,1)S(1)}, u32[]{:S(2)}, u32[]{:S(2)}) collective-permute-start(bf16[64,1024]{1,0:T(8,128)(2,1)S(1)} %collective-permute-done.refs_1_), channel_id=1, source_target_pairs={{0,1},{1,0},{2,3},{3,2},{4,5},{5,4},{6,7},{7,6},{8,9},{9,8},{10,11... | collective-permute-start | bytes 393224 | tf_op jit(solution)/shard_map/ppermute | solution.py:472
  14.3 6.4 %collective-permute-start.3 = (bf16[32,1024]{1,0:T(8,128)(2,1)S(1)}, bf16[32,1024]{1,0:T(8,128)(2,1)S(1)}, u32[]{:S(2)}, u32[]{:S(2)}) collective-permute-start(bf16[32,1024]{1,0:T(8,128)(2,1)S(1)} %pick_rows.1), channel_id=1, source_target_pairs={{0,16},{4,20},{8,24},{12,28},{16,0},{20,4},{24,8},{28,12},{1,17},{... | collective-permute-start | bytes 196616 | tf_op jit(solution)/shard_map/ppermute | solution.py:496
  15.2 45.1 %all-to-all-start = ((bf16[8,128,768]{2,1,0:T(8,128)(2,1)}), bf16[8,128,768]{2,1,0:T(8,128)(2,1)S(1)}, u32[]{:S(2)}, u32[]{:S(2)}) async-start(bf16[8,128,768]{2,1,0:T(8,128)(2,1)} %spread_units.1), calls=%async_computation | async-start | bytes 3145728 | tf_op jit(solution)/shard_map/all_to_all | solution.py:484
  20.8 28.1 %collective-permute-start.5 = (bf16[64,1024]{1,0:T(8,128)(2,1)S(1)}, bf16[64,1024]{1,0:T(8,128)(2,1)S(1)}, u32[]{:S(2)}, u32[]{:S(2)}) collective-permute-start(bf16[64,1024]{1,0:T(8,128)(2,1)S(1)} %pad_maximum_fusion.1), channel_id=1, source_target_pairs={{0,8},{4,12},{8,0},{12,4},{16,24},{20,28},{24,16},{28,20},{1,9},{5... | collective-permute-start | bytes 393224 | tf_op jit(solution)/shard_map/ppermute | solution.py:496
  22.3 26.7 %collective-permute-start.6 = (bf16[512,384]{1,0:T(8,128)(2,1)S(1)}, bf16[512,384]{1,0:T(8,128)(2,1)}, u32[]{:S(2)}, u32[]{:S(2)}) collective-permute-start(bf16[512,384]{1,0:T(8,128)(2,1)S(1)} %collective-permute-done.4), channel_id=1, source_target_pairs={{0,0},{1,2},{2,1},{3,3},{4,4},{5,6},{6,5},{7,7},{8,9},{9,11},{10,8... | collective-permute-start | bytes 1179656 | tf_op jit(solution)/shard_map/ppermute | solution.py:506
  31.4 23.0 %collective-permute-start.10 = (bf16[768,384]{1,0:T(8,128)(2,1)S(1)}, bf16[768,384]{1,0:T(8,128)(2,1)S(1)}, u32[]{:S(2)}, u32[]{:S(2)}) collective-permute-start(bf16[768,384]{1,0:T(8,128)(2,1)S(1)} %get-tuple-element.88), channel_id=1, source_target_pairs={{0,4},{4,0},{8,12},{12,8},{16,20},{20,16},{24,28},{28,24},{1,5},{5... | collective-permute-start | bytes 1769480 | tf_op jit(solution)/shard_map/ppermute | solution.py:512
  48.9 10.9 %collective-permute-start.7 = (bf16[128,1024]{1,0:T(8,128)(2,1)S(1)}, bf16[128,1024]{1,0:T(8,128)(2,1)S(1)}, u32[]{:S(2)}, u32[]{:S(2)}) collective-permute-start(bf16[128,1024]{1,0:T(8,128)(2,1)S(1)} %pad_maximum_fusion.refs_0_), channel_id=1, source_target_pairs={{0,4},{4,0},{8,12},{12,8},{16,20},{20,16},{24,28},{28,24},{1,5},{5... | collective-permute-start | bytes 786440 | tf_op jit(solution)/shard_map/ppermute | solution.py:528
  49.6 11.9 %collective-permute-start.8 = (bf16[128,1024]{1,0:T(8,128)(2,1)S(1)}, bf16[128,1024]{1,0:T(8,128)(2,1)S(1)}, u32[]{:S(2)}, u32[]{:S(2)}) collective-permute-start(bf16[128,1024]{1,0:T(8,128)(2,1)S(1)} %pad_maximum_fusion.refs_0_), channel_id=1, source_target_pairs={{0,1},{1,0},{2,3},{3,2},{4,5},{5,4},{6,7},{7,6},{8,9},{9,8},{10,11... | collective-permute-start | bytes 786440 | tf_op jit(solution)/shard_map/ppermute | solution.py:529
  72.7 17.9 %all-to-all-start.1 = ((bf16[32,16,384]{2,1,0:T(8,128)(2,1)}), bf16[32,16,384]{2,1,0:T(8,128)(2,1)S(1)}, u32[]{:S(2)}, u32[]{:S(2)}) async-start(bf16[32,16,384]{2,1,0:T(8,128)(2,1)} %bitcast.11), calls=%async_computation.1 | async-start | bytes 786432 | tf_op jit(solution)/shard_map/all_to_all | solution.py:556
  77.9 28.5 %collective-permute-start.13 = (bf16[512,384]{1,0:T(8,128)(2,1)}, bf16[512,384]{1,0:T(8,128)(2,1)}, u32[]{:S(2)}, u32[]{:S(2)}) collective-permute-start(bf16[512,384]{1,0:T(8,128)(2,1)} %collective-permute-done.6.refs_0_), channel_id=1, source_target_pairs={{0,4},{4,0},{8,12},{12,8},{16,20},{20,16},{24,28},{28,24},{1,5},{5... | collective-permute-start | bytes 1179656 | tf_op jit(solution)/shard_map/ppermute | solution.py:542
  79.4 27.1 %collective-permute-start.14 = (bf16[512,384]{1,0:T(8,128)(2,1)}, bf16[512,384]{1,0:T(8,128)(2,1)}, u32[]{:S(2)}, u32[]{:S(2)}) collective-permute-start(bf16[512,384]{1,0:T(8,128)(2,1)} %collective-permute-done.6.refs_0_), channel_id=1, source_target_pairs={{0,8},{4,12},{8,0},{12,4},{16,24},{20,28},{24,16},{28,20},{1,9},{5... | collective-permute-start | bytes 1179656 | tf_op jit(solution)/shard_map/ppermute | solution.py:542
  80.5 25.9 %collective-permute-start.12 = (bf16[512,384]{1,0:T(8,128)(2,1)}, bf16[512,384]{1,0:T(8,128)(2,1)}, u32[]{:S(2)}, u32[]{:S(2)}) collective-permute-start(bf16[512,384]{1,0:T(8,128)(2,1)} %collective-permute-done.6.refs_0_), channel_id=1, source_target_pairs={{0,16},{4,20},{8,24},{12,28},{16,0},{20,4},{24,8},{28,12},{1,17},{... | collective-permute-start | bytes 1179656 | tf_op jit(solution)/shard_map/ppermute | solution.py:542
  106.5 10.1 %all-to-all-start.2 = ((bf16[8,64,128]{2,1,0:T(8,128)(2,1)}), bf16[8,64,128]{2,1,0:T(8,128)(2,1)S(1)}, u32[]{:S(2)}, u32[]{:S(2)}) async-start(bf16[8,64,128]{2,1,0:T(8,128)(2,1)} %bitcast.23), calls=%async_computation.2 | async-start | bytes 262144 | tf_op jit(solution)/shard_map/all_to_all | solution.py:575
  110.1 14.9 %collective-permute-start.16 = (bf16[512,384]{1,0:T(8,128)(2,1)}, bf16[512,384]{1,0:T(8,128)(2,1)S(1)}, u32[]{:S(2)}, u32[]{:S(2)}) collective-permute-start(bf16[512,384]{1,0:T(8,128)(2,1)} %collective-permute-done.12.refs_3_), channel_id=1, source_target_pairs={{0,4},{4,0},{8,12},{12,8},{16,20},{20,16},{24,28},{28,24},{1,5},{5... | collective-permute-start | bytes 1179656 | tf_op jit(solution)/shard_map/ppermute | solution.py:542
  111.6 13.4 %collective-permute-start.17 = (bf16[512,384]{1,0:T(8,128)(2,1)}, bf16[512,384]{1,0:T(8,128)(2,1)S(1)}, u32[]{:S(2)}, u32[]{:S(2)}) collective-permute-start(bf16[512,384]{1,0:T(8,128)(2,1)} %collective-permute-done.12.refs_3_), channel_id=1, source_target_pairs={{0,8},{4,12},{8,0},{12,4},{16,24},{20,28},{24,16},{28,20},{1,9},{5... | collective-permute-start | bytes 1179656 | tf_op jit(solution)/shard_map/ppermute | solution.py:542
  117.2 9.6 %all-to-all-start.3 = ((bf16[8,64,128]{2,1,0:T(8,128)(2,1)}), bf16[8,64,128]{2,1,0:T(8,128)(2,1)S(1)}, u32[]{:S(2)}, u32[]{:S(2)}) async-start(bf16[8,64,128]{2,1,0:T(8,128)(2,1)} %fusion.3), calls=%async_computation.3 | async-start | bytes 262144 | tf_op jit(solution)/shard_map/all_to_all | solution.py:578
  127.4 15.5 %collective-permute-start.19 = (bf16[512,512]{1,0:T(8,128)(2,1)S(1)}, bf16[512,512]{1,0:T(8,128)(2,1)S(1)}, u32[]{:S(2)}, u32[]{:S(2)}) collective-permute-start(bf16[512,512]{1,0:T(8,128)(2,1)S(1)} %finish.1.refs_0_), channel_id=1, source_target_pairs={{0,1},{1,0},{2,3},{3,2},{4,5},{5,4},{6,7},{7,6},{8,9},{9,8},{10,11... | collective-permute-start | bytes 1572872 | tf_op jit(solution)/shard_map/ppermute | solution.py:586
  131.2 13.5 %collective-permute-start.20 = (bf16[512,512]{1,0:T(8,128)(2,1)S(1)}, bf16[512,512]{1,0:T(8,128)(2,1)S(1)}, u32[]{:S(2)}, u32[]{:S(2)}) collective-permute-start(bf16[512,512]{1,0:T(8,128)(2,1)S(1)} %finish.1.refs_0_), channel_id=1, source_target_pairs={{0,2},{1,3},{2,0},{3,1},{4,6},{5,7},{6,4},{7,5},{8,10},{9,11},{10,... | collective-permute-start | bytes 1572872 | tf_op jit(solution)/shard_map/ppermute | solution.py:592
  132.4 10.6 %collective-permute-start.15 = (bf16[512,384]{1,0:T(8,128)(2,1)}, bf16[512,384]{1,0:T(8,128)(2,1)S(1)}, u32[]{:S(2)}, u32[]{:S(2)}) collective-permute-start(bf16[512,384]{1,0:T(8,128)(2,1)} %collective-permute-done.13.refs_1_), channel_id=1, source_target_pairs={{0,8},{4,12},{8,0},{12,4},{16,24},{20,28},{24,16},{28,20},{1,9},{5... | collective-permute-start | bytes 1179656 | tf_op jit(solution)/shard_map/ppermute | solution.py:542
  132.4 10.6 %collective-permute-start.18 = (bf16[512,384]{1,0:T(8,128)(2,1)S(1)}, bf16[512,384]{1,0:T(8,128)(2,1)S(1)}, u32[]{:S(2)}, u32[]{:S(2)}) collective-permute-start(bf16[512,384]{1,0:T(8,128)(2,1)S(1)} %collective-permute-done.17.refs_5_), channel_id=1, source_target_pairs={{0,4},{4,0},{8,12},{12,8},{16,20},{20,16},{24,28},{28,24},{1,5},{5... | collective-permute-start | bytes 1179656 | tf_op jit(solution)/shard_map/ppermute | solution.py:542
  144.7 4.1 %collective-permute-start.21 = (bf16[512,512]{1,0:T(8,128)(2,1)S(1)}, bf16[512,512]{1,0:T(8,128)(2,1)S(1)}, u32[]{:S(2)}, u32[]{:S(2)}) collective-permute-start(bf16[512,512]{1,0:T(8,128)(2,1)S(1)} %collective-permute-done.20.refs_0_), channel_id=1, source_target_pairs={{0,1},{1,0},{2,3},{3,2},{4,5},{5,4},{6,7},{7,6},{8,9},{9,8},{10,11... | collective-permute-start | bytes 1572872 | tf_op jit(solution)/shard_map/ppermute | solution.py:601
  (27 other events, 91.9 us)
